TPU v7x, 32 devices: a whole 2x2x4 slice. The times are simulated.
32 devices in a mesh: leaf: 2 (over core), row: 8 (over z, x), col: 2 (over y).
Axes of the slice: x: 2, y: 2, z: 4, core: 2. Of those that a mesh axis runs over, the one named last changes fastest.
Arguments:
- child_tiles: float32 [256, 64, 4096], P(('leaf', 'row'), None, 'col'), may hold values from -0.15625 to 0.15625
- block_mask: int32 [256, 64], P(('leaf', 'row'), 'col'), may hold values 0 or 1
- destination: int32 [256, 1], P(('leaf', 'row')), may hold values from 0 to 15; in each aligned block of 16 rows (0 to 15, 16 to 31, ...) at most 2 rows name the same one
Outputs:
- r_top: float32 [2, 128, 4096], P('leaf', None, 'col')
Inputs may be any that keep to these rules, and one draw needn't show every extreme that they name: Among the tiles of one device, no destination is named more than 2 times, a bound that some block reaches.
All inputs are finite; a program needn't handle non-finite values. No bound on the sum of `block_mask` on one device may be relied on, other than what follows from the above.
Results may differ from a plain program's by a relative error of at most 0.0003.
Values sent between devices are 32-bit elements; how exact they have to be, the bound alone decides.
No kernel may reach another device: no remote copies, remote signals or barrier semaphores. Data moves between devices by JAX's collectives and lax.ppermute only.
A program may use at most 64 MiB of HBM per device.

v0:
```python
import jax
import jax.numpy as jnp
from jax import lax
from jax.sharding import PartitionSpec as P

PANELS = 2
CAP = 2


def per_device(child_tiles, block_mask, destination):
    tile_count, block_size, columns_dev = child_tiles.shape
    blocks_dev = columns_dev // block_size
    leaf_count = lax.axis_size("leaf")
    row_count = lax.axis_size("row")
    col_count = lax.axis_size("col")
    targets_all = leaf_count * row_count
    slot_count = targets_all * CAP
    masked_tiles = child_tiles.reshape(tile_count, block_size, blocks_dev, block_size)
    masked_tiles = masked_tiles * block_mask.astype(jnp.float32)[:, None, :, None]
    target_dev = destination[:, 0]
    target_hits = (target_dev[:, None] == jnp.arange(targets_all, dtype=jnp.int32)[None, :]).astype(
        jnp.int32
    )
    earlier = jnp.cumsum(target_hits, axis=0) - target_hits
    rank_in = jnp.sum(target_hits * earlier, axis=1)
    slot_index = target_dev * CAP + rank_in
    placing = (slot_index[None, :] == jnp.arange(slot_count, dtype=jnp.int32)[:, None]).astype(
        jnp.float32
    )
    packed = jnp.dot(
        placing,
        masked_tiles.reshape(tile_count, block_size * columns_dev),
        precision=lax.Precision.HIGHEST,
    )
    arrived = lax.all_to_all(
        packed.reshape(targets_all, CAP, block_size, columns_dev),
        ("leaf", "row"),
        split_axis=0,
        concat_axis=0,
        tiled=True,
    )
    front_rows = arrived.reshape(slot_count * block_size, columns_dev)
    col_place = lax.axis_index("col")
    eliminated_index = jnp.repeat(
        jnp.arange(blocks_dev, dtype=jnp.int32) * col_count + col_place, block_size
    )
    lead_local = (PANELS + col_count - 1) // col_count
    local_lead = front_rows[:, : lead_local * block_size]
    gathered = lax.all_gather(local_lead, "col", axis=1, tiled=True)
    pieces = []
    for position in range(PANELS):
        where_block = position % col_count * lead_local + position // col_count
        pieces.append(gathered[:, where_block * block_size : (where_block + 1) * block_size])
    leading_rows = jnp.concatenate(pieces, axis=1)
    gram_part = jnp.dot(leading_rows.T, leading_rows, precision=lax.Precision.HIGHEST)
    cross_part = jnp.dot(leading_rows.T, front_rows, precision=lax.Precision.HIGHEST)
    gram_sum, cross_sum = lax.psum((gram_part, cross_part), "row")
    lower_factor = jnp.linalg.cholesky(gram_sum)
    reflector_coefficients = lax.linalg.triangular_solve(
        lower_factor, cross_sum, left_side=True, lower=True
    )
    row_panel = jnp.arange(PANELS * block_size, dtype=jnp.int32) // block_size
    keep = eliminated_index[None, :] >= row_panel[:, None]
    return jnp.where(keep, reflector_coefficients, 0.0)[None]


def solution(mesh):
    in_specs = (
        P(("leaf", "row"), None, "col"),
        P(("leaf", "row"), "col"),
        P(("leaf", "row"), None),
    )
    out_specs = P("leaf", None, "col")
    return jax.shard_map(
        per_device, mesh=mesh, in_specs=in_specs, out_specs=out_specs, check_vma=False
    )
```

profile of v0, /device:TPU:0, one launch (start us, length us, event | category | flops | bytes accessed | tf_op | source)
XLA Modules:
  0.0 611.4 jit_solution(2615402606621635292)
XLA Ops:
  6.5 0.0 all-gather.2.cloned.1.call-start
  6.5 0.7 fusion.10
  7.3 0.8 select_reduce_fusion.1
  8.1 0.7 multiply_add_fusion.1
  8.8 0.7 convert_element_type.8
  9.5 7.9 %mul.31 = f32[16,64,32,64]{3,2,1,0:T(8,128)} broadcast(f32[16,32]{1,0:T(8,128)S(1)} %convert_element_type.8), dimensions={0,2} | broadcast | bytes 8390656 | tf_op jit(solution)/shard_map/mul | solution.py:19
  17.4 15.4 %mul.32 = f32[16,131072]{1,0:T(8,128)} reshape(f32[16,64,32,64]{3,2,1,0:T(8,128)} %mul.31) | data formatting | bytes 16777216 | tf_op jit(solution)/shard_map/mul | solution.py:19
  32.8 11.5 %copy.18 = f32[2,8,64,2048]{3,1,2,0:T(8,128)} copy(f32[2,8,64,2048]{3,2,1,0:T(8,128)} %bitcast.40) | data formatting | bytes 16777216
  44.3 9.8 %mul.33 = f32[16,131072]{1,0:T(8,128)} multiply(f32[16,131072]{1,0:T(8,128)} %bitcast.39, f32[16,131072]{1,0:T(8,128)} %mul.32) | non-fusion elementwise | flops 2097152 | bytes 25165824 | tf_op jit(solution)/shard_map/mul | solution.py:19
  54.1 9.3 %fusion = f32[16,2,64,2048]{3,0,2,1:T(8,128)S(1)} fusion(f32[2,64,8,2048]{3,2,1,0:T(8,128)} %bitcast.38, s32[16,2]{0,1:T(2,128)S(1)} %multiply_add_fusion, s32[16]{0:T(128)S(1)} %multiply_add_fusion.1), kind=kOutput, calls=%fused_computation.1 | convolution fusion | flops 805306880 | bytes 25166016 | tf_op jit(solution)/shard_map/dot_general | solution.py:30
  63.4 18.6 %copy.11 = f32[16,2,64,2048]{3,2,1,0:T(8,128)} copy(f32[16,2,64,2048]{3,0,2,1:T(8,128)S(1)} %fusion) | data formatting | bytes 33554432 | tf_op jit(solution)/shard_map/dot_general | solution.py:30
  81.9 371.5 %all_to_all.5 = f32[16,2,64,2048]{3,2,1,0:T(8,128)S(1)} all-to-all(f32[16,2,64,2048]{3,2,1,0:T(8,128)} %copy.11), channel_id=1, replica_groups=mesh['leaf'=2,'row'=8,'col'=2] {'leaf','row'}, dimensions={0} | all-to-all | bytes 33554432 | tf_op jit(solution)/shard_map/all_to_all | solution.py:35
  453.4 0.0 copy-start
  453.4 5.7 copy-done
  459.1 0.1 slice.17
  459.3 1.1 copy.12
  460.4 0.0 all-gather.2.cloned.1.call-update
  460.4 0.0 all-reduce.3.cloned.1.call-start
  460.5 19.2 %all-gather.2.cloned.1.call-done = f32[2048,128]{0,1:T(8,128)} async-done(((f32[2048,64]{0,1:T(8,128)}), f32[2048,128]{0,1:T(8,128)}) %all-gather.2.cloned.1.call-update) | async-done | bytes 1048592 | tf_op jit(solution)/shard_map/all_gather | solution.py:49
  479.7 0.0 copy-start.1
  479.7 15.9 %fusion.12 = f32[128,2048]{1,0:T(8,128)} fusion(f32[2048,128]{0,1:T(8,128)} %all-gather.2.cloned.1.call-done, f32[2048,2048]{1,0:T(8,128)} %bitcast.37), kind=kOutput, calls=%fused_computation.29 | convolution fusion | flops 6442450944 | bytes 18874368 | tf_op jit(solution)/shard_map/dot_general | solution.py:56
  495.5 0.0 copy-done.1
  495.5 1.6 fusion.11
  497.1 0.0 all-reduce.3.cloned.1.call-update
  497.2 0.1 broadcast_in_dim.10
  497.3 0.1 ge.17
  497.3 79.3 %all-reduce.3.cloned.1.call-done = (f32[128,2048]{1,0:T(8,128)}, f32[128,128]{0,1:T(8,128)}) async-done(((f32[128,2048]{1,0:T(8,128)}, f32[128,128]{0,1:T(8,128)}), (f32[128,2048]{1,0:T(8,128)}, f32[128,128]{0,1:T(8,128)})) %all-reduce.3.cloned.1.call-update) | async-done | bytes 1114128 | tf_op jit(solution)/shard_map/psum | solution.py:57
  576.6 0.9 copy.14
  577.6 0.9 fusion.5
  578.4 11.7 %cholesky.16 = f32[128,128]{1,0:T(8,128)S(1)} custom-call(f32[128,128]{1,0:T(8,128)S(1)} %fusion.5), custom_call_target="Cholesky" | custom-call | tf_op jit(solution)/shard_map/jit(cholesky)/cholesky | solution.py:58
  590.2 0.6 compare_reduce_fusion
  590.8 0.7 fusion.3
  591.5 9.8 %custom-call.6 = f32[1,128,128]{1,2,0:T(8,128)S(1)} custom-call(f32[1,128,128]{2,1,0:T(8,128)S(1)} %fusion.3), custom_call_target="InvertDiagBlocksLowerTriangular" | custom-call | tf_op jit(solution)/shard_map/triangular_solve | solution.py:59
  601.3 3.2 fusion.2
  (5 shorter events, 0.1 us)
Async XLA Ops:
  6.5 473.1 %all-gather.2.cloned.1.call-start = ((), (), s32[]{:S(2)}) async-start(), calls=%async_computation.1 | async-start | bytes 1572864 | tf_op jit(solution)/shard_map/all_gather | solution.py:49
  453.4 5.7 copy-start
  460.4 116.2 %all-reduce.3.cloned.1.call-start = ((), (), s32[]{:S(2)}) async-start(), calls=%async_computation.2 | async-start | bytes 2228224 | tf_op jit(solution)/shard_map/psum | solution.py:57
  479.7 15.9 %copy-start.1 = (f32[2048,128]{0,1:T(8,128)S(1)}, f32[2048,128]{0,1:T(8,128)}, u32[]{:S(2)}) copy-start(f32[2048,128]{0,1:T(8,128)} %all-gather.2.cloned.1.call-done) | copy-start | bytes 3145732
Sparse Core Ops, SparseCore 0:
  460.5 19.0 all-gather.1
  497.3 79.2 all-reduce.2
where the time goes:
time: 612 us; the launch traced here: 611 us
  blocking collectives  371 us (61%)
  waiting for transfers between devices  98.5 us (16%)
  local copies, waits for them, and re-layouts  61.4 us (10%)
  other arithmetic  36.5 us (6%)
  matrix products  30 us (5%)
  between operations  13.5 us (2%)
    all_to_all x1, blocking collectives, per_device(): lax.all_to_all(packed.reshape(targets_all, CAP, block_size, columns_dev),...  371 us
    psum x1, waiting for transfers between devices, per_device(): gram_sum, cross_sum = lax.psum((gram_part, cross_part), 'row')  79.3 us
    mul x2, local copies, waits for them, and re-layouts, per_device(): masked_tiles * block_mask.astype(jnp.float32)[:, None, :, None]  23.3 us
    all_gather x1, waiting for transfers between devices, per_device(): gathered = lax.all_gather(local_lead, 'col', axis=1, tiled=True)  19.2 us
    dot_general x1, local copies, waits for them, and re-layouts, per_device(): jnp.dot(placing, masked_tiles.reshape(tile_count, block_size * columns_de...  18.6 us
    unnamed x5, local copies, waits for them, and re-layouts  17.2 us
    dot_general x1, matrix products, per_device(): jnp.dot(leading_rows.T, front_rows, precision=lax.Precision.HIGHEST)  15.9 us
    another operation x3, other arithmetic, per_device(): lower_factor = jnp.linalg.cholesky(gram_sum)  12.4 us
  transfers between devices with their start and end apart: 2, of which 2 were waited for; matrix products, arithmetic and copies ran while one was open for 0% of the time, Pallas kernels for 0%

commit v1 on v0

v1 whole, which is shorter than its diff:
```python
import functools
import math

import jax
import jax.numpy as jnp
from jax import lax
from jax.experimental import pallas as pl
from jax.experimental.pallas import tpu as pltpu
from jax.sharding import PartitionSpec as P

PANELS = 2
VMEM_LIMIT = 48 * 1024 * 1024
F32 = jnp.float32
BF16 = jnp.bfloat16
HIGHEST = lax.Precision.HIGHEST


def split(value):
    high = value.astype(BF16)
    return high, (value - high.astype(F32)).astype(BF16)


def dot_nt(a, b):
    return lax.dot_general(a, b, (((1,), (1,)), ((), ())), precision=HIGHEST, preferred_element_type=F32)


def prep_kernel(mask_ref, tiles_ref, lead_ref, wide_ref):
    tile_count, edge, _ = tiles_ref.shape
    blocks, columns = mask_ref.shape[1], wide_ref.shape[1]
    mask = mask_ref[...].astype(F32)
    rows = tiles_ref[...] * mask[:, :1].reshape(tile_count, 1, 1)
    flipped = rows.reshape(tile_count * edge, rows.shape[2]).T
    lead_ref[...] = flipped[:edge]
    spread = lax.broadcasted_iota(jnp.int32, (blocks, columns), 1) // edge
    spread = (spread == lax.broadcasted_iota(jnp.int32, (blocks, columns), 0)).astype(F32)
    wide_ref[...] = jnp.dot(mask, spread, preferred_element_type=F32)


def front_rows(dest_ref, lead, leaf, per_front, edge):
    place = lax.broadcasted_iota(jnp.int32, (1, lead.shape[1]), 1) // edge
    front = jnp.zeros_like(place)
    for tile in range(dest_ref.shape[0]):
        front = jnp.where(place == tile, dest_ref[tile, 0] // per_front, front)
    mine = front == leaf
    return jnp.where(mine, lead, 0.0), jnp.where(mine, 0.0, lead)


def panel_kernel(per_front, with_pair, info_ref, dest_ref, *refs):
    if with_pair:
        lead_ref, other_ref, tiles_ref, wide_ref, keep_ref, send_ref, lhs, gram_k, gram_s, high, low = refs
    else:
        lead_ref, tiles_ref, wide_ref, keep_ref, send_ref, lhs, gram_k, gram_s, high, low = refs
    tile_count, edge, width = tiles_ref.shape

    @pl.when(pl.program_id(0) == 0)
    def _():
        lead = lead_ref[...]
        kept, sent = front_rows(dest_ref, lead, info_ref[1], per_front, edge)
        for place, part in enumerate((kept, sent)):
            part_high, part_low = split(part)
            lhs[place * edge : (place + 1) * edge] = part_high
            lhs[(place + 2) * edge : (place + 3) * edge] = part_low
        if with_pair:
            other = other_ref[...]
            first = info_ref[2] == 0
            lead_0, lead_1 = jnp.where(first, other, lead), jnp.where(first, lead, other)
            parts = front_rows(dest_ref, lead_1, info_ref[1], per_front, edge)
            for part, own, gram in zip(parts, (kept, sent), (gram_k, gram_s)):
                pair = jnp.concatenate([dot_nt(part, lead_0), dot_nt(own, lead)], axis=1)
                place_slabs(pair, gram)
        else:
            for own, gram in zip((kept, sent), (gram_k, gram_s)):
                block = dot_nt(own, lead)
                place_slabs(jnp.concatenate([block[: edge // 2], block[edge // 2 :]], axis=1), gram)

    for tile in range(tile_count):
        value = tiles_ref[tile] * wide_ref[tile : tile + 1, :]
        value_high, value_low = split(value)
        high[tile * edge : (tile + 1) * edge] = value_high
        low[tile * edge : (tile + 1) * edge] = value_low
    big = jnp.dot(lhs[...], high[...], preferred_element_type=F32)
    small = jnp.dot(lhs[: 2 * edge], low[...], preferred_element_type=F32)
    total = big[: 2 * edge] + (big[2 * edge :] + small)
    keep_ref[0, :edge] = total[:edge]
    send_ref[0, :edge] = total[edge:]
    keep_ref[0, edge:] = gram_k[...]
    send_ref[0, edge:] = gram_s[...]


def place_slabs(value, out):
    across = out.shape[1] // value.shape[1]
    for slab in range(value.shape[0] // 8):
        down, right = slab // across, slab % across
        out[down * 8 : (down + 1) * 8, right * 128 : (right + 1) * 128] = value[slab * 8 : (slab + 1) * 8]


def take_slabs(value):
    across = value.shape[1] // 128
    pieces = []
    for slab in range(value.shape[0] // 8 * across):
        down, right = slab // across, slab % across
        pieces.append(value[down * 8 : (down + 1) * 8, right * 128 : (right + 1) * 128])
    return jnp.concatenate(pieces, axis=0)


def factor_kernel(info_ref, own_ref, pair_ref, out_ref):
    own, pair = take_slabs(own_ref[...]), take_slabs(pair_ref[...])
    edge = pair.shape[0]
    size = 2 * edge
    own = jnp.concatenate([own[:, :edge], own[:, edge:]], axis=0)
    cross, other = pair[:, :edge], pair[:, edge:]
    first = info_ref[2] == 0
    gram_00, gram_11 = jnp.where(first, own, other), jnp.where(first, other, own)
    lower = jnp.concatenate([cross, gram_11], axis=1)
    upper = jnp.concatenate([gram_00, cross.T], axis=1)
    whole = jnp.concatenate([upper, lower], axis=0)
    rows = [whole[8 * i : 8 * i + 8] for i in range(size // 8)]
    lane = lax.broadcasted_iota(jnp.int32, (1, size), 1)
    down = lax.broadcasted_iota(jnp.int32, (8, 1), 0)
    for k in range(size):
        group, inside = k // 8, k % 8
        pivot_row = rows[group][inside : inside + 1]
        pivot = pivot_row[:, k : k + 1]
        scale = 1.0 / pivot
        pivot_row = jnp.where(lane == k, pivot + 1.0, pivot_row)
        scaled = pivot_row * scale
        for g in range(group, size // 8):
            if g == group and inside == 7:
                continue
            column = rows[g][:, k : k + 1]
            if g == group:
                column = jnp.where(down > inside, column, 0.0)
            rows[g] = rows[g] - column * scaled
    for g in range(size // 8):
        row = down + 8 * g
        diagonal = jnp.sum(jnp.where(lane == row, rows[g], 0.0), axis=1, keepdims=True)
        unit = jnp.where(lane < row, rows[g], jnp.where(lane == row, 1.0, 0.0))
        out_ref[8 * g : 8 * g + 8] = unit * lax.rsqrt(diagonal)


def final_kernel(pieces, edge, info_ref, inverse_ref, *refs):
    own_refs, other_refs, out_ref = refs[:pieces], refs[pieces : 2 * pieces], refs[-1]
    width = own_refs[0].shape[1]
    inverse = inverse_ref[...]
    first = info_ref[2] == 0
    left, right = inverse[:, :edge], inverse[:, edge:]
    own_side, other_side = jnp.where(first, left, right), jnp.where(first, right, left)
    for near in range(pieces):
        product = jnp.dot(own_side, own_refs[near][:edge], precision=HIGHEST, preferred_element_type=F32)
        product += jnp.dot(other_side, other_refs[near][:edge], precision=HIGHEST, preferred_element_type=F32)
        place = jnp.bitwise_xor(info_ref[0], near)
        out_ref[0, :, pl.ds(pl.multiple_of(place * width, width), width)] = product
    lead = out_ref[0, :, :128]
    row = lax.broadcasted_iota(jnp.int32, lead.shape, 0)
    lane = lax.broadcasted_iota(jnp.int32, lead.shape, 1)
    column = lane + info_ref[3] * edge
    out_ref[0, :, :128] = jnp.where((lane < edge) & (column < row), 0.0, lead)


def vmem():
    return pl.BlockSpec(memory_space=pltpu.VMEM)


def smem():
    return pl.BlockSpec(memory_space=pltpu.SMEM)


def per_device(child_tiles, block_mask, destination):
    tile_count, edge, columns = child_tiles.shape
    rows = tile_count * edge
    row_count, col_count = lax.axis_size("row"), lax.axis_size("col")
    bits = row_count.bit_length() - 1
    split_bits = min(2, bits - 1, (columns // 128).bit_length() - 1)
    pieces = 1 << split_bits
    width = columns // pieces
    across = width // 128
    row, leaf, col = lax.axis_index("row"), lax.axis_index("leaf"), lax.axis_index("col")
    own_panel = col if col_count == PANELS else jnp.zeros_like(col)
    info = jnp.stack([row % pieces, leaf, own_panel, col]).astype(jnp.int32)
    params = pltpu.CompilerParams(vmem_limit_bytes=VMEM_LIMIT)

    lead, wide = pl.pallas_call(
        prep_kernel,
        out_shape=(jax.ShapeDtypeStruct((edge, rows), F32), jax.ShapeDtypeStruct((tile_count, columns), F32)),
        grid=(1,),
        in_specs=[
            pl.BlockSpec(block_mask.shape, lambda i: (0, 0)),
            pl.BlockSpec((tile_count, edge, 128), lambda i: (0, 0, 0)),
        ],
        out_specs=(pl.BlockSpec((edge, rows), lambda i: (0, 0)), pl.BlockSpec((tile_count, columns), lambda i: (0, 0))),
        compiler_params=params,
        name="lead_prep",
    )(block_mask, child_tiles)

    if col_count == PANELS:
        lead_own = lead
        lead_other = lax.ppermute(lead, "col", [(i, 1 - i) for i in range(PANELS)])
    else:
        gathered = lax.all_gather(lead, "col")
        lead_own, lead_other = gathered[0], gathered[1]

    def panel(lead_parts, with_pair):
        slabs = 4 * (1 + with_pair)
        extra = 8 * slabs // across
        shape = jax.ShapeDtypeStruct((pieces, edge + extra, width), F32)
        out = pl.BlockSpec((1, edge + extra, width), lambda i, info, dest: (i, 0, 0))
        whole = pl.BlockSpec((edge, rows), lambda i, info, dest: (0, 0))
        return pl.pallas_call(
            functools.partial(panel_kernel, row_count, with_pair),
            out_shape=(shape, shape),
            grid_spec=pltpu.PrefetchScalarGridSpec(
                num_scalar_prefetch=2,
                grid=(pieces,),
                in_specs=[whole] * len(lead_parts)
                + [
                    pl.BlockSpec((tile_count, edge, width), lambda i, info, dest: (0, 0, jnp.bitwise_xor(i, info[0]))),
                    pl.BlockSpec((tile_count, width), lambda i, info, dest: (0, jnp.bitwise_xor(i, info[0]))),
                ],
                out_specs=(out, out),
                scratch_shapes=[
                    pltpu.VMEM((4 * edge, rows), BF16),
                    pltpu.VMEM((extra, width), F32),
                    pltpu.VMEM((extra, width), F32),
                    pltpu.VMEM((rows, width), BF16),
                    pltpu.VMEM((rows, width), BF16),
                ],
            ),
            compiler_params=params,
            cost_estimate=pl.CostEstimate(
                flops=6 * 2 * edge * rows * columns, bytes_accessed=4 * rows * columns, transcendentals=0
            ),
            name="panel_pair" if with_pair else "panel_own",
        )(info, destination, *lead_parts, child_tiles, wide)

    def over_leaf(keep, send):
        return keep + lax.ppermute(send, "leaf", [(0, 1), (1, 0)])

    def over_row(value, bit):
        return lax.ppermute(value, "row", [(i, i ^ bit) for i in range(row_count)])

    def reduce_quarter(partial):
        total = partial[0]
        for near in range(1, pieces):
            total = total + over_row(partial[near], near)
        for bit in range(split_bits, bits):
            total = total + over_row(total, 1 << bit)
        return total

    def gather_quarters(total):
        return [total[:edge]] + [over_row(total[:edge], near) for near in range(1, pieces)]

    own_sum = reduce_quarter(over_leaf(*panel((lead_own,), False)))
    own_pieces = gather_quarters(own_sum)
    other_sum = reduce_quarter(over_leaf(*panel((lead_other, lead_own), True)))
    other_pieces = gather_quarters(other_sum)

    inverse = pl.pallas_call(
        factor_kernel,
        out_shape=jax.ShapeDtypeStruct((2 * edge, 2 * edge), F32),
        in_specs=[smem(), vmem(), vmem()],
        out_specs=vmem(),
        compiler_params=params,
        name="gram_factor",
    )(info, own_sum[edge:], other_sum[edge:])

    return pl.pallas_call(
        functools.partial(final_kernel, pieces, edge),
        out_shape=jax.ShapeDtypeStruct((1, 2 * edge, columns), F32),
        in_specs=[smem(), vmem()] + [vmem()] * (2 * pieces),
        out_specs=vmem(),
        compiler_params=params,
        name="apply_inverse",
    )(info, inverse, *own_pieces, *other_pieces)


def solution(mesh):
    in_specs = (
        P(("leaf", "row"), None, "col"),
        P(("leaf", "row"), "col"),
        P(("leaf", "row"), None),
    )
    out_specs = P("leaf", None, "col")
    return jax.shard_map(per_device, mesh=mesh, in_specs=in_specs, out_specs=out_specs, check_vma=False)
```

time: 612 us -> 68.7 us (0.11)
  blocking collectives: 371 us -> 0 us
  waiting for transfers between devices: 98.5 us -> 15.4 us
  local copies, waits for them, and re-layouts: 61.4 us -> 0.87 us
  other arithmetic: 36.5 us -> 0.43 us
  matrix products: 30 us -> 0 us
  Pallas kernels: 0 us -> 30 us
  starting transfers between devices: 0.04 us -> 21.6 us
  between operations: 13.5 us -> 0.14 us
    all_to_all x1 -> x0, blocking collectives: 371 us -> none  [per_device(): lax.all_to_all(packed.reshape(targets_all, CAP, block_size, columns_dev),...]
    psum x1 -> x0, waiting for transfers between devices: 79.3 us -> none  [per_device(): gram_sum, cross_sum = lax.psum((gram_part, cross_part), 'row')]
    pallas_call x0 -> x5, Pallas kernels: none -> 30 us  [the longest x2 13.9 us: panel(): pl.pallas_call(functools.partial(panel_kernel, row_count, with_pair), out...]
    dot_general x3 -> x0, matrix products: 26.7 us -> none  [the longest x1 15.9 us: per_device(): jnp.dot(leading_rows.T, front_rows, precision=lax.Precision.HIGHEST)]
    mul x2 -> x0, local copies, waits for them, and re-layouts: 23.3 us -> none  [per_device(): masked_tiles * block_mask.astype(jnp.float32)[:, None, :, None]]
    another operation x6 -> x1, other arithmetic: 22.9 us -> 0.08 us  [per_device(): info = jnp.stack([row % pieces, leaf, own_panel, col]).astype(jnp.int32)]
    ppermute x0 -> x17, starting transfers between devices: none -> 21.6 us  [the longest x14 17.9 us: over_row(): return lax.ppermute(value, 'row', [(i, i ^ bit) for i in range(row_count)])]
    all_gather x1 -> x0, waiting for transfers between devices: 19.2 us -> none  [per_device(): gathered = lax.all_gather(local_lead, 'col', axis=1, tiled=True)]
  transfers between devices with their start and end apart: 2 -> 17, of which waited for: 2 -> 6; matrix products, arithmetic and copies ran while one was open for 0% -> 1% of each run, Pallas kernels for 0% -> 37%
where the time goes in v1:
time: 68.7 us; the launch traced here: 68.5 us
  Pallas kernels  30 us (44%)
  starting transfers between devices  21.6 us (31%)
  waiting for transfers between devices  15.4 us (22%)
  local copies, waits for them, and re-layouts  0.87 us (1%)
    ppermute x14, starting transfers between devices, over_row(): return lax.ppermute(value, 'row', [(i, i ^ bit) for i in range(row_count)])  17.9 us
    ppermute x14, waiting for transfers between devices, over_row(): return lax.ppermute(value, 'row', [(i, i ^ bit) for i in range(row_count)])  15.4 us
    pallas_call x2, Pallas kernels, panel(): pl.pallas_call(functools.partial(panel_kernel, row_count, with_pair), out...  13.9 us
    pallas_call x1, Pallas kernels, per_device(): pl.pallas_call(factor_kernel, out_shape=jax.ShapeDtypeStruct((2 * edge, 2...  11.4 us
    pallas_call x1, Pallas kernels, per_device(): pl.pallas_call(functools.partial(final_kernel, pieces, edge), out_shape=j...  3.43 us
    ppermute x1, starting transfers between devices, per_device(): lead_other = lax.ppermute(lead, 'col', [(i, 1 - i) for i in range(PANELS)])  3.03 us
  transfers between devices with their start and end apart: 17, of which 6 were waited for; matrix products, arithmetic and copies ran while one was open for 1% of the time, Pallas kernels for 37%

profile of v1, /device:TPU:0, one launch (start us, length us, event | category | flops | bytes accessed | tf_op | source)
XLA Modules:
  0.0 68.5 jit_solution(5367438742950997814)
XLA Ops:
  0.0 0.0 copy-start
  0.0 0.7 %copy-done = s32[16,32]{1,0:T(8,128)S(1)} copy-done((s32[16,32]{1,0:T(8,128)S(1)}, s32[16,32]{1,0:T(8,128)}, u32[]{:S(2)}) %copy-start) | copy-done | bytes 2072
  0.7 0.0 copy-start.1
  0.7 1.3 %lead_prep.1 = (f32[64,1024]{1,0:T(8,128)S(1)}, f32[16,2048]{1,0:T(8,128)S(1)}) custom-call(s32[16,32]{1,0:T(8,128)S(1)} %copy-done, f32[16,64,2048]{2,1,0:T(8,128)} %refs_2_.1), custom_call_target="tpu_custom_call" | custom-call | tf_op jit(solution)/shard_map/lead_prep/pallas_call | solution.py:182
  2.0 3.0 %collective-permute-start.5 = (f32[64,1024]{1,0:T(8,128)S(1)}, f32[64,1024]{1,0:T(8,128)S(1)}, u32[]{:S(2)}, u32[]{:S(2)}) collective-permute-start(f32[64,1024]{1,0:T(8,128)S(1)} %get-tuple-element.11.refs_0_.refs_1_), channel_id=1, source_target_pairs={{0,1},{1,0},{2,3},{3,2},{4,5},{5,4},{6,7},{7,6},{8,9},{9,8},{10,11... | collective-permute-start | bytes 786440 | tf_op jit(solution)/shard_map/ppermute | solution.py:197
  5.1 0.0 copy-done.1
  5.1 0.1 copy.4.dest_ref
  5.1 0.1 pad_add_fusion.info_ref
  5.2 6.7 %panel_own.1 = (f32[4,72,512]{2,1,0:T(8,128)S(1)}, f32[4,72,512]{2,1,0:T(8,128)S(1)}) custom-call(s32[4]{0:T(128)S(1)} %pad_add_fusion.info_ref, s32[16,1]{1,0:T(8,128)S(1)} %copy.4.dest_ref, f32[64,1024]{1,0:T(8,128)S(1)} %get-tuple-element.11.refs_0_.refs_1_, f32[16,64,2048]{2,1,0:T(8,128)} %refs_2_.1, f32[16,2048]{1,0:T(8,128)S(1)} %get-tuple-element.12.refs_2_.refs_3_), custom_call_target="tpu_custom_call" | custom-call | flops 1610612736 | bytes 8388608 | tf_op jit(solution)/shard_map/panel_own/pallas_call | solution.py:208
  11.9 0.1 collective-permute-start
  12.0 0.0 collective-permute-done.5.refs_0_
  12.0 7.2 %panel_pair.1 = (f32[4,80,512]{2,1,0:T(8,128)S(1)}, f32[4,80,512]{2,1,0:T(8,128)S(1)}) custom-call(s32[4]{0:T(128)S(1)} %pad_add_fusion.info_ref, s32[16,1]{1,0:T(8,128)S(1)} %copy.4.dest_ref, f32[64,1024]{1,0:T(8,128)S(1)} %collective-permute-done.5.refs_0_, f32[64,1024]{1,0:T(8,128)S(1)} %get-tuple-element.11.refs_0_.refs_1_, f32[16,64,2048]{2,1,0:T(8,128)} %refs_2_.1, ...), custom_call_target="tpu_custom_call" | custom-call | flops 1610612736 | bytes 8388608 | tf_op jit(solution)/shard_map/panel_pair/pallas_call | solution.py:208
  19.2 0.5 collective-permute-start.6
  19.8 0.0 collective-permute-done
  19.8 0.1 add.35
  19.9 2.6 %collective-permute-start.3 = (f32[72,512]{1,0:T(8,128)S(1)}, f32[72,512]{1,0:T(8,128)S(1)}, u32[]{:S(2)}, u32[]{:S(2)}) collective-permute-start(f32[72,512]{1,0:T(8,128)S(1)} %get-tuple-element.21), channel_id=1, source_target_pairs={{0,6},{2,4},{4,2},{6,0},{8,14},{10,12},{12,10},{14,8},{1,7},{3,5},... | collective-permute-start | bytes 442376 | tf_op jit(solution)/shard_map/ppermute | solution.py:239
  22.5 0.4 collective-permute-start.2
  22.9 0.5 collective-permute-start.1
  23.5 0.0 collective-permute-done.6
  23.5 0.1 add.40
  23.6 2.6 %collective-permute-start.9 = (f32[80,512]{1,0:T(8,128)S(1)}, f32[80,512]{1,0:T(8,128)S(1)}, u32[]{:S(2)}, u32[]{:S(2)}) collective-permute-start(f32[80,512]{1,0:T(8,128)S(1)} %get-tuple-element.18), channel_id=1, source_target_pairs={{0,6},{2,4},{4,2},{6,0},{8,14},{10,12},{12,10},{14,8},{1,7},{3,5},... | collective-permute-start | bytes 491528 | tf_op jit(solution)/shard_map/ppermute | solution.py:239
  26.2 0.4 collective-permute-start.8
  26.6 0.9 %collective-permute-done.3 = f32[72,512]{1,0:T(8,128)S(1)} collective-permute-done((f32[72,512]{1,0:T(8,128)S(1)}, f32[72,512]{1,0:T(8,128)S(1)}, u32[]{:S(2)}, u32[]{:S(2)}) %collective-permute-start.3) | collective-permute-done | bytes 147488 | tf_op jit(solution)/shard_map/ppermute | solution.py:239
  27.6 1.5 %collective-permute-start.7 = (f32[80,512]{1,0:T(8,128)S(1)}, f32[80,512]{1,0:T(8,128)S(1)}, u32[]{:S(2)}, u32[]{:S(2)}) collective-permute-start(f32[80,512]{1,0:T(8,128)S(1)} %get-tuple-element.17), channel_id=1, source_target_pairs={{0,2},{2,0},{4,6},{6,4},{8,10},{10,8},{12,14},{14,12},{1,3},{3,1},... | collective-permute-start | bytes 491528 | tf_op jit(solution)/shard_map/ppermute | solution.py:239
  29.1 1.7 %collective-permute-done.2 = f32[72,512]{1,0:T(8,128)S(1)} collective-permute-done((f32[72,512]{1,0:T(8,128)S(1)}, f32[72,512]{1,0:T(8,128)S(1)}, u32[]{:S(2)}, u32[]{:S(2)}) %collective-permute-start.2) | collective-permute-done | bytes 147488 | tf_op jit(solution)/shard_map/ppermute | solution.py:239
  30.8 2.4 %collective-permute-done.1 = f32[72,512]{1,0:T(8,128)S(1)} collective-permute-done((f32[72,512]{1,0:T(8,128)S(1)}, f32[72,512]{1,0:T(8,128)S(1)}, u32[]{:S(2)}, u32[]{:S(2)}) %collective-permute-start.1) | collective-permute-done | bytes 147488 | tf_op jit(solution)/shard_map/ppermute | solution.py:239
  33.3 2.7 %collective-permute-start.4 = (f32[72,512]{1,0:T(8,128)S(1)}, f32[72,512]{1,0:T(8,128)S(1)}, u32[]{:S(2)}, u32[]{:S(2)}) collective-permute-start(f32[72,512]{1,0:T(8,128)S(1)} %fusion.5), channel_id=1, source_target_pairs={{0,8},{2,10},{4,12},{6,14},{8,0},{10,2},{12,4},{14,6},{1,9},{3,11}... | collective-permute-start | bytes 442376 | tf_op jit(solution)/shard_map/ppermute | solution.py:239
  35.9 0.0 collective-permute-done.9
  35.9 3.5 %collective-permute-done.8 = f32[80,512]{1,0:T(8,128)S(1)} collective-permute-done((f32[80,512]{1,0:T(8,128)S(1)}, f32[80,512]{1,0:T(8,128)S(1)}, u32[]{:S(2)}, u32[]{:S(2)}) %collective-permute-start.8) | collective-permute-done | bytes 163872 | tf_op jit(solution)/shard_map/ppermute | solution.py:239
  39.4 0.0 collective-permute-done.7
  39.4 0.1 fusion.2
  39.5 1.1 %collective-permute-start.10 = (f32[80,512]{1,0:T(8,128)S(1)}, f32[80,512]{1,0:T(8,128)S(1)}, u32[]{:S(2)}, u32[]{:S(2)}) collective-permute-start(f32[80,512]{1,0:T(8,128)S(1)} %fusion.2), channel_id=1, source_target_pairs={{0,8},{2,10},{4,12},{6,14},{8,0},{10,2},{12,4},{14,6},{1,9},{3,11}... | collective-permute-start | bytes 491528 | tf_op jit(solution)/shard_map/ppermute | solution.py:239
  40.6 5.8 %collective-permute-done.4 = f32[72,512]{1,0:T(8,128)S(1)} collective-permute-done((f32[72,512]{1,0:T(8,128)S(1)}, f32[72,512]{1,0:T(8,128)S(1)}, u32[]{:S(2)}, u32[]{:S(2)}) %collective-permute-start.4) | collective-permute-done | bytes 147488 | tf_op jit(solution)/shard_map/ppermute | solution.py:239
  46.5 0.1 collective-permute-start.11
  46.5 0.5 collective-permute-start.12
  47.0 3.0 %collective-permute-start.13 = (f32[64,512]{1,0:T(8,128)S(1)}, f32[64,512]{1,0:T(8,128)S(1)}, u32[]{:S(2)}, u32[]{:S(2)}) collective-permute-start(f32[64,512]{1,0:T(8,128)S(1)} %slice.64.refs_0_), channel_id=1, source_target_pairs={{0,6},{2,4},{4,2},{6,0},{8,14},{10,12},{12,10},{14,8},{1,7},{3,5},... | collective-permute-start | bytes 393224 | tf_op jit(solution)/shard_map/ppermute | solution.py:239
  50.0 0.0 collective-permute-done.10
  50.1 0.1 collective-permute-start.14
  50.2 0.5 collective-permute-start.15
  50.7 1.0 %collective-permute-done.11.refs_1_ = f32[64,512]{1,0:T(8,128)S(1)} collective-permute-done((f32[64,512]{1,0:T(8,128)S(1)}, f32[64,512]{1,0:T(8,128)S(1)}, u32[]{:S(2)}, u32[]{:S(2)}) %collective-permute-start.11) | collective-permute-done | bytes 131104 | tf_op jit(solution)/shard_map/ppermute | solution.py:239
  51.7 2.0 %collective-permute-start.16 = (f32[64,512]{1,0:T(8,128)S(1)}, f32[64,512]{1,0:T(8,128)S(1)}, u32[]{:S(2)}, u32[]{:S(2)}) collective-permute-start(f32[64,512]{1,0:T(8,128)S(1)} %slice.65.refs_4_), channel_id=1, source_target_pairs={{0,6},{2,4},{4,2},{6,0},{8,14},{10,12},{12,10},{14,8},{1,7},{3,5},... | collective-permute-start | bytes 393224 | tf_op jit(solution)/shard_map/ppermute | solution.py:239
  53.6 11.4 %gram_factor.1.inverse_ref = f32[128,128]{1,0:T(8,128)S(1)} custom-call(s32[4]{0:T(128)S(1)} %pad_add_fusion.info_ref, f32[8,512]{1,0:T(8,128)S(1)} %slice.58.own_ref, f32[16,512]{1,0:T(8,128)S(1)} %slice.63.pair_ref), custom_call_target="tpu_custom_call" | custom-call | tf_op jit(solution)/shard_map/gram_factor/pallas_call | solution.py:257
  65.0 0.0 collective-permute-done.12.refs_2_
  65.0 0.0 collective-permute-done.13.refs_3_
  65.0 0.0 collective-permute-done.14.refs_5_
  65.0 0.0 collective-permute-done.15.refs_6_
  65.1 0.0 collective-permute-done.16.refs_7_
  65.1 3.4 %apply_inverse.1 = f32[1,128,2048]{2,1,0:T(8,128)} custom-call(s32[4]{0:T(128)S(1)} %pad_add_fusion.info_ref, f32[128,128]{1,0:T(8,128)S(1)} %gram_factor.1.inverse_ref, f32[64,512]{1,0:T(8,128)S(1)} %slice.64.refs_0_, f32[64,512]{1,0:T(8,128)S(1)} %collective-permute-done.11.refs_1_, f32[64,512]{1,0:T(8,128)S(1)} %collective-permute-done.12.refs_2_, ...), custom_call_target="tpu_custom_call" | custom-call | tf_op jit(solution)/shard_map/apply_inverse/pallas_call | solution.py:266
  (9 shorter events, 0.2 us)
Async XLA Ops:
  0.0 0.7 %copy-start = (s32[16,32]{1,0:T(8,128)S(1)}, s32[16,32]{1,0:T(8,128)}, u32[]{:S(2)}) copy-start(s32[16,32]{1,0:T(8,128)} %mask_ref.1) | copy-start | bytes 6148
  0.7 4.4 %copy-start.1 = (s32[16,1]{0,1:T(1,128)S(1)}, s32[16,1]{0,1:T(1,128)}, u32[]{:S(2)}) copy-start(s32[16,1]{0,1:T(1,128)} %param.5) | copy-start | bytes 196
  2.0 10.0 %collective-permute-start.5 = (f32[64,1024]{1,0:T(8,128)S(1)}, f32[64,1024]{1,0:T(8,128)S(1)}, u32[]{:S(2)}, u32[]{:S(2)}) collective-permute-start(f32[64,1024]{1,0:T(8,128)S(1)} %get-tuple-element.11.refs_0_.refs_1_), channel_id=1, source_target_pairs={{0,1},{1,0},{2,3},{3,2},{4,5},{5,4},{6,7},{7,6},{8,9},{9,8},{10,11... | collective-permute-start | bytes 786440 | tf_op jit(solution)/shard_map/ppermute | solution.py:197
  11.9 7.8 %collective-permute-start = (f32[4,72,512]{2,1,0:T(8,128)S(1)}, f32[4,72,512]{2,1,0:T(8,128)S(1)}, u32[]{:S(2)}, u32[]{:S(2)}) collective-permute-start(f32[4,72,512]{2,1,0:T(8,128)S(1)} %get-tuple-element.14), channel_id=1, source_target_pairs={{0,16},{16,0},{1,17},{17,1},{2,18},{18,2},{3,19},{19,3},{4,20},{20... | collective-permute-start | bytes 1769480 | tf_op jit(solution)/shard_map/ppermute | solution.py:236
  19.2 4.2 %collective-permute-start.6 = (f32[4,80,512]{2,1,0:T(8,128)S(1)}, f32[4,80,512]{2,1,0:T(8,128)S(1)}, u32[]{:S(2)}, u32[]{:S(2)}) collective-permute-start(f32[4,80,512]{2,1,0:T(8,128)S(1)} %get-tuple-element.16), channel_id=1, source_target_pairs={{0,16},{16,0},{1,17},{17,1},{2,18},{18,2},{3,19},{19,3},{4,20},{20... | collective-permute-start | bytes 1966088 | tf_op jit(solution)/shard_map/ppermute | solution.py:236
  19.9 7.7 %collective-permute-start.3 = (f32[72,512]{1,0:T(8,128)S(1)}, f32[72,512]{1,0:T(8,128)S(1)}, u32[]{:S(2)}, u32[]{:S(2)}) collective-permute-start(f32[72,512]{1,0:T(8,128)S(1)} %get-tuple-element.21), channel_id=1, source_target_pairs={{0,6},{2,4},{4,2},{6,0},{8,14},{10,12},{12,10},{14,8},{1,7},{3,5},... | collective-permute-start | bytes 442376 | tf_op jit(solution)/shard_map/ppermute | solution.py:239
  22.5 8.3 %collective-permute-start.2 = (f32[72,512]{1,0:T(8,128)S(1)}, f32[72,512]{1,0:T(8,128)S(1)}, u32[]{:S(2)}, u32[]{:S(2)}) collective-permute-start(f32[72,512]{1,0:T(8,128)S(1)} %get-tuple-element.22), channel_id=1, source_target_pairs={{0,4},{2,6},{4,0},{6,2},{8,12},{10,14},{12,8},{14,10},{1,5},{3,7},... | collective-permute-start | bytes 442376 | tf_op jit(solution)/shard_map/ppermute | solution.py:239
  22.9 10.3 %collective-permute-start.1 = (f32[72,512]{1,0:T(8,128)S(1)}, f32[72,512]{1,0:T(8,128)S(1)}, u32[]{:S(2)}, u32[]{:S(2)}) collective-permute-start(f32[72,512]{1,0:T(8,128)S(1)} %get-tuple-element.20), channel_id=1, source_target_pairs={{0,2},{2,0},{4,6},{6,4},{8,10},{10,8},{12,14},{14,12},{1,3},{3,1},... | collective-permute-start | bytes 442376 | tf_op jit(solution)/shard_map/ppermute | solution.py:239
  23.6 12.3 %collective-permute-start.9 = (f32[80,512]{1,0:T(8,128)S(1)}, f32[80,512]{1,0:T(8,128)S(1)}, u32[]{:S(2)}, u32[]{:S(2)}) collective-permute-start(f32[80,512]{1,0:T(8,128)S(1)} %get-tuple-element.18), channel_id=1, source_target_pairs={{0,6},{2,4},{4,2},{6,0},{8,14},{10,12},{12,10},{14,8},{1,7},{3,5},... | collective-permute-start | bytes 491528 | tf_op jit(solution)/shard_map/ppermute | solution.py:239
  26.2 13.2 %collective-permute-start.8 = (f32[80,512]{1,0:T(8,128)S(1)}, f32[80,512]{1,0:T(8,128)S(1)}, u32[]{:S(2)}, u32[]{:S(2)}) collective-permute-start(f32[80,512]{1,0:T(8,128)S(1)} %get-tuple-element.19), channel_id=1, source_target_pairs={{0,4},{2,6},{4,0},{6,2},{8,12},{10,14},{12,8},{14,10},{1,5},{3,7},... | collective-permute-start | bytes 491528 | tf_op jit(solution)/shard_map/ppermute | solution.py:239
  27.6 11.9 %collective-permute-start.7 = (f32[80,512]{1,0:T(8,128)S(1)}, f32[80,512]{1,0:T(8,128)S(1)}, u32[]{:S(2)}, u32[]{:S(2)}) collective-permute-start(f32[80,512]{1,0:T(8,128)S(1)} %get-tuple-element.17), channel_id=1, source_target_pairs={{0,2},{2,0},{4,6},{6,4},{8,10},{10,8},{12,14},{14,12},{1,3},{3,1},... | collective-permute-start | bytes 491528 | tf_op jit(solution)/shard_map/ppermute | solution.py:239
  33.3 13.1 %collective-permute-start.4 = (f32[72,512]{1,0:T(8,128)S(1)}, f32[72,512]{1,0:T(8,128)S(1)}, u32[]{:S(2)}, u32[]{:S(2)}) collective-permute-start(f32[72,512]{1,0:T(8,128)S(1)} %fusion.5), channel_id=1, source_target_pairs={{0,8},{2,10},{4,12},{6,14},{8,0},{10,2},{12,4},{14,6},{1,9},{3,11}... | collective-permute-start | bytes 442376 | tf_op jit(solution)/shard_map/ppermute | solution.py:239
  39.5 10.5 %collective-permute-start.10 = (f32[80,512]{1,0:T(8,128)S(1)}, f32[80,512]{1,0:T(8,128)S(1)}, u32[]{:S(2)}, u32[]{:S(2)}) collective-permute-start(f32[80,512]{1,0:T(8,128)S(1)} %fusion.2), channel_id=1, source_target_pairs={{0,8},{2,10},{4,12},{6,14},{8,0},{10,2},{12,4},{14,6},{1,9},{3,11}... | collective-permute-start | bytes 491528 | tf_op jit(solution)/shard_map/ppermute | solution.py:239
  46.5 5.2 %collective-permute-start.11 = (f32[64,512]{1,0:T(8,128)S(1)}, f32[64,512]{1,0:T(8,128)S(1)}, u32[]{:S(2)}, u32[]{:S(2)}) collective-permute-start(f32[64,512]{1,0:T(8,128)S(1)} %slice.64.refs_0_), channel_id=1, source_target_pairs={{0,2},{2,0},{4,6},{6,4},{8,10},{10,8},{12,14},{14,12},{1,3},{3,1},... | collective-permute-start | bytes 393224 | tf_op jit(solution)/shard_map/ppermute | solution.py:239
  46.5 18.5 %collective-permute-start.12 = (f32[64,512]{1,0:T(8,128)S(1)}, f32[64,512]{1,0:T(8,128)S(1)}, u32[]{:S(2)}, u32[]{:S(2)}) collective-permute-start(f32[64,512]{1,0:T(8,128)S(1)} %slice.64.refs_0_), channel_id=1, source_target_pairs={{0,4},{2,6},{4,0},{6,2},{8,12},{10,14},{12,8},{14,10},{1,5},{3,7},... | collective-permute-start | bytes 393224 | tf_op jit(solution)/shard_map/ppermute | solution.py:239
  47.0 18.0 %collective-permute-start.13 = (f32[64,512]{1,0:T(8,128)S(1)}, f32[64,512]{1,0:T(8,128)S(1)}, u32[]{:S(2)}, u32[]{:S(2)}) collective-permute-start(f32[64,512]{1,0:T(8,128)S(1)} %slice.64.refs_0_), channel_id=1, source_target_pairs={{0,6},{2,4},{4,2},{6,0},{8,14},{10,12},{12,10},{14,8},{1,7},{3,5},... | collective-permute-start | bytes 393224 | tf_op jit(solution)/shard_map/ppermute | solution.py:239
  50.1 15.0 %collective-permute-start.14 = (f32[64,512]{1,0:T(8,128)S(1)}, f32[64,512]{1,0:T(8,128)S(1)}, u32[]{:S(2)}, u32[]{:S(2)}) collective-permute-start(f32[64,512]{1,0:T(8,128)S(1)} %slice.65.refs_4_), channel_id=1, source_target_pairs={{0,2},{2,0},{4,6},{6,4},{8,10},{10,8},{12,14},{14,12},{1,3},{3,1},... | collective-permute-start | bytes 393224 | tf_op jit(solution)/shard_map/ppermute | solution.py:239
  50.2 14.8 %collective-permute-start.15 = (f32[64,512]{1,0:T(8,128)S(1)}, f32[64,512]{1,0:T(8,128)S(1)}, u32[]{:S(2)}, u32[]{:S(2)}) collective-permute-start(f32[64,512]{1,0:T(8,128)S(1)} %slice.65.refs_4_), channel_id=1, source_target_pairs={{0,4},{2,6},{4,0},{6,2},{8,12},{10,14},{12,8},{14,10},{1,5},{3,7},... | collective-permute-start | bytes 393224 | tf_op jit(solution)/shard_map/ppermute | solution.py:239
  51.7 13.4 %collective-permute-start.16 = (f32[64,512]{1,0:T(8,128)S(1)}, f32[64,512]{1,0:T(8,128)S(1)}, u32[]{:S(2)}, u32[]{:S(2)}) collective-permute-start(f32[64,512]{1,0:T(8,128)S(1)} %slice.65.refs_4_), channel_id=1, source_target_pairs={{0,6},{2,4},{4,2},{6,0},{8,14},{10,12},{12,10},{14,8},{1,7},{3,5},... | collective-permute-start | bytes 393224 | tf_op jit(solution)/shard_map/ppermute | solution.py:239

commit v2 on v0

v2 whole, which is shorter than its diff:
```python
import functools

import jax
import jax.numpy as jnp
from jax import lax
from jax.experimental import pallas as pl
from jax.experimental.pallas import tpu as pltpu
from jax.sharding import PartitionSpec as P

PANELS = 2
VMEM_LIMIT = 16 * 1024 * 1024
OWN_VMEM_LIMIT = 44 * 1024 * 1024
F32 = jnp.float32
BF16 = jnp.bfloat16
HIGHEST = lax.Precision.HIGHEST


def split(value):
    high = value.astype(BF16)
    return high, (value - high.astype(F32)).astype(BF16)


def dot_nt(a, b):
    return lax.dot_general(a, b, (((1,), (1,)), ((), ())), precision=HIGHEST, preferred_element_type=F32)


def prep_kernel(lead_ref, flipped_ref, mask_ref):
    edge = flipped_ref.shape[0]
    mask = lead_ref[:, edge:]
    flipped_ref[...] = (lead_ref[:, :edge] * mask[:, :, :1]).reshape(-1, edge).T
    mask_ref[...] = mask.reshape(mask_ref.shape)


def spread_mask(mask, columns, edge):
    blocks = mask.shape[1]
    over = lax.broadcasted_iota(jnp.int32, (blocks, columns), 1) // edge
    over = (over == lax.broadcasted_iota(jnp.int32, (blocks, columns), 0)).astype(F32)
    return jnp.dot(mask, over, preferred_element_type=F32)


def spread_front(dest_ref, leaf, per_front, rows):
    tile_count = dest_ref.shape[1]
    place = lax.broadcasted_iota(jnp.int32, (1, rows), 1) // (rows // tile_count)
    mine = jnp.zeros((1, rows), F32)
    for tile in range(tile_count):
        here = (dest_ref[0, tile] // per_front == leaf).astype(F32)
        mine = jnp.where(place == tile, here, mine)
    return mine


def by_front(lead, mine):
    return lead * mine, lead * (1.0 - mine)


def fill_factor(lhs, kept, sent, edge):
    for place, part in enumerate((kept, sent)):
        part_high, part_low = split(part)
        lhs[place * edge : (place + 1) * edge] = part_high
        lhs[(place + 2) * edge : (place + 3) * edge] = part_low


def panel_product(lhs, high, low, edge):
    big = jnp.dot(lhs, high, preferred_element_type=F32)
    small = jnp.dot(lhs[: 2 * edge], low, preferred_element_type=F32)
    return big[: 2 * edge] + (big[2 * edge :] + small)


def put_gram(blocks, out, edge):
    for near in range(out.shape[0]):
        place_slabs(blocks, out.at[near, edge:])


def halves_beside(block):
    return jnp.concatenate([block[: block.shape[0] // 2], block[block.shape[0] // 2 :]], axis=1)


def own_kernel(per_front, info_ref, dest_ref, mask_ref, lead_ref, tiles_ref, keep_ref, send_ref, high, low, mine_ref, lhs, held, wide_ref, total_ref, sems):
    tile_count, edge, columns = held.shape
    pieces, _, width = keep_ref.shape
    copies = [pltpu.make_async_copy(tiles_ref.at[tile], held.at[tile], sems.at[tile]) for tile in range(tile_count)]
    for copy in copies:
        copy.start()
    wide_ref[...] = spread_mask(mask_ref[...], columns, edge)
    mine_ref[...] = spread_front(dest_ref, info_ref[1], per_front, lead_ref.shape[1])
    lead = lead_ref[...]
    parts = by_front(lead, mine_ref[...])
    fill_factor(lhs, *parts, edge)
    gram = dot_nt(jnp.concatenate(parts, axis=0), lead)
    put_gram(halves_beside(gram[:edge]), keep_ref, edge)
    put_gram(halves_beside(gram[edge:]), send_ref, edge)
    group = max(1, 256 // edge)
    for first in range(0, tile_count, group):
        for tile in range(first, first + group):
            copies[tile].wait()
            value = held[tile] * wide_ref[tile : tile + 1, :]
            value_high, value_low = split(value)
            high[tile * edge : (tile + 1) * edge] = value_high
            low[tile * edge : (tile + 1) * edge] = value_low
        deep = slice(first * edge, (first + group) * edge)
        for piece in range(pieces):
            here = slice(piece * width, (piece + 1) * width)
            part = panel_product(lhs[:, deep], high[deep, here], low[deep, here], edge)
            if first + group < tile_count:
                total_ref[:, here] = part if first == 0 else total_ref[:, here] + part
                continue
            total = total_ref[:, here] + part if first else part
            near = jnp.bitwise_xor(info_ref[0], piece)
            keep_ref[near, :edge] = total[:edge]
            send_ref[near, :edge] = total[edge:]


def pair_kernel(with_other, info_ref, mine_ref, lead_ref, own_ref, high, low, keep_ref, send_ref, lhs):
    edge = lead_ref.shape[0]
    pieces, _, width = keep_ref.shape
    lead, own = lead_ref[...], own_ref[...]
    parts = by_front(lead, mine_ref[...])
    fill_factor(lhs, *parts, edge)
    both = jnp.concatenate(parts, axis=0)
    cross = dot_nt(both, own)
    other = dot_nt(both, lead) if with_other else None
    for place, out in enumerate((keep_ref, send_ref)):
        here = slice(place * edge, (place + 1) * edge)
        blocks = halves_beside(cross[here])
        if with_other:
            blocks = jnp.concatenate([blocks, halves_beside(other[here])], axis=0)
        put_gram(blocks, out, edge)
    for piece in range(pieces):
        here = slice(piece * width, (piece + 1) * width)
        total = panel_product(lhs[...], high[:, here], low[:, here], edge)
        near = jnp.bitwise_xor(info_ref[0], piece)
        keep_ref[near, :edge] = total[:edge]
        send_ref[near, :edge] = total[edge:]


def place_slabs(value, out):
    across = out.shape[1] // value.shape[1]
    for slab in range(value.shape[0] // 8):
        down, right = slab // across, slab % across
        out[down * 8 : (down + 1) * 8, right * 128 : (right + 1) * 128] = value[slab * 8 : (slab + 1) * 8]


def take_block(ref, edge, start=0):
    across = ref.shape[1] // 128
    slabs = []
    for slab in range(start, start + edge // 16):
        down, right = slab // across, slab % across
        slabs.append(ref[down * 8 : (down + 1) * 8, right * 128 : (right + 1) * 128])
    value = jnp.concatenate(slabs, axis=0)
    return jnp.concatenate([value[:, :edge], value[:, edge:]], axis=0)


STEP = 8


def inverse_factor(whole, put):
    size = whole.shape[0]
    groups = size // 8
    rows = [whole[8 * i : 8 * i + 8] for i in range(groups)]
    lane = lax.broadcasted_iota(jnp.int32, (8, size), 1)
    down = lax.broadcasted_iota(jnp.int32, (8, size), 0)
    span = range(STEP)
    for k in range(0, size, STEP):
        group, inside = k // 8, k % 8
        pivot = [jnp.broadcast_to(rows[group][inside + j : inside + j + 1], (8, size)) for j in span]
        entry = [[jnp.broadcast_to(pivot[i][:, k + j : k + j + 1], (8, size)) for j in range(i + 1)] for i in span]
        ratio = [[None] * STEP for _ in span]
        inverse = [None] * STEP
        for j in span:
            inverse[j] = 1.0 / entry[j][j]
            for i in range(j + 1, STEP):
                ratio[i][j] = entry[i][j] * inverse[j]
            for i in range(j + 1, STEP):
                for m in range(j + 1, i + 1):
                    entry[i][m] = entry[i][m] - ratio[i][j] * entry[m][j]
        solved = []
        for j in span:
            unit = jnp.where(lane < k, pivot[j], jnp.where(lane == k + j, 1.0, 0.0))
            for i in range(j):
                unit = unit - ratio[j][i] * solved[i]
            solved.append(unit)
            put(k + j, (unit * lax.rsqrt(entry[j][j]))[:1])
        if k + STEP == size:
            break
        front = [jnp.where(lane == k + j, pivot[j] + 1.0, pivot[j]) for j in span]
        for j in span:
            for i in range(j):
                front[j] = front[j] - ratio[j][i] * front[i]
        back = [front[j] * inverse[j] for j in span]
        for j in reversed(span):
            for i in range(j + 1, STEP):
                back[j] = back[j] - ratio[i][j] * back[i]
        for g in range((k + STEP) // 8, groups):
            change = None
            for j in span:
                term = jnp.broadcast_to(rows[g][:, k + j : k + j + 1], (8, size)) * back[j]
                change = term if change is None else change + term
            if g == group:
                change = jnp.where(down < inside + STEP, 0.0, change)
            rows[g] = rows[g] - change


def both_grams(info_ref, own_ref, other_ref, other_start, edge):
    own, other = take_block(own_ref, edge), take_block(other_ref, edge, other_start)
    first = info_ref[2] == 0
    return jnp.where(first, own, other), jnp.where(first, other, own)


def first_factor_kernel(start, info_ref, own_ref, other_ref, out_ref):
    edge = out_ref.shape[0]
    gram, _ = both_grams(info_ref, own_ref, other_ref, start, edge)

    def put(index, row):
        out_ref[index : index + 1] = row

    inverse_factor(gram, put)


def rest_factor_kernel(start, info_ref, own_ref, other_ref, pair_ref, corner_ref, out_ref):
    edge = corner_ref.shape[0]
    _, gram = both_grams(info_ref, own_ref, other_ref, start, edge)
    cross = take_block(pair_ref, edge)
    cross = jnp.where(info_ref[2] == 0, cross, cross.T)
    corner = corner_ref[...]
    lower = dot_nt(cross, corner)
    both = jnp.dot(lower, corner, precision=HIGHEST, preferred_element_type=F32)
    out_ref[:edge, :edge] = corner
    out_ref[:edge, edge:] = jnp.zeros_like(corner)

    def put(index, row):
        out_ref[edge + index : edge + index + 1, edge:] = row

    inverse_factor(gram - dot_nt(lower, lower), put)
    out_ref[edge:, :edge] = -jnp.dot(out_ref[edge:, edge:], both, precision=HIGHEST, preferred_element_type=F32)


def final_kernel(pieces, edge, info_ref, inverse_ref, *refs):
    own_refs, other_refs, (out_ref, held, sems) = refs[:pieces], refs[pieces : 2 * pieces], refs[2 * pieces :]
    width = own_refs[0].shape[1]
    inverse = inverse_ref[...]
    first = info_ref[2] == 0
    left, right = inverse[:, :edge], inverse[:, edge:]
    inverse = jnp.concatenate([jnp.where(first, left, right), jnp.where(first, right, left)], axis=1)
    inverse_high, inverse_low = split(inverse)
    both = jnp.concatenate([inverse_high, inverse_low], axis=0)
    row = lax.broadcasted_iota(jnp.int32, (2 * edge, width), 0)
    lane = lax.broadcasted_iota(jnp.int32, (2 * edge, width), 1)
    copies = []
    for near in range(pieces):
        part = jnp.concatenate([own_refs[near][:edge], other_refs[near][:edge]], axis=0)
        part_high, part_low = split(part)
        product = jnp.dot(both, part_high, preferred_element_type=F32)
        small = jnp.dot(inverse_high, part_low, preferred_element_type=F32)
        product = product[: 2 * edge] + (product[2 * edge :] + small)
        place = jnp.bitwise_xor(info_ref[0], near)
        place_lane = lane + place * width
        early = (place_lane < edge) & (place_lane + info_ref[3] * edge < row)
        held[near] = jnp.where(early, 0.0, product)
        copy = pltpu.make_async_copy(
            held.at[near],
            out_ref.at[0, :, pl.ds(pl.multiple_of(place * width, width), width)],
            sems.at[near],
        )
        copy.start()
        copies.append(copy)
    for copy in copies:
        copy.wait()


def vmem():
    return pl.BlockSpec(memory_space=pltpu.VMEM)


def smem():
    return pl.BlockSpec(memory_space=pltpu.SMEM)


def per_device(child_tiles, block_mask, destination):
    tile_count, edge, columns = child_tiles.shape
    rows = tile_count * edge
    row_count, col_count = lax.axis_size("row"), lax.axis_size("col")
    bits = row_count.bit_length() - 1
    split_bits = min(2, bits - 1, (columns // 128).bit_length() - 1)
    pieces = 1 << split_bits
    width = columns // pieces
    row, leaf, col = lax.axis_index("row"), lax.axis_index("leaf"), lax.axis_index("col")
    own_panel = col if col_count == PANELS else jnp.zeros_like(col)
    info = jnp.stack([row % pieces, leaf, own_panel, col]).astype(jnp.int32)
    params = pltpu.CompilerParams(vmem_limit_bytes=VMEM_LIMIT)
    wide_params = pltpu.CompilerParams(vmem_limit_bytes=OWN_VMEM_LIMIT)

    blocks = columns // edge
    mask_row = jnp.pad(block_mask.astype(F32), ((0, 0), (0, edge - blocks)))[:, None]
    lead, mask = pl.pallas_call(
        prep_kernel,
        out_shape=(jax.ShapeDtypeStruct((edge, rows), F32), jax.ShapeDtypeStruct((tile_count, edge), F32)),
        in_specs=[vmem()],
        out_specs=(vmem(), vmem()),
        compiler_params=params,
        name="lead_prep",
    )(jnp.concatenate([child_tiles[:, :, :edge], mask_row], axis=1))

    if col_count == PANELS:
        lead_own = lead
        lead_other = lax.ppermute(lead, "col", [(i, 1 - i) for i in range(PANELS)])
    else:
        gathered = lax.all_gather(lead, "col")
        lead_own, lead_other = gathered[0], gathered[1]

    swap = col_count == PANELS
    gram_rows = edge * edge // width
    factor = pltpu.VMEM((4 * edge, rows), BF16)
    work = pl.CostEstimate(flops=12 * edge * rows * columns, bytes_accessed=4 * rows * columns, transcendentals=0)

    def sums(extra):
        return jax.ShapeDtypeStruct((pieces, edge + extra, width), F32)

    halves = jax.ShapeDtypeStruct((rows, columns), BF16)
    keep, send, high, low, mine = pl.pallas_call(
        functools.partial(own_kernel, row_count),
        out_shape=(sums(gram_rows), sums(gram_rows), halves, halves, jax.ShapeDtypeStruct((1, rows), F32)),
        in_specs=[smem(), smem(), vmem(), vmem(), pl.BlockSpec(memory_space=pl.ANY)],
        out_specs=(vmem(),) * 5,
        scratch_shapes=[
            factor,
            pltpu.VMEM((tile_count, edge, columns), F32),
            pltpu.VMEM((tile_count, columns), F32),
            pltpu.VMEM((2 * edge, columns), F32),
            pltpu.SemaphoreType.DMA((tile_count,)),
        ],
        compiler_params=wide_params,
        cost_estimate=work,
        name="panel_own",
    )(info, destination.reshape(1, tile_count), mask, lead_own, child_tiles)

    def over_leaf(keep, send):
        return keep + lax.ppermute(send, "leaf", [(0, 1), (1, 0)])

    def over_row(value, bit):
        return lax.ppermute(value, "row", [(i, i ^ bit) for i in range(row_count)])

    def reduce_near(partial):
        total = partial[0]
        for near in range(1, pieces):
            total = total + over_row(partial[near], near)
        return total

    def reduce_far(total):
        for bit in range(split_bits, bits):
            total = total + over_row(total, 1 << bit)
        return total

    def gather_pieces(total):
        return [total[:edge]] + [over_row(total[:edge], near) for near in range(1, pieces)]

    send, lead_other = lax.optimization_barrier((send, lead_other))
    own_sum = reduce_far(reduce_near(over_leaf(keep, send)))
    own_pieces = gather_pieces(own_sum)

    pair_rows = gram_rows if swap else 2 * gram_rows
    keep, send = pl.pallas_call(
        functools.partial(pair_kernel, not swap),
        out_shape=(sums(pair_rows), sums(pair_rows)),
        in_specs=[smem(), vmem(), vmem(), vmem(), vmem(), vmem()],
        out_specs=(vmem(),) * 2,
        scratch_shapes=[factor],
        compiler_params=params,
        cost_estimate=work,
        name="panel_pair",
    )(info, mine, lead_other, lead_own, high, low)
    other_sum = reduce_far(reduce_near(over_leaf(keep, send)))

    own_gram = own_sum[edge:]
    if swap:
        other_gram, start = lax.ppermute(own_gram, "col", [(i, 1 - i) for i in range(PANELS)]), 0
    else:
        other_gram, start = other_sum[edge:], edge // 16
    corner = pl.pallas_call(
        functools.partial(first_factor_kernel, start),
        out_shape=jax.ShapeDtypeStruct((edge, edge), F32),
        in_specs=[smem(), vmem(), vmem()],
        out_specs=vmem(),
        compiler_params=params,
        cost_estimate=pl.CostEstimate(flops=work.flops // 2, bytes_accessed=work.bytes_accessed // 2, transcendentals=0),
        name="gram_factor_first",
    )(info, own_gram, other_gram)
    if swap:
        other_sum, corner = lax.optimization_barrier((other_sum, corner))
    other_pieces = gather_pieces(other_sum)
    pair_gram = other_sum[edge:]
    inverse = pl.pallas_call(
        functools.partial(rest_factor_kernel, start),
        out_shape=jax.ShapeDtypeStruct((2 * edge, 2 * edge), F32),
        in_specs=[smem()] + [vmem()] * 4,
        out_specs=vmem(),
        compiler_params=params,
        name="gram_factor_rest",
    )(info, own_gram, other_gram, pair_gram, corner)

    return pl.pallas_call(
        functools.partial(final_kernel, pieces, edge),
        out_shape=jax.ShapeDtypeStruct((1, 2 * edge, columns), F32),
        in_specs=[smem(), vmem()] + [vmem()] * (2 * pieces),
        out_specs=pl.BlockSpec(memory_space=pl.ANY),
        scratch_shapes=[pltpu.VMEM((pieces, 2 * edge, width), F32), pltpu.SemaphoreType.DMA((pieces,))],
        compiler_params=params,
        name="apply_inverse",
    )(info, inverse, *own_pieces, *other_pieces)


def solution(mesh):
    in_specs = (
        P(("leaf", "row"), None, "col"),
        P(("leaf", "row"), "col"),
        P(("leaf", "row"), None),
    )
    out_specs = P("leaf", None, "col")
    return jax.shard_map(per_device, mesh=mesh, in_specs=in_specs, out_specs=out_specs, check_vma=False)
```

time: 612 us -> 58.5 us (0.10)
  blocking collectives: 371 us -> 0 us
  waiting for transfers between devices: 98.5 us -> 12 us
  local copies, waits for them, and re-layouts: 61.4 us -> 1.83 us
  other arithmetic: 36.5 us -> 1.16 us
  matrix products: 30 us -> 0 us
  starting transfers between devices: 0.04 us -> 24.9 us
  Pallas kernels: 0 us -> 18.2 us
  between operations: 13.5 us -> 0.17 us
    all_to_all x1 -> x0, blocking collectives: 371 us -> none  [per_device(): lax.all_to_all(packed.reshape(targets_all, CAP, block_size, columns_dev),...]
    psum x1 -> x0, waiting for transfers between devices: 79.3 us -> none  [per_device(): gram_sum, cross_sum = lax.psum((gram_part, cross_part), 'row')]
    dot_general x3 -> x0, matrix products: 26.7 us -> none  [the longest x1 15.9 us: per_device(): jnp.dot(leading_rows.T, front_rows, precision=lax.Precision.HIGHEST)]
    ppermute x0 -> x18, starting transfers between devices: none -> 24.9 us  [the longest x14 20.3 us: over_row(): return lax.ppermute(value, 'row', [(i, i ^ bit) for i in range(row_count)])]
    mul x2 -> x0, local copies, waits for them, and re-layouts: 23.3 us -> none  [per_device(): masked_tiles * block_mask.astype(jnp.float32)[:, None, :, None]]
    another operation x6 -> x1, other arithmetic: 22.9 us -> 0.08 us  [per_device(): info = jnp.stack([row % pieces, leaf, own_panel, col]).astype(jnp.int32)]
    all_gather x1 -> x0, waiting for transfers between devices: 19.2 us -> none  [per_device(): gathered = lax.all_gather(local_lead, 'col', axis=1, tiled=True)]
    dot_general x1 -> x0, local copies, waits for them, and re-layouts: 18.6 us -> none  [per_device(): jnp.dot(placing, masked_tiles.reshape(tile_count, block_size * columns_de...]
  transfers between devices with their start and end apart: 2 -> 18, of which waited for: 2 -> 7; matrix products, arithmetic and copies ran while one was open for 0% -> 1% of each run, Pallas kernels for 0% -> 28%
where the time goes in v2:
time: 58.5 us; the launch traced here: 58.3 us
  starting transfers between devices  24.9 us (43%)
  Pallas kernels  18.2 us (31%)
  waiting for transfers between devices  12 us (21%)
  local copies, waits for them, and re-layouts  1.83 us (3%)
  other arithmetic  1.16 us (2%)
    ppermute x14, starting transfers between devices, over_row(): return lax.ppermute(value, 'row', [(i, i ^ bit) for i in range(row_count)])  20.3 us
    ppermute x14, waiting for transfers between devices, over_row(): return lax.ppermute(value, 'row', [(i, i ^ bit) for i in range(row_count)])  12 us
    pallas_call x1, Pallas kernels, per_device(): pl.pallas_call(functools.partial(own_kernel, row_count), out_shape=(sums(...  6.31 us
    pallas_call x1, Pallas kernels, per_device(): pl.pallas_call(functools.partial(rest_factor_kernel, start), out_shape=ja...  3.97 us
    pallas_call x1, Pallas kernels, per_device(): pl.pallas_call(functools.partial(first_factor_kernel, start), out_shape=j...  3.06 us
    ppermute x1, starting transfers between devices, per_device(): lead_other = lax.ppermute(lead, 'col', [(i, 1 - i) for i in range(PANELS)])  3.03 us
    pallas_call x1, Pallas kernels, per_device(): pl.pallas_call(functools.partial(pair_kernel, not swap), out_shape=(sums(...  2.73 us
    pallas_call x1, Pallas kernels, per_device(): pl.pallas_call(functools.partial(final_kernel, pieces, edge), out_shape=j...  1.93 us
  transfers between devices with their start and end apart: 18, of which 7 were waited for; matrix products, arithmetic and copies ran while one was open for 1% of the time, Pallas kernels for 28%

profile of v2, /device:TPU:0, one launch (start us, length us, event | category | flops | bytes accessed | tf_op | source)
XLA Modules:
  0.0 58.3 jit_solution(7491430289521481200)
XLA Ops:
  0.0 1.1 %slice.45 = f32[16,64,64]{2,1,0:T(8,128)S(1)} slice(f32[16,64,2048]{2,1,0:T(8,128)} %tiles_ref.1), slice={[0:16], [0:64], [0:64]} | slice | bytes 524288 | tf_op jit(solution)/shard_map/slice | solution.py:300
  1.1 0.7 %convert_element_type.5 = f32[16,32]{1,0:T(8,128)S(1)} convert(s32[16,32]{1,0:T(8,128)} %param.4) | non-fusion elementwise | flops 512 | bytes 4096 | tf_op jit(solution)/shard_map/convert_element_type | solution.py:292
  1.8 0.2 lead_prep.1
  2.1 3.0 %collective-permute-start = (f32[64,1024]{1,0:T(8,128)S(1)}, f32[64,1024]{1,0:T(8,128)S(1)}, u32[]{:S(2)}, u32[]{:S(2)}) collective-permute-start(f32[64,1024]{1,0:T(8,128)S(1)} %get-tuple-element.19.lead_ref.own_ref), channel_id=1, source_target_pairs={{0,1},{1,0},{2,3},{3,2},{4,5},{5,4},{6,7},{7,6},{8,9},{9,8},{10,11... | collective-permute-start | bytes 786440 | tf_op jit(solution)/shard_map/ppermute | solution.py:304
  5.1 0.1 pad_add_fusion.info_ref
  5.2 0.0 copy-start
  5.2 0.7 %copy-done = s32[16,1]{0,1:T(1,128)S(1)} copy-done((s32[16,1]{0,1:T(1,128)S(1)}, s32[16,1]{0,1:T(1,128)}, u32[]{:S(2)}) %copy-start) | copy-done | bytes 88
  5.8 6.3 %panel_own.1 = (f32[4,72,512]{2,1,0:T(8,128)S(1)}, f32[4,72,512]{2,1,0:T(8,128)S(1)}, bf16[1024,2048]{1,0:T(8,128)(2,1)S(1)}, bf16[1024,2048]{1,0:T(8,128)(2,1)S(1)}, f32[1,1024]{1,0:T(1,128)S(1)}) custom-call(s32[4]{0:T(128)S(1)} %pad_add_fusion.info_ref, s32[1,16]{1,0:T(1,128)S(1)} %bitcast.33, f32[16,64]{1,0:T(8,128)S(1)} %get-tuple-element.18.mask_ref, ...), custom_call_target="tpu_custom_call" | custom-call | flops 1610612736 | bytes 8388608 | tf_op jit(solution)/shard_map/panel_own/pallas_call | solution.py:318
  12.2 0.0 collective-permute-done.lead_ref
  12.2 0.1 collective-permute-start.1
  12.2 2.7 %panel_pair.1 = (f32[4,72,512]{2,1,0:T(8,128)S(1)}, f32[4,72,512]{2,1,0:T(8,128)S(1)}) custom-call(s32[4]{0:T(128)S(1)} %pad_add_fusion.info_ref, f32[1,1024]{1,0:T(1,128)S(1)} %get-tuple-element.23.mine_ref, f32[64,1024]{1,0:T(8,128)S(1)} %collective-permute-done.lead_ref, f32[64,1024]{1,0:T(8,128)S(1)} %get-tuple-element.19.lead_ref.own_ref, ...), custom_call_target="tpu_custom_call" | custom-call | flops 1610612736 | bytes 8388608 | tf_op jit(solution)/shard_map/panel_pair/pallas_call | solution.py:360
  15.0 0.6 collective-permute-start.7
  15.5 0.0 collective-permute-done.1
  15.5 0.1 add.37
  15.7 1.6 %collective-permute-start.2 = (f32[72,512]{1,0:T(8,128)S(1)}, f32[72,512]{1,0:T(8,128)S(1)}, u32[]{:S(2)}, u32[]{:S(2)}) collective-permute-start(f32[72,512]{1,0:T(8,128)S(1)} %get-tuple-element.34), channel_id=1, source_target_pairs={{0,2},{2,0},{4,6},{6,4},{8,10},{10,8},{12,14},{14,12},{1,3},{3,1},... | collective-permute-start | bytes 442376 | tf_op jit(solution)/shard_map/ppermute | solution.py:339
  17.2 1.6 %collective-permute-start.3 = (f32[72,512]{1,0:T(8,128)S(1)}, f32[72,512]{1,0:T(8,128)S(1)}, u32[]{:S(2)}, u32[]{:S(2)}) collective-permute-start(f32[72,512]{1,0:T(8,128)S(1)} %get-tuple-element.36), channel_id=1, source_target_pairs={{0,4},{2,6},{4,0},{6,2},{8,12},{10,14},{12,8},{14,10},{1,5},{3,7},... | collective-permute-start | bytes 442376 | tf_op jit(solution)/shard_map/ppermute | solution.py:339
  18.8 0.4 collective-permute-start.4
  19.2 0.0 collective-permute-done.7
  19.2 0.1 add.42
  19.4 2.6 %collective-permute-start.10 = (f32[72,512]{1,0:T(8,128)S(1)}, f32[72,512]{1,0:T(8,128)S(1)}, u32[]{:S(2)}, u32[]{:S(2)}) collective-permute-start(f32[72,512]{1,0:T(8,128)S(1)} %get-tuple-element.32), channel_id=1, source_target_pairs={{0,6},{2,4},{4,2},{6,0},{8,14},{10,12},{12,10},{14,8},{1,7},{3,5},... | collective-permute-start | bytes 442376 | tf_op jit(solution)/shard_map/ppermute | solution.py:339
  21.9 0.5 collective-permute-start.8
  22.5 0.0 collective-permute-done.2
  22.5 0.7 %collective-permute-start.9 = (f32[72,512]{1,0:T(8,128)S(1)}, f32[72,512]{1,0:T(8,128)S(1)}, u32[]{:S(2)}, u32[]{:S(2)}) collective-permute-start(f32[72,512]{1,0:T(8,128)S(1)} %get-tuple-element.33), channel_id=1, source_target_pairs={{0,4},{2,6},{4,0},{6,2},{8,12},{10,14},{12,8},{14,10},{1,5},{3,7},... | collective-permute-start | bytes 442376 | tf_op jit(solution)/shard_map/ppermute | solution.py:339
  23.2 0.8 %collective-permute-done.3 = f32[72,512]{1,0:T(8,128)S(1)} collective-permute-done((f32[72,512]{1,0:T(8,128)S(1)}, f32[72,512]{1,0:T(8,128)S(1)}, u32[]{:S(2)}, u32[]{:S(2)}) %collective-permute-start.3) | collective-permute-done | bytes 147488 | tf_op jit(solution)/shard_map/ppermute | solution.py:339
  24.0 2.9 %collective-permute-done.4 = f32[72,512]{1,0:T(8,128)S(1)} collective-permute-done((f32[72,512]{1,0:T(8,128)S(1)}, f32[72,512]{1,0:T(8,128)S(1)}, u32[]{:S(2)}, u32[]{:S(2)}) %collective-permute-start.4) | collective-permute-done | bytes 147488 | tf_op jit(solution)/shard_map/ppermute | solution.py:339
  26.9 2.7 %collective-permute-start.5 = (f32[72,512]{1,0:T(8,128)S(1)}, f32[72,512]{1,0:T(8,128)S(1)}, u32[]{:S(2)}, u32[]{:S(2)}) collective-permute-start(f32[72,512]{1,0:T(8,128)S(1)} %fusion.5), channel_id=1, source_target_pairs={{0,8},{2,10},{4,12},{6,14},{8,0},{10,2},{12,4},{14,6},{1,9},{3,11}... | collective-permute-start | bytes 442376 | tf_op jit(solution)/shard_map/ppermute | solution.py:339
  29.6 2.0 %collective-permute-done.10 = f32[72,512]{1,0:T(8,128)S(1)} collective-permute-done((f32[72,512]{1,0:T(8,128)S(1)}, f32[72,512]{1,0:T(8,128)S(1)}, u32[]{:S(2)}, u32[]{:S(2)}) %collective-permute-start.10) | collective-permute-done | bytes 147488 | tf_op jit(solution)/shard_map/ppermute | solution.py:339
  31.6 0.5 collective-permute-done.8
  32.1 3.3 %collective-permute-done.9 = f32[72,512]{1,0:T(8,128)S(1)} collective-permute-done((f32[72,512]{1,0:T(8,128)S(1)}, f32[72,512]{1,0:T(8,128)S(1)}, u32[]{:S(2)}, u32[]{:S(2)}) %collective-permute-start.9) | collective-permute-done | bytes 147488 | tf_op jit(solution)/shard_map/ppermute | solution.py:339
  35.4 0.1 fusion.2
  35.5 1.0 %collective-permute-start.11 = (f32[72,512]{1,0:T(8,128)S(1)}, f32[72,512]{1,0:T(8,128)S(1)}, u32[]{:S(2)}, u32[]{:S(2)}) collective-permute-start(f32[72,512]{1,0:T(8,128)S(1)} %fusion.2), channel_id=1, source_target_pairs={{0,8},{2,10},{4,12},{6,14},{8,0},{10,2},{12,4},{14,6},{1,9},{3,11}... | collective-permute-start | bytes 442376 | tf_op jit(solution)/shard_map/ppermute | solution.py:339
  36.5 0.0 collective-permute-done.5
  36.5 0.1 collective-permute-start.12
  36.7 0.9 %collective-permute-start.6 = (f32[8,512]{1,0:T(8,128)S(1)}, f32[8,512]{1,0:T(8,128)S(1)}, u32[]{:S(2)}, u32[]{:S(2)}) collective-permute-start(f32[8,512]{1,0:T(8,128)S(1)} %slice.62.own_ref), channel_id=1, source_target_pairs={{0,1},{1,0},{2,3},{3,2},{4,5},{5,4},{6,7},{7,6},{8,9},{9,8},{10,11... | collective-permute-start | bytes 49160 | tf_op jit(solution)/shard_map/ppermute | solution.py:374
  37.6 5.6 %collective-permute-start.13 = (f32[64,512]{1,0:T(8,128)S(1)}, f32[64,512]{1,0:T(8,128)S(1)}, u32[]{:S(2)}, u32[]{:S(2)}) collective-permute-start(f32[64,512]{1,0:T(8,128)S(1)} %slice.67.refs_0_), channel_id=1, source_target_pairs={{0,4},{2,6},{4,0},{6,2},{8,12},{10,14},{12,8},{14,10},{1,5},{3,7},... | collective-permute-start | bytes 393224 | tf_op jit(solution)/shard_map/ppermute | solution.py:339
  43.2 0.0 collective-permute-start.14
  43.2 1.0 %collective-permute-done.11 = f32[72,512]{1,0:T(8,128)S(1)} collective-permute-done((f32[72,512]{1,0:T(8,128)S(1)}, f32[72,512]{1,0:T(8,128)S(1)}, u32[]{:S(2)}, u32[]{:S(2)}) %collective-permute-start.11) | collective-permute-done | bytes 147488 | tf_op jit(solution)/shard_map/ppermute | solution.py:339
  44.2 0.0 collective-permute-done.6.other_ref
  44.2 3.1 %gram_factor_first.1.corner_ref = f32[64,64]{1,0:T(8,128)S(1)} custom-call(s32[4]{0:T(128)S(1)} %pad_add_fusion.info_ref, f32[8,512]{1,0:T(8,128)S(1)} %slice.62.own_ref, f32[8,512]{1,0:T(8,128)S(1)} %collective-permute-done.6.other_ref), custom_call_target="tpu_custom_call" | custom-call | flops 805306368 | bytes 4194304 | tf_op jit(solution)/shard_map/gram_factor_first/pallas_call | solution.py:377
  47.3 0.5 collective-permute-start.15
  47.9 2.0 %collective-permute-start.16 = (f32[64,512]{1,0:T(8,128)S(1)}, f32[64,512]{1,0:T(8,128)S(1)}, u32[]{:S(2)}, u32[]{:S(2)}) collective-permute-start(f32[64,512]{1,0:T(8,128)S(1)} %slice.57.refs_4_), channel_id=1, source_target_pairs={{0,4},{2,6},{4,0},{6,2},{8,12},{10,14},{12,8},{14,10},{1,5},{3,7},... | collective-permute-start | bytes 393224 | tf_op jit(solution)/shard_map/ppermute | solution.py:339
  49.9 0.0 collective-permute-done.12.refs_1_
  49.9 1.0 %collective-permute-start.17 = (f32[64,512]{1,0:T(8,128)S(1)}, f32[64,512]{1,0:T(8,128)S(1)}, u32[]{:S(2)}, u32[]{:S(2)}) collective-permute-start(f32[64,512]{1,0:T(8,128)S(1)} %slice.57.refs_4_), channel_id=1, source_target_pairs={{0,6},{2,4},{4,2},{6,0},{8,14},{10,12},{12,10},{14,8},{1,7},{3,5},... | collective-permute-start | bytes 393224 | tf_op jit(solution)/shard_map/ppermute | solution.py:339
  50.9 4.0 %gram_factor_rest.1.inverse_ref = f32[128,128]{1,0:T(8,128)S(1)} custom-call(s32[4]{0:T(128)S(1)} %pad_add_fusion.info_ref, f32[8,512]{1,0:T(8,128)S(1)} %slice.62.own_ref, f32[8,512]{1,0:T(8,128)S(1)} %collective-permute-done.6.other_ref, f32[8,512]{1,0:T(8,128)S(1)} %slice.55.pair_ref, f32[64,64]{1,0:T(8,128)S(1)} %gram_factor_first.1.corner_ref), custom_call_target="tpu_custom_call" | custom-call | tf_op jit(solution)/shard_map/gram_factor_rest/pallas_call | solution.py:390
  54.9 0.0 collective-permute-done.13.refs_2_
  54.9 0.0 collective-permute-done.14.refs_3_
  54.9 0.0 collective-permute-done.15.refs_5_
  54.9 0.0 collective-permute-done.16.refs_6_
  54.9 1.4 %collective-permute-done.17.refs_7_ = f32[64,512]{1,0:T(8,128)S(1)} collective-permute-done((f32[64,512]{1,0:T(8,128)S(1)}, f32[64,512]{1,0:T(8,128)S(1)}, u32[]{:S(2)}, u32[]{:S(2)}) %collective-permute-start.17) | collective-permute-done | bytes 131104 | tf_op jit(solution)/shard_map/ppermute | solution.py:339
  56.3 1.9 %apply_inverse.1 = f32[1,128,2048]{2,1,0:T(8,128)} custom-call(s32[4]{0:T(128)S(1)} %pad_add_fusion.info_ref, f32[128,128]{1,0:T(8,128)S(1)} %gram_factor_rest.1.inverse_ref, f32[64,512]{1,0:T(8,128)S(1)} %slice.67.refs_0_, f32[64,512]{1,0:T(8,128)S(1)} %collective-permute-done.12.refs_1_, f32[64,512]{1,0:T(8,128)S(1)} %collective-permute-done.13.refs_2_, ...), custom_call_target="tpu_custom_call" | custom-call | tf_op jit(solution)/shard_map/apply_inverse/pallas_call | solution.py:399
  (11 shorter events, 0.2 us)
Async XLA Ops:
  2.1 10.1 %collective-permute-start = (f32[64,1024]{1,0:T(8,128)S(1)}, f32[64,1024]{1,0:T(8,128)S(1)}, u32[]{:S(2)}, u32[]{:S(2)}) collective-permute-start(f32[64,1024]{1,0:T(8,128)S(1)} %get-tuple-element.19.lead_ref.own_ref), channel_id=1, source_target_pairs={{0,1},{1,0},{2,3},{3,2},{4,5},{5,4},{6,7},{7,6},{8,9},{9,8},{10,11... | collective-permute-start | bytes 786440 | tf_op jit(solution)/shard_map/ppermute | solution.py:304
  5.2 0.7 %copy-start = (s32[16,1]{0,1:T(1,128)S(1)}, s32[16,1]{0,1:T(1,128)}, u32[]{:S(2)}) copy-start(s32[16,1]{0,1:T(1,128)} %param.5) | copy-start | bytes 196
  12.2 3.4 %collective-permute-start.1 = (f32[4,72,512]{2,1,0:T(8,128)S(1)}, f32[4,72,512]{2,1,0:T(8,128)S(1)}, u32[]{:S(2)}, u32[]{:S(2)}) collective-permute-start(f32[4,72,512]{2,1,0:T(8,128)S(1)} %get-tuple-element.22), channel_id=1, source_target_pairs={{0,16},{16,0},{1,17},{17,1},{2,18},{18,2},{3,19},{19,3},{4,20},{20... | collective-permute-start | bytes 1769480 | tf_op jit(solution)/shard_map/ppermute | solution.py:336
  15.0 4.3 %collective-permute-start.7 = (f32[4,72,512]{2,1,0:T(8,128)S(1)}, f32[4,72,512]{2,1,0:T(8,128)S(1)}, u32[]{:S(2)}, u32[]{:S(2)}) collective-permute-start(f32[4,72,512]{2,1,0:T(8,128)S(1)} %get-tuple-element.28), channel_id=1, source_target_pairs={{0,16},{16,0},{1,17},{17,1},{2,18},{18,2},{3,19},{19,3},{4,20},{20... | collective-permute-start | bytes 1769480 | tf_op jit(solution)/shard_map/ppermute | solution.py:336
  15.7 6.8 %collective-permute-start.2 = (f32[72,512]{1,0:T(8,128)S(1)}, f32[72,512]{1,0:T(8,128)S(1)}, u32[]{:S(2)}, u32[]{:S(2)}) collective-permute-start(f32[72,512]{1,0:T(8,128)S(1)} %get-tuple-element.34), channel_id=1, source_target_pairs={{0,2},{2,0},{4,6},{6,4},{8,10},{10,8},{12,14},{14,12},{1,3},{3,1},... | collective-permute-start | bytes 442376 | tf_op jit(solution)/shard_map/ppermute | solution.py:339
  17.2 6.8 %collective-permute-start.3 = (f32[72,512]{1,0:T(8,128)S(1)}, f32[72,512]{1,0:T(8,128)S(1)}, u32[]{:S(2)}, u32[]{:S(2)}) collective-permute-start(f32[72,512]{1,0:T(8,128)S(1)} %get-tuple-element.36), channel_id=1, source_target_pairs={{0,4},{2,6},{4,0},{6,2},{8,12},{10,14},{12,8},{14,10},{1,5},{3,7},... | collective-permute-start | bytes 442376 | tf_op jit(solution)/shard_map/ppermute | solution.py:339
  18.8 8.1 %collective-permute-start.4 = (f32[72,512]{1,0:T(8,128)S(1)}, f32[72,512]{1,0:T(8,128)S(1)}, u32[]{:S(2)}, u32[]{:S(2)}) collective-permute-start(f32[72,512]{1,0:T(8,128)S(1)} %get-tuple-element.35), channel_id=1, source_target_pairs={{0,6},{2,4},{4,2},{6,0},{8,14},{10,12},{12,10},{14,8},{1,7},{3,5},... | collective-permute-start | bytes 442376 | tf_op jit(solution)/shard_map/ppermute | solution.py:339
  19.4 12.2 %collective-permute-start.10 = (f32[72,512]{1,0:T(8,128)S(1)}, f32[72,512]{1,0:T(8,128)S(1)}, u32[]{:S(2)}, u32[]{:S(2)}) collective-permute-start(f32[72,512]{1,0:T(8,128)S(1)} %get-tuple-element.32), channel_id=1, source_target_pairs={{0,6},{2,4},{4,2},{6,0},{8,14},{10,12},{12,10},{14,8},{1,7},{3,5},... | collective-permute-start | bytes 442376 | tf_op jit(solution)/shard_map/ppermute | solution.py:339
  21.9 10.1 %collective-permute-start.8 = (f32[72,512]{1,0:T(8,128)S(1)}, f32[72,512]{1,0:T(8,128)S(1)}, u32[]{:S(2)}, u32[]{:S(2)}) collective-permute-start(f32[72,512]{1,0:T(8,128)S(1)} %get-tuple-element.31), channel_id=1, source_target_pairs={{0,2},{2,0},{4,6},{6,4},{8,10},{10,8},{12,14},{14,12},{1,3},{3,1},... | collective-permute-start | bytes 442376 | tf_op jit(solution)/shard_map/ppermute | solution.py:339
  22.5 12.9 %collective-permute-start.9 = (f32[72,512]{1,0:T(8,128)S(1)}, f32[72,512]{1,0:T(8,128)S(1)}, u32[]{:S(2)}, u32[]{:S(2)}) collective-permute-start(f32[72,512]{1,0:T(8,128)S(1)} %get-tuple-element.33), channel_id=1, source_target_pairs={{0,4},{2,6},{4,0},{6,2},{8,12},{10,14},{12,8},{14,10},{1,5},{3,7},... | collective-permute-start | bytes 442376 | tf_op jit(solution)/shard_map/ppermute | solution.py:339
  26.9 9.5 %collective-permute-start.5 = (f32[72,512]{1,0:T(8,128)S(1)}, f32[72,512]{1,0:T(8,128)S(1)}, u32[]{:S(2)}, u32[]{:S(2)}) collective-permute-start(f32[72,512]{1,0:T(8,128)S(1)} %fusion.5), channel_id=1, source_target_pairs={{0,8},{2,10},{4,12},{6,14},{8,0},{10,2},{12,4},{14,6},{1,9},{3,11}... | collective-permute-start | bytes 442376 | tf_op jit(solution)/shard_map/ppermute | solution.py:339
  35.5 8.7 %collective-permute-start.11 = (f32[72,512]{1,0:T(8,128)S(1)}, f32[72,512]{1,0:T(8,128)S(1)}, u32[]{:S(2)}, u32[]{:S(2)}) collective-permute-start(f32[72,512]{1,0:T(8,128)S(1)} %fusion.2), channel_id=1, source_target_pairs={{0,8},{2,10},{4,12},{6,14},{8,0},{10,2},{12,4},{14,6},{1,9},{3,11}... | collective-permute-start | bytes 442376 | tf_op jit(solution)/shard_map/ppermute | solution.py:339
  36.5 13.4 %collective-permute-start.12 = (f32[64,512]{1,0:T(8,128)S(1)}, f32[64,512]{1,0:T(8,128)S(1)}, u32[]{:S(2)}, u32[]{:S(2)}) collective-permute-start(f32[64,512]{1,0:T(8,128)S(1)} %slice.67.refs_0_), channel_id=1, source_target_pairs={{0,2},{2,0},{4,6},{6,4},{8,10},{10,8},{12,14},{14,12},{1,3},{3,1},... | collective-permute-start | bytes 393224 | tf_op jit(solution)/shard_map/ppermute | solution.py:339
  36.7 7.6 %collective-permute-start.6 = (f32[8,512]{1,0:T(8,128)S(1)}, f32[8,512]{1,0:T(8,128)S(1)}, u32[]{:S(2)}, u32[]{:S(2)}) collective-permute-start(f32[8,512]{1,0:T(8,128)S(1)} %slice.62.own_ref), channel_id=1, source_target_pairs={{0,1},{1,0},{2,3},{3,2},{4,5},{5,4},{6,7},{7,6},{8,9},{9,8},{10,11... | collective-permute-start | bytes 49160 | tf_op jit(solution)/shard_map/ppermute | solution.py:374
  37.6 17.3 %collective-permute-start.13 = (f32[64,512]{1,0:T(8,128)S(1)}, f32[64,512]{1,0:T(8,128)S(1)}, u32[]{:S(2)}, u32[]{:S(2)}) collective-permute-start(f32[64,512]{1,0:T(8,128)S(1)} %slice.67.refs_0_), channel_id=1, source_target_pairs={{0,4},{2,6},{4,0},{6,2},{8,12},{10,14},{12,8},{14,10},{1,5},{3,7},... | collective-permute-start | bytes 393224 | tf_op jit(solution)/shard_map/ppermute | solution.py:339
  43.2 11.7 %collective-permute-start.14 = (f32[64,512]{1,0:T(8,128)S(1)}, f32[64,512]{1,0:T(8,128)S(1)}, u32[]{:S(2)}, u32[]{:S(2)}) collective-permute-start(f32[64,512]{1,0:T(8,128)S(1)} %slice.67.refs_0_), channel_id=1, source_target_pairs={{0,6},{2,4},{4,2},{6,0},{8,14},{10,12},{12,10},{14,8},{1,7},{3,5},... | collective-permute-start | bytes 393224 | tf_op jit(solution)/shard_map/ppermute | solution.py:339
  47.3 7.6 %collective-permute-start.15 = (f32[64,512]{1,0:T(8,128)S(1)}, f32[64,512]{1,0:T(8,128)S(1)}, u32[]{:S(2)}, u32[]{:S(2)}) collective-permute-start(f32[64,512]{1,0:T(8,128)S(1)} %slice.57.refs_4_), channel_id=1, source_target_pairs={{0,2},{2,0},{4,6},{6,4},{8,10},{10,8},{12,14},{14,12},{1,3},{3,1},... | collective-permute-start | bytes 393224 | tf_op jit(solution)/shard_map/ppermute | solution.py:339
  47.9 7.0 %collective-permute-start.16 = (f32[64,512]{1,0:T(8,128)S(1)}, f32[64,512]{1,0:T(8,128)S(1)}, u32[]{:S(2)}, u32[]{:S(2)}) collective-permute-start(f32[64,512]{1,0:T(8,128)S(1)} %slice.57.refs_4_), channel_id=1, source_target_pairs={{0,4},{2,6},{4,0},{6,2},{8,12},{10,14},{12,8},{14,10},{1,5},{3,7},... | collective-permute-start | bytes 393224 | tf_op jit(solution)/shard_map/ppermute | solution.py:339
  49.9 6.4 %collective-permute-start.17 = (f32[64,512]{1,0:T(8,128)S(1)}, f32[64,512]{1,0:T(8,128)S(1)}, u32[]{:S(2)}, u32[]{:S(2)}) collective-permute-start(f32[64,512]{1,0:T(8,128)S(1)} %slice.57.refs_4_), channel_id=1, source_target_pairs={{0,6},{2,4},{4,2},{6,0},{8,14},{10,12},{12,10},{14,8},{1,7},{3,5},... | collective-permute-start | bytes 393224 | tf_op jit(solution)/shard_map/ppermute | solution.py:339

commit v3 on v2

--- a/solution.py
+++ b/solution.py
@@ -26,9 +26,10 @@
 
 def prep_kernel(lead_ref, flipped_ref, mask_ref):
     edge = flipped_ref.shape[0]
-    mask = lead_ref[:, edge:]
-    flipped_ref[...] = (lead_ref[:, :edge] * mask[:, :, :1]).reshape(-1, edge).T
-    mask_ref[...] = mask.reshape(mask_ref.shape)
+    tile_count, blocks = mask_ref.shape
+    mask = lead_ref[tile_count, :tile_count, :blocks]
+    mask_ref[...] = mask
+    flipped_ref[...] = (lead_ref[:tile_count] * mask[:, :1].reshape(tile_count, 1, 1)).reshape(-1, edge).T
 
 
 def spread_mask(mask, columns, edge):
@@ -205,32 +206,18 @@
     return jnp.where(first, own, other), jnp.where(first, other, own)
 
 
-def first_factor_kernel(start, info_ref, own_ref, other_ref, out_ref):
-    edge = out_ref.shape[0]
-    gram, _ = both_grams(info_ref, own_ref, other_ref, start, edge)
+def factor_kernel(start, info_ref, own_ref, other_ref, pair_ref, out_ref):
+    edge = out_ref.shape[0] // 2
+    gram_00, gram_11 = both_grams(info_ref, own_ref, other_ref, start, edge)
+    cross = take_block(pair_ref, edge)
+    cross = jnp.where(info_ref[2] == 0, cross, cross.T)
+    upper = jnp.concatenate([gram_00, cross.T], axis=1)
+    lower = jnp.concatenate([cross, gram_11], axis=1)
 
     def put(index, row):
         out_ref[index : index + 1] = row
 
-    inverse_factor(gram, put)
-
-
-def rest_factor_kernel(start, info_ref, own_ref, other_ref, pair_ref, corner_ref, out_ref):
-    edge = corner_ref.shape[0]
-    _, gram = both_grams(info_ref, own_ref, other_ref, start, edge)
-    cross = take_block(pair_ref, edge)
-    cross = jnp.where(info_ref[2] == 0, cross, cross.T)
-    corner = corner_ref[...]
-    lower = dot_nt(cross, corner)
-    both = jnp.dot(lower, corner, precision=HIGHEST, preferred_element_type=F32)
-    out_ref[:edge, :edge] = corner
-    out_ref[:edge, edge:] = jnp.zeros_like(corner)
-
-    def put(index, row):
-        out_ref[edge + index : edge + index + 1, edge:] = row
-
-    inverse_factor(gram - dot_nt(lower, lower), put)
-    out_ref[edge:, :edge] = -jnp.dot(out_ref[edge:, edge:], both, precision=HIGHEST, preferred_element_type=F32)
+    inverse_factor(jnp.concatenate([upper, lower], axis=0), put)
 
 
 def final_kernel(pieces, edge, info_ref, inverse_ref, *refs):
@@ -289,15 +276,15 @@
     wide_params = pltpu.CompilerParams(vmem_limit_bytes=OWN_VMEM_LIMIT)
 
     blocks = columns // edge
-    mask_row = jnp.pad(block_mask.astype(F32), ((0, 0), (0, edge - blocks)))[:, None]
+    mask_tile = jnp.pad(block_mask.astype(F32), ((0, edge - tile_count), (0, edge - blocks)))[None]
     lead, mask = pl.pallas_call(
         prep_kernel,
-        out_shape=(jax.ShapeDtypeStruct((edge, rows), F32), jax.ShapeDtypeStruct((tile_count, edge), F32)),
+        out_shape=(jax.ShapeDtypeStruct((edge, rows), F32), jax.ShapeDtypeStruct((tile_count, blocks), F32)),
         in_specs=[vmem()],
         out_specs=(vmem(), vmem()),
         compiler_params=params,
         name="lead_prep",
-    )(jnp.concatenate([child_tiles[:, :, :edge], mask_row], axis=1))
+    )(jnp.concatenate([child_tiles[:, :, :edge], mask_tile], axis=0))
 
     if col_count == PANELS:
         lead_own = lead
@@ -338,10 +325,10 @@
     def over_row(value, bit):
         return lax.ppermute(value, "row", [(i, i ^ bit) for i in range(row_count)])
 
-    def reduce_near(partial):
+    def reduce_near(partial, order):
         total = partial[0]
-        for near in range(1, pieces):
-            total = total + over_row(partial[near], near)
+        for near in order:
+            total = lax.optimization_barrier(total + over_row(partial[near], near))
         return total
 
     def reduce_far(total):
@@ -353,7 +340,7 @@
         return [total[:edge]] + [over_row(total[:edge], near) for near in range(1, pieces)]
 
     send, lead_other = lax.optimization_barrier((send, lead_other))
-    own_sum = reduce_far(reduce_near(over_leaf(keep, send)))
+    own_sum = reduce_far(reduce_near(over_leaf(keep, send), range(1, pieces)))
     own_pieces = gather_pieces(own_sum)
 
     pair_rows = gram_rows if swap else 2 * gram_rows
@@ -367,34 +354,22 @@
         cost_estimate=work,
         name="panel_pair",
     )(info, mine, lead_other, lead_own, high, low)
-    other_sum = reduce_far(reduce_near(over_leaf(keep, send)))
-
-    own_gram = own_sum[edge:]
+    other_sum = reduce_far(reduce_near(over_leaf(keep, send), range(1, pieces)))
+
+    other_pieces = gather_pieces(other_sum)
+    own_gram, pair_gram = own_sum[edge:], other_sum[edge:]
     if swap:
         other_gram, start = lax.ppermute(own_gram, "col", [(i, 1 - i) for i in range(PANELS)]), 0
     else:
-        other_gram, start = other_sum[edge:], edge // 16
-    corner = pl.pallas_call(
-        functools.partial(first_factor_kernel, start),
-        out_shape=jax.ShapeDtypeStruct((edge, edge), F32),
-        in_specs=[smem(), vmem(), vmem()],
+        other_gram, start = pair_gram, edge // 16
+    inverse = pl.pallas_call(
+        functools.partial(factor_kernel, start),
+        out_shape=jax.ShapeDtypeStruct((2 * edge, 2 * edge), F32),
+        in_specs=[smem()] + [vmem()] * 3,
         out_specs=vmem(),
         compiler_params=params,
-        cost_estimate=pl.CostEstimate(flops=work.flops // 2, bytes_accessed=work.bytes_accessed // 2, transcendentals=0),
-        name="gram_factor_first",
-    )(info, own_gram, other_gram)
-    if swap:
-        other_sum, corner = lax.optimization_barrier((other_sum, corner))
-    other_pieces = gather_pieces(other_sum)
-    pair_gram = other_sum[edge:]
-    inverse = pl.pallas_call(
-        functools.partial(rest_factor_kernel, start),
-        out_shape=jax.ShapeDtypeStruct((2 * edge, 2 * edge), F32),
-        in_specs=[smem()] + [vmem()] * 4,
-        out_specs=vmem(),
-        compiler_params=params,
-        name="gram_factor_rest",
-    )(info, own_gram, other_gram, pair_gram, corner)
+        name="gram_factor",
+    )(info, own_gram, other_gram, pair_gram)
 
     return pl.pallas_call(
         functools.partial(final_kernel, pieces, edge),

time: 58.5 us -> 56.5 us (0.966)
  waiting for transfers between devices: 12 us -> 10.7 us
  starting transfers between devices: 24.9 us -> 24.3 us
    ppermute x14, waiting for transfers between devices: 12 us -> 10.7 us  [over_row(): return lax.ppermute(value, 'row', [(i, i ^ bit) for i in range(row_count)])]
    pallas_call x2 -> x1, Pallas kernels: 7.04 us -> 6.65 us  [per_device(): pl.pallas_call(functools.partial(factor_kernel, start), out_shape=jax.Sha...]
  transfers between devices with their start and end apart: 18 -> 18, of which waited for: 7 -> 4; matrix products, arithmetic and copies ran while one was open for 1% -> 1% of each run, Pallas kernels for 28% -> 28%
where the time goes in v3:
time: 56.5 us; the launch traced here: 56.3 us
  starting transfers between devices  24.3 us (43%)
  Pallas kernels  18.1 us (32%)
  waiting for transfers between devices  10.7 us (19%)
  local copies, waits for them, and re-layouts  1.83 us (3%)
  other arithmetic  1.18 us (2%)
    ppermute x14, starting transfers between devices, over_row(): return lax.ppermute(value, 'row', [(i, i ^ bit) for i in range(row_count)])  20 us
    ppermute x14, waiting for transfers between devices, over_row(): return lax.ppermute(value, 'row', [(i, i ^ bit) for i in range(row_count)])  10.7 us
    pallas_call x1, Pallas kernels, per_device(): pl.pallas_call(functools.partial(factor_kernel, start), out_shape=jax.Sha...  6.65 us
    pallas_call x1, Pallas kernels, per_device(): pl.pallas_call(functools.partial(own_kernel, row_count), out_shape=(sums(...  6.54 us
    ppermute x1, starting transfers between devices, per_device(): lead_other = lax.ppermute(lead, 'col', [(i, 1 - i) for i in range(PANELS)])  3.03 us
    pallas_call x1, Pallas kernels, per_device(): pl.pallas_call(functools.partial(pair_kernel, not swap), out_shape=(sums(...  2.73 us
    pallas_call x1, Pallas kernels, per_device(): pl.pallas_call(functools.partial(final_kernel, pieces, edge), out_shape=j...  1.93 us
  transfers between devices with their start and end apart: 18, of which 4 were waited for; matrix products, arithmetic and copies ran while one was open for 1% of the time, Pallas kernels for 28%

profile of v3, /device:TPU:0, one launch (start us, length us, event | category | flops | bytes accessed | tf_op | source)
XLA Modules:
  0.0 56.3 jit_solution(11396277455729217181)
XLA Ops:
  0.0 0.7 %convert_element_type.5 = f32[16,32]{1,0:T(8,128)S(1)} convert(s32[16,32]{1,0:T(8,128)} %param.4) | non-fusion elementwise | flops 512 | bytes 4096 | tf_op jit(solution)/shard_map/convert_element_type | solution.py:279
  0.7 1.1 %slice.45 = f32[16,64,64]{2,1,0:T(8,128)S(1)} slice(f32[16,64,2048]{2,1,0:T(8,128)} %tiles_ref.1), slice={[0:16], [0:64], [0:64]} | slice | bytes 524288 | tf_op jit(solution)/shard_map/slice | solution.py:287
  1.8 0.3 lead_prep.1
  2.1 3.0 %collective-permute-start = (f32[64,1024]{1,0:T(8,128)S(1)}, f32[64,1024]{1,0:T(8,128)S(1)}, u32[]{:S(2)}, u32[]{:S(2)}) collective-permute-start(f32[64,1024]{1,0:T(8,128)S(1)} %get-tuple-element.17.lead_ref.own_ref), channel_id=1, source_target_pairs={{0,1},{1,0},{2,3},{3,2},{4,5},{5,4},{6,7},{7,6},{8,9},{9,8},{10,11... | collective-permute-start | bytes 786440 | tf_op jit(solution)/shard_map/ppermute | solution.py:291
  5.1 0.1 pad_add_fusion.info_ref
  5.2 0.0 copy-start
  5.2 0.7 %copy-done = s32[16,1]{0,1:T(1,128)S(1)} copy-done((s32[16,1]{0,1:T(1,128)S(1)}, s32[16,1]{0,1:T(1,128)}, u32[]{:S(2)}) %copy-start) | copy-done | bytes 88
  5.9 6.5 %panel_own.1 = (f32[4,72,512]{2,1,0:T(8,128)S(1)}, f32[4,72,512]{2,1,0:T(8,128)S(1)}, bf16[1024,2048]{1,0:T(8,128)(2,1)S(1)}, bf16[1024,2048]{1,0:T(8,128)(2,1)S(1)}, f32[1,1024]{1,0:T(1,128)S(1)}) custom-call(s32[4]{0:T(128)S(1)} %pad_add_fusion.info_ref, s32[1,16]{1,0:T(1,128)S(1)} %bitcast.26, f32[16,32]{1,0:T(8,128)S(1)} %get-tuple-element.16.mask_ref, ...), custom_call_target="tpu_custom_call" | custom-call | flops 1610612736 | bytes 8388608 | tf_op jit(solution)/shard_map/panel_own/pallas_call | solution.py:305
  12.4 0.0 collective-permute-done.lead_ref
  12.4 0.1 collective-permute-start.1
  12.5 2.7 %panel_pair.1 = (f32[4,72,512]{2,1,0:T(8,128)S(1)}, f32[4,72,512]{2,1,0:T(8,128)S(1)}) custom-call(s32[4]{0:T(128)S(1)} %pad_add_fusion.info_ref, f32[1,1024]{1,0:T(1,128)S(1)} %get-tuple-element.21.mine_ref, f32[64,1024]{1,0:T(8,128)S(1)} %collective-permute-done.lead_ref, f32[64,1024]{1,0:T(8,128)S(1)} %get-tuple-element.17.lead_ref.own_ref, ...), custom_call_target="tpu_custom_call" | custom-call | flops 1610612736 | bytes 8388608 | tf_op jit(solution)/shard_map/panel_pair/pallas_call | solution.py:347
  15.2 0.6 collective-permute-start.7
  15.8 0.0 collective-permute-done.1
  15.8 0.1 add.37
  15.9 1.6 %collective-permute-start.2 = (f32[72,512]{1,0:T(8,128)S(1)}, f32[72,512]{1,0:T(8,128)S(1)}, u32[]{:S(2)}, u32[]{:S(2)}) collective-permute-start(f32[72,512]{1,0:T(8,128)S(1)} %get-tuple-element.32), channel_id=1, source_target_pairs={{0,2},{2,0},{4,6},{6,4},{8,10},{10,8},{12,14},{14,12},{1,3},{3,1},... | collective-permute-start | bytes 442376 | tf_op jit(solution)/shard_map/ppermute | solution.py:326
  17.5 1.6 %collective-permute-start.3 = (f32[72,512]{1,0:T(8,128)S(1)}, f32[72,512]{1,0:T(8,128)S(1)}, u32[]{:S(2)}, u32[]{:S(2)}) collective-permute-start(f32[72,512]{1,0:T(8,128)S(1)} %get-tuple-element.31), channel_id=1, source_target_pairs={{0,4},{2,6},{4,0},{6,2},{8,12},{10,14},{12,8},{14,10},{1,5},{3,7},... | collective-permute-start | bytes 442376 | tf_op jit(solution)/shard_map/ppermute | solution.py:326
  19.1 0.4 collective-permute-start.4
  19.5 0.0 collective-permute-done.7
  19.5 0.1 add.42
  19.6 1.6 %collective-permute-start.8 = (f32[72,512]{1,0:T(8,128)S(1)}, f32[72,512]{1,0:T(8,128)S(1)}, u32[]{:S(2)}, u32[]{:S(2)}) collective-permute-start(f32[72,512]{1,0:T(8,128)S(1)} %get-tuple-element.29), channel_id=1, source_target_pairs={{0,2},{2,0},{4,6},{6,4},{8,10},{10,8},{12,14},{14,12},{1,3},{3,1},... | collective-permute-start | bytes 442376 | tf_op jit(solution)/shard_map/ppermute | solution.py:326
  21.2 1.6 %collective-permute-start.9 = (f32[72,512]{1,0:T(8,128)S(1)}, f32[72,512]{1,0:T(8,128)S(1)}, u32[]{:S(2)}, u32[]{:S(2)}) collective-permute-start(f32[72,512]{1,0:T(8,128)S(1)} %get-tuple-element.28), channel_id=1, source_target_pairs={{0,4},{2,6},{4,0},{6,2},{8,12},{10,14},{12,8},{14,10},{1,5},{3,7},... | collective-permute-start | bytes 442376 | tf_op jit(solution)/shard_map/ppermute | solution.py:326
  22.8 0.0 collective-permute-done.2
  22.8 2.1 %collective-permute-start.10 = (f32[72,512]{1,0:T(8,128)S(1)}, f32[72,512]{1,0:T(8,128)S(1)}, u32[]{:S(2)}, u32[]{:S(2)}) collective-permute-start(f32[72,512]{1,0:T(8,128)S(1)} %get-tuple-element.27), channel_id=1, source_target_pairs={{0,6},{2,4},{4,2},{6,0},{8,14},{10,12},{12,10},{14,8},{1,7},{3,5},... | collective-permute-start | bytes 442376 | tf_op jit(solution)/shard_map/ppermute | solution.py:326
  24.8 0.0 collective-permute-done.3
  24.9 2.2 %collective-permute-done.4 = f32[72,512]{1,0:T(8,128)S(1)} collective-permute-done((f32[72,512]{1,0:T(8,128)S(1)}, f32[72,512]{1,0:T(8,128)S(1)}, u32[]{:S(2)}, u32[]{:S(2)}) %collective-permute-start.4) | collective-permute-done | bytes 147488 | tf_op jit(solution)/shard_map/ppermute | solution.py:326
  27.1 2.7 %collective-permute-start.5 = (f32[72,512]{1,0:T(8,128)S(1)}, f32[72,512]{1,0:T(8,128)S(1)}, u32[]{:S(2)}, u32[]{:S(2)}) collective-permute-start(f32[72,512]{1,0:T(8,128)S(1)} %add.40), channel_id=1, source_target_pairs={{0,8},{2,10},{4,12},{6,14},{8,0},{10,2},{12,4},{14,6},{1,9},{3,11}... | collective-permute-start | bytes 442376 | tf_op jit(solution)/shard_map/ppermute | solution.py:326
  29.8 0.0 collective-permute-done.8
  29.8 3.9 %collective-permute-done.9 = f32[72,512]{1,0:T(8,128)S(1)} collective-permute-done((f32[72,512]{1,0:T(8,128)S(1)}, f32[72,512]{1,0:T(8,128)S(1)}, u32[]{:S(2)}, u32[]{:S(2)}) %collective-permute-start.9) | collective-permute-done | bytes 147488 | tf_op jit(solution)/shard_map/ppermute | solution.py:326
  33.7 1.9 %collective-permute-done.10 = f32[72,512]{1,0:T(8,128)S(1)} collective-permute-done((f32[72,512]{1,0:T(8,128)S(1)}, f32[72,512]{1,0:T(8,128)S(1)}, u32[]{:S(2)}, u32[]{:S(2)}) %collective-permute-start.10) | collective-permute-done | bytes 147488 | tf_op jit(solution)/shard_map/ppermute | solution.py:326
  35.7 1.0 %collective-permute-start.11 = (f32[72,512]{1,0:T(8,128)S(1)}, f32[72,512]{1,0:T(8,128)S(1)}, u32[]{:S(2)}, u32[]{:S(2)}) collective-permute-start(f32[72,512]{1,0:T(8,128)S(1)} %add.45), channel_id=1, source_target_pairs={{0,8},{2,10},{4,12},{6,14},{8,0},{10,2},{12,4},{14,6},{1,9},{3,11}... | collective-permute-start | bytes 442376 | tf_op jit(solution)/shard_map/ppermute | solution.py:326
  36.7 0.0 collective-permute-done.5
  36.8 1.2 %collective-permute-start.12 = (f32[64,512]{1,0:T(8,128)S(1)}, f32[64,512]{1,0:T(8,128)S(1)}, u32[]{:S(2)}, u32[]{:S(2)}) collective-permute-start(f32[64,512]{1,0:T(8,128)S(1)} %slice.68.refs_0_), channel_id=1, source_target_pairs={{0,2},{2,0},{4,6},{6,4},{8,10},{10,8},{12,14},{14,12},{1,3},{3,1},... | collective-permute-start | bytes 393224 | tf_op jit(solution)/shard_map/ppermute | solution.py:326
  38.0 0.7 %collective-permute-start.6 = (f32[8,512]{1,0:T(8,128)S(1)}, f32[8,512]{1,0:T(8,128)S(1)}, u32[]{:S(2)}, u32[]{:S(2)}) collective-permute-start(f32[8,512]{1,0:T(8,128)S(1)} %slice.62.own_ref), channel_id=1, source_target_pairs={{0,1},{1,0},{2,3},{3,2},{4,5},{5,4},{6,7},{7,6},{8,9},{9,8},{10,11... | collective-permute-start | bytes 49160 | tf_op jit(solution)/shard_map/ppermute | solution.py:362
  38.7 2.8 %collective-permute-start.13 = (f32[64,512]{1,0:T(8,128)S(1)}, f32[64,512]{1,0:T(8,128)S(1)}, u32[]{:S(2)}, u32[]{:S(2)}) collective-permute-start(f32[64,512]{1,0:T(8,128)S(1)} %slice.68.refs_0_), channel_id=1, source_target_pairs={{0,4},{2,6},{4,0},{6,2},{8,12},{10,14},{12,8},{14,10},{1,5},{3,7},... | collective-permute-start | bytes 393224 | tf_op jit(solution)/shard_map/ppermute | solution.py:326
  41.5 0.0 collective-permute-start.14
  41.5 2.6 %collective-permute-done.11 = f32[72,512]{1,0:T(8,128)S(1)} collective-permute-done((f32[72,512]{1,0:T(8,128)S(1)}, f32[72,512]{1,0:T(8,128)S(1)}, u32[]{:S(2)}, u32[]{:S(2)}) %collective-permute-start.11) | collective-permute-done | bytes 147488 | tf_op jit(solution)/shard_map/ppermute | solution.py:326
  44.1 1.8 %collective-permute-start.15 = (f32[64,512]{1,0:T(8,128)S(1)}, f32[64,512]{1,0:T(8,128)S(1)}, u32[]{:S(2)}, u32[]{:S(2)}) collective-permute-start(f32[64,512]{1,0:T(8,128)S(1)} %slice.69.refs_4_), channel_id=1, source_target_pairs={{0,2},{2,0},{4,6},{6,4},{8,10},{10,8},{12,14},{14,12},{1,3},{3,1},... | collective-permute-start | bytes 393224 | tf_op jit(solution)/shard_map/ppermute | solution.py:326
  46.0 0.0 collective-permute-done.6.other_ref
  46.0 0.0 collective-permute-start.16
  46.0 0.0 collective-permute-done.12.refs_1_
  46.0 1.7 %collective-permute-start.17 = (f32[64,512]{1,0:T(8,128)S(1)}, f32[64,512]{1,0:T(8,128)S(1)}, u32[]{:S(2)}, u32[]{:S(2)}) collective-permute-start(f32[64,512]{1,0:T(8,128)S(1)} %slice.69.refs_4_), channel_id=1, source_target_pairs={{0,6},{2,4},{4,2},{6,0},{8,14},{10,12},{12,10},{14,8},{1,7},{3,5},... | collective-permute-start | bytes 393224 | tf_op jit(solution)/shard_map/ppermute | solution.py:326
  47.7 6.6 %gram_factor.1.inverse_ref = f32[128,128]{1,0:T(8,128)S(1)} custom-call(s32[4]{0:T(128)S(1)} %pad_add_fusion.info_ref, f32[8,512]{1,0:T(8,128)S(1)} %slice.62.own_ref, f32[8,512]{1,0:T(8,128)S(1)} %collective-permute-done.6.other_ref, f32[8,512]{1,0:T(8,128)S(1)} %slice.67.pair_ref), custom_call_target="tpu_custom_call" | custom-call | tf_op jit(solution)/shard_map/gram_factor/pallas_call | solution.py:365
  54.3 0.0 collective-permute-done.13.refs_2_
  54.4 0.0 collective-permute-done.14.refs_3_
  54.4 0.0 collective-permute-done.15.refs_5_
  54.4 0.0 collective-permute-done.16.refs_6_
  54.4 0.0 collective-permute-done.17.refs_7_
  54.4 1.9 %apply_inverse.1 = f32[1,128,2048]{2,1,0:T(8,128)} custom-call(s32[4]{0:T(128)S(1)} %pad_add_fusion.info_ref, f32[128,128]{1,0:T(8,128)S(1)} %gram_factor.1.inverse_ref, f32[64,512]{1,0:T(8,128)S(1)} %slice.68.refs_0_, f32[64,512]{1,0:T(8,128)S(1)} %collective-permute-done.12.refs_1_, f32[64,512]{1,0:T(8,128)S(1)} %collective-permute-done.13.refs_2_, ...), custom_call_target="tpu_custom_call" | custom-call | tf_op jit(solution)/shard_map/apply_inverse/pallas_call | solution.py:374
  (16 shorter events, 0.3 us)
Async XLA Ops:
  2.1 10.3 %collective-permute-start = (f32[64,1024]{1,0:T(8,128)S(1)}, f32[64,1024]{1,0:T(8,128)S(1)}, u32[]{:S(2)}, u32[]{:S(2)}) collective-permute-start(f32[64,1024]{1,0:T(8,128)S(1)} %get-tuple-element.17.lead_ref.own_ref), channel_id=1, source_target_pairs={{0,1},{1,0},{2,3},{3,2},{4,5},{5,4},{6,7},{7,6},{8,9},{9,8},{10,11... | collective-permute-start | bytes 786440 | tf_op jit(solution)/shard_map/ppermute | solution.py:291
  5.2 0.7 %copy-start = (s32[16,1]{0,1:T(1,128)S(1)}, s32[16,1]{0,1:T(1,128)}, u32[]{:S(2)}) copy-start(s32[16,1]{0,1:T(1,128)} %param.5) | copy-start | bytes 196
  12.4 3.4 %collective-permute-start.1 = (f32[4,72,512]{2,1,0:T(8,128)S(1)}, f32[4,72,512]{2,1,0:T(8,128)S(1)}, u32[]{:S(2)}, u32[]{:S(2)}) collective-permute-start(f32[4,72,512]{2,1,0:T(8,128)S(1)} %get-tuple-element.20), channel_id=1, source_target_pairs={{0,16},{16,0},{1,17},{17,1},{2,18},{18,2},{3,19},{19,3},{4,20},{20... | collective-permute-start | bytes 1769480 | tf_op jit(solution)/shard_map/ppermute | solution.py:323
  15.2 4.3 %collective-permute-start.7 = (f32[4,72,512]{2,1,0:T(8,128)S(1)}, f32[4,72,512]{2,1,0:T(8,128)S(1)}, u32[]{:S(2)}, u32[]{:S(2)}) collective-permute-start(f32[4,72,512]{2,1,0:T(8,128)S(1)} %get-tuple-element.26), channel_id=1, source_target_pairs={{0,16},{16,0},{1,17},{17,1},{2,18},{18,2},{3,19},{19,3},{4,20},{20... | collective-permute-start | bytes 1769480 | tf_op jit(solution)/shard_map/ppermute | solution.py:323
  15.9 6.8 %collective-permute-start.2 = (f32[72,512]{1,0:T(8,128)S(1)}, f32[72,512]{1,0:T(8,128)S(1)}, u32[]{:S(2)}, u32[]{:S(2)}) collective-permute-start(f32[72,512]{1,0:T(8,128)S(1)} %get-tuple-element.32), channel_id=1, source_target_pairs={{0,2},{2,0},{4,6},{6,4},{8,10},{10,8},{12,14},{14,12},{1,3},{3,1},... | collective-permute-start | bytes 442376 | tf_op jit(solution)/shard_map/ppermute | solution.py:326
  17.5 7.4 %collective-permute-start.3 = (f32[72,512]{1,0:T(8,128)S(1)}, f32[72,512]{1,0:T(8,128)S(1)}, u32[]{:S(2)}, u32[]{:S(2)}) collective-permute-start(f32[72,512]{1,0:T(8,128)S(1)} %get-tuple-element.31), channel_id=1, source_target_pairs={{0,4},{2,6},{4,0},{6,2},{8,12},{10,14},{12,8},{14,10},{1,5},{3,7},... | collective-permute-start | bytes 442376 | tf_op jit(solution)/shard_map/ppermute | solution.py:326
  19.1 8.0 %collective-permute-start.4 = (f32[72,512]{1,0:T(8,128)S(1)}, f32[72,512]{1,0:T(8,128)S(1)}, u32[]{:S(2)}, u32[]{:S(2)}) collective-permute-start(f32[72,512]{1,0:T(8,128)S(1)} %get-tuple-element.30), channel_id=1, source_target_pairs={{0,6},{2,4},{4,2},{6,0},{8,14},{10,12},{12,10},{14,8},{1,7},{3,5},... | collective-permute-start | bytes 442376 | tf_op jit(solution)/shard_map/ppermute | solution.py:326
  19.6 10.2 %collective-permute-start.8 = (f32[72,512]{1,0:T(8,128)S(1)}, f32[72,512]{1,0:T(8,128)S(1)}, u32[]{:S(2)}, u32[]{:S(2)}) collective-permute-start(f32[72,512]{1,0:T(8,128)S(1)} %get-tuple-element.29), channel_id=1, source_target_pairs={{0,2},{2,0},{4,6},{6,4},{8,10},{10,8},{12,14},{14,12},{1,3},{3,1},... | collective-permute-start | bytes 442376 | tf_op jit(solution)/shard_map/ppermute | solution.py:326
  21.2 12.5 %collective-permute-start.9 = (f32[72,512]{1,0:T(8,128)S(1)}, f32[72,512]{1,0:T(8,128)S(1)}, u32[]{:S(2)}, u32[]{:S(2)}) collective-permute-start(f32[72,512]{1,0:T(8,128)S(1)} %get-tuple-element.28), channel_id=1, source_target_pairs={{0,4},{2,6},{4,0},{6,2},{8,12},{10,14},{12,8},{14,10},{1,5},{3,7},... | collective-permute-start | bytes 442376 | tf_op jit(solution)/shard_map/ppermute | solution.py:326
  22.8 12.9 %collective-permute-start.10 = (f32[72,512]{1,0:T(8,128)S(1)}, f32[72,512]{1,0:T(8,128)S(1)}, u32[]{:S(2)}, u32[]{:S(2)}) collective-permute-start(f32[72,512]{1,0:T(8,128)S(1)} %get-tuple-element.27), channel_id=1, source_target_pairs={{0,6},{2,4},{4,2},{6,0},{8,14},{10,12},{12,10},{14,8},{1,7},{3,5},... | collective-permute-start | bytes 442376 | tf_op jit(solution)/shard_map/ppermute | solution.py:326
  27.1 9.6 %collective-permute-start.5 = (f32[72,512]{1,0:T(8,128)S(1)}, f32[72,512]{1,0:T(8,128)S(1)}, u32[]{:S(2)}, u32[]{:S(2)}) collective-permute-start(f32[72,512]{1,0:T(8,128)S(1)} %add.40), channel_id=1, source_target_pairs={{0,8},{2,10},{4,12},{6,14},{8,0},{10,2},{12,4},{14,6},{1,9},{3,11}... | collective-permute-start | bytes 442376 | tf_op jit(solution)/shard_map/ppermute | solution.py:326
  35.7 8.4 %collective-permute-start.11 = (f32[72,512]{1,0:T(8,128)S(1)}, f32[72,512]{1,0:T(8,128)S(1)}, u32[]{:S(2)}, u32[]{:S(2)}) collective-permute-start(f32[72,512]{1,0:T(8,128)S(1)} %add.45), channel_id=1, source_target_pairs={{0,8},{2,10},{4,12},{6,14},{8,0},{10,2},{12,4},{14,6},{1,9},{3,11}... | collective-permute-start | bytes 442376 | tf_op jit(solution)/shard_map/ppermute | solution.py:326
  36.8 9.2 %collective-permute-start.12 = (f32[64,512]{1,0:T(8,128)S(1)}, f32[64,512]{1,0:T(8,128)S(1)}, u32[]{:S(2)}, u32[]{:S(2)}) collective-permute-start(f32[64,512]{1,0:T(8,128)S(1)} %slice.68.refs_0_), channel_id=1, source_target_pairs={{0,2},{2,0},{4,6},{6,4},{8,10},{10,8},{12,14},{14,12},{1,3},{3,1},... | collective-permute-start | bytes 393224 | tf_op jit(solution)/shard_map/ppermute | solution.py:326
  38.0 8.0 %collective-permute-start.6 = (f32[8,512]{1,0:T(8,128)S(1)}, f32[8,512]{1,0:T(8,128)S(1)}, u32[]{:S(2)}, u32[]{:S(2)}) collective-permute-start(f32[8,512]{1,0:T(8,128)S(1)} %slice.62.own_ref), channel_id=1, source_target_pairs={{0,1},{1,0},{2,3},{3,2},{4,5},{5,4},{6,7},{7,6},{8,9},{9,8},{10,11... | collective-permute-start | bytes 49160 | tf_op jit(solution)/shard_map/ppermute | solution.py:362
  38.7 15.7 %collective-permute-start.13 = (f32[64,512]{1,0:T(8,128)S(1)}, f32[64,512]{1,0:T(8,128)S(1)}, u32[]{:S(2)}, u32[]{:S(2)}) collective-permute-start(f32[64,512]{1,0:T(8,128)S(1)} %slice.68.refs_0_), channel_id=1, source_target_pairs={{0,4},{2,6},{4,0},{6,2},{8,12},{10,14},{12,8},{14,10},{1,5},{3,7},... | collective-permute-start | bytes 393224 | tf_op jit(solution)/shard_map/ppermute | solution.py:326
  41.5 12.9 %collective-permute-start.14 = (f32[64,512]{1,0:T(8,128)S(1)}, f32[64,512]{1,0:T(8,128)S(1)}, u32[]{:S(2)}, u32[]{:S(2)}) collective-permute-start(f32[64,512]{1,0:T(8,128)S(1)} %slice.68.refs_0_), channel_id=1, source_target_pairs={{0,6},{2,4},{4,2},{6,0},{8,14},{10,12},{12,10},{14,8},{1,7},{3,5},... | collective-permute-start | bytes 393224 | tf_op jit(solution)/shard_map/ppermute | solution.py:326
  44.1 10.2 %collective-permute-start.15 = (f32[64,512]{1,0:T(8,128)S(1)}, f32[64,512]{1,0:T(8,128)S(1)}, u32[]{:S(2)}, u32[]{:S(2)}) collective-permute-start(f32[64,512]{1,0:T(8,128)S(1)} %slice.69.refs_4_), channel_id=1, source_target_pairs={{0,2},{2,0},{4,6},{6,4},{8,10},{10,8},{12,14},{14,12},{1,3},{3,1},... | collective-permute-start | bytes 393224 | tf_op jit(solution)/shard_map/ppermute | solution.py:326
  46.0 8.4 %collective-permute-start.16 = (f32[64,512]{1,0:T(8,128)S(1)}, f32[64,512]{1,0:T(8,128)S(1)}, u32[]{:S(2)}, u32[]{:S(2)}) collective-permute-start(f32[64,512]{1,0:T(8,128)S(1)} %slice.69.refs_4_), channel_id=1, source_target_pairs={{0,4},{2,6},{4,0},{6,2},{8,12},{10,14},{12,8},{14,10},{1,5},{3,7},... | collective-permute-start | bytes 393224 | tf_op jit(solution)/shard_map/ppermute | solution.py:326
  46.0 8.4 %collective-permute-start.17 = (f32[64,512]{1,0:T(8,128)S(1)}, f32[64,512]{1,0:T(8,128)S(1)}, u32[]{:S(2)}, u32[]{:S(2)}) collective-permute-start(f32[64,512]{1,0:T(8,128)S(1)} %slice.69.refs_4_), channel_id=1, source_target_pairs={{0,6},{2,4},{4,2},{6,0},{8,14},{10,12},{12,10},{14,8},{1,7},{3,5},... | collective-permute-start | bytes 393224 | tf_op jit(solution)/shard_map/ppermute | solution.py:326

commit v4 on v3

--- a/solution.py
+++ b/solution.py
@@ -172,7 +172,7 @@
                 ratio[i][j] = entry[i][j] * inverse[j]
             for i in range(j + 1, STEP):
                 for m in range(j + 1, i + 1):
-                    entry[i][m] = entry[i][m] - ratio[i][j] * entry[m][j]
+                    entry[i][m] = entry[i][m] - entry[i][j] * entry[m][j] * inverse[j]
         solved = []
         for j in span:
             unit = jnp.where(lane < k, pivot[j], jnp.where(lane == k + j, 1.0, 0.0))
@@ -188,16 +188,13 @@
                 front[j] = front[j] - ratio[j][i] * front[i]
         back = [front[j] * inverse[j] for j in span]
         for j in reversed(span):
-            for i in range(j + 1, STEP):
+            for i in reversed(range(j + 1, STEP)):
                 back[j] = back[j] - ratio[i][j] * back[i]
         for g in range((k + STEP) // 8, groups):
-            change = None
-            for j in span:
-                term = jnp.broadcast_to(rows[g][:, k + j : k + j + 1], (8, size)) * back[j]
-                change = term if change is None else change + term
-            if g == group:
-                change = jnp.where(down < inside + STEP, 0.0, change)
-            rows[g] = rows[g] - change
+            row = rows[g]
+            for j in reversed(span):
+                row = row - jnp.broadcast_to(rows[g][:, k + j : k + j + 1], (8, size)) * back[j]
+            rows[g] = jnp.where(down < inside + STEP, rows[g], row) if g == group else row
 
 
 def both_grams(info_ref, own_ref, other_ref, other_start, edge):

time: 56.5 us -> 56.4 us (level)
  Pallas kernels: 18.1 us -> 16.6 us
  waiting for transfers between devices: 10.7 us -> 12.1 us
    pallas_call x1, Pallas kernels: 6.65 us -> 5.12 us  [per_device(): pl.pallas_call(functools.partial(factor_kernel, start), out_shape=jax.Sha...]
    ppermute x14, waiting for transfers between devices: 10.7 us -> 12 us  [over_row(): return lax.ppermute(value, 'row', [(i, i ^ bit) for i in range(row_count)])]
  transfers between devices with their start and end apart: 18 -> 18, of which waited for: 4 -> 5; matrix products, arithmetic and copies ran while one was open for 1% -> 1% of each run, Pallas kernels for 28% -> 26%
where the time goes in v4:
time: 56.4 us; the launch traced here: 56.2 us
  starting transfers between devices  24.3 us (43%)
  Pallas kernels  16.6 us (29%)
  waiting for transfers between devices  12.1 us (21%)
  local copies, waits for them, and re-layouts  1.83 us (3%)
  other arithmetic  1.18 us (2%)
    ppermute x14, starting transfers between devices, over_row(): return lax.ppermute(value, 'row', [(i, i ^ bit) for i in range(row_count)])  20 us
    ppermute x14, waiting for transfers between devices, over_row(): return lax.ppermute(value, 'row', [(i, i ^ bit) for i in range(row_count)])  12 us
    pallas_call x1, Pallas kernels, per_device(): pl.pallas_call(functools.partial(own_kernel, row_count), out_shape=(sums(...  6.54 us
    pallas_call x1, Pallas kernels, per_device(): pl.pallas_call(functools.partial(factor_kernel, start), out_shape=jax.Sha...  5.12 us
    ppermute x1, starting transfers between devices, per_device(): lead_other = lax.ppermute(lead, 'col', [(i, 1 - i) for i in range(PANELS)])  3.03 us
    pallas_call x1, Pallas kernels, per_device(): pl.pallas_call(functools.partial(pair_kernel, not swap), out_shape=(sums(...  2.73 us
    pallas_call x1, Pallas kernels, per_device(): pl.pallas_call(functools.partial(final_kernel, pieces, edge), out_shape=j...  1.93 us
  transfers between devices with their start and end apart: 18, of which 5 were waited for; matrix products, arithmetic and copies ran while one was open for 1% of the time, Pallas kernels for 26%

profile of v4, /device:TPU:0, one launch (start us, length us, event | category | flops | bytes accessed | tf_op | source)
XLA Modules:
  0.0 56.2 jit_solution(16611637192155906216)
XLA Ops:
  0.0 0.7 %convert_element_type.5 = f32[16,32]{1,0:T(8,128)S(1)} convert(s32[16,32]{1,0:T(8,128)} %param.4) | non-fusion elementwise | flops 512 | bytes 4096 | tf_op jit(solution)/shard_map/convert_element_type | solution.py:276
  0.7 1.1 %slice.45 = f32[16,64,64]{2,1,0:T(8,128)S(1)} slice(f32[16,64,2048]{2,1,0:T(8,128)} %tiles_ref.1), slice={[0:16], [0:64], [0:64]} | slice | bytes 524288 | tf_op jit(solution)/shard_map/slice | solution.py:284
  1.8 0.3 lead_prep.1
  2.1 3.0 %collective-permute-start = (f32[64,1024]{1,0:T(8,128)S(1)}, f32[64,1024]{1,0:T(8,128)S(1)}, u32[]{:S(2)}, u32[]{:S(2)}) collective-permute-start(f32[64,1024]{1,0:T(8,128)S(1)} %get-tuple-element.17.lead_ref.own_ref), channel_id=1, source_target_pairs={{0,1},{1,0},{2,3},{3,2},{4,5},{5,4},{6,7},{7,6},{8,9},{9,8},{10,11... | collective-permute-start | bytes 786440 | tf_op jit(solution)/shard_map/ppermute | solution.py:288
  5.1 0.1 pad_add_fusion.info_ref
  5.2 0.0 copy-start
  5.2 0.7 %copy-done = s32[16,1]{0,1:T(1,128)S(1)} copy-done((s32[16,1]{0,1:T(1,128)S(1)}, s32[16,1]{0,1:T(1,128)}, u32[]{:S(2)}) %copy-start) | copy-done | bytes 88
  5.9 6.5 %panel_own.1 = (f32[4,72,512]{2,1,0:T(8,128)S(1)}, f32[4,72,512]{2,1,0:T(8,128)S(1)}, bf16[1024,2048]{1,0:T(8,128)(2,1)S(1)}, bf16[1024,2048]{1,0:T(8,128)(2,1)S(1)}, f32[1,1024]{1,0:T(1,128)S(1)}) custom-call(s32[4]{0:T(128)S(1)} %pad_add_fusion.info_ref, s32[1,16]{1,0:T(1,128)S(1)} %bitcast.26, f32[16,32]{1,0:T(8,128)S(1)} %get-tuple-element.16.mask_ref, ...), custom_call_target="tpu_custom_call" | custom-call | flops 1610612736 | bytes 8388608 | tf_op jit(solution)/shard_map/panel_own/pallas_call | solution.py:302
  12.4 0.0 collective-permute-done.lead_ref
  12.4 0.1 collective-permute-start.1
  12.5 2.7 %panel_pair.1 = (f32[4,72,512]{2,1,0:T(8,128)S(1)}, f32[4,72,512]{2,1,0:T(8,128)S(1)}) custom-call(s32[4]{0:T(128)S(1)} %pad_add_fusion.info_ref, f32[1,1024]{1,0:T(1,128)S(1)} %get-tuple-element.21.mine_ref, f32[64,1024]{1,0:T(8,128)S(1)} %collective-permute-done.lead_ref, f32[64,1024]{1,0:T(8,128)S(1)} %get-tuple-element.17.lead_ref.own_ref, ...), custom_call_target="tpu_custom_call" | custom-call | flops 1610612736 | bytes 8388608 | tf_op jit(solution)/shard_map/panel_pair/pallas_call | solution.py:344
  15.2 0.6 collective-permute-start.7
  15.8 0.0 collective-permute-done.1
  15.8 0.1 add.37
  15.9 1.6 %collective-permute-start.2 = (f32[72,512]{1,0:T(8,128)S(1)}, f32[72,512]{1,0:T(8,128)S(1)}, u32[]{:S(2)}, u32[]{:S(2)}) collective-permute-start(f32[72,512]{1,0:T(8,128)S(1)} %get-tuple-element.32), channel_id=1, source_target_pairs={{0,2},{2,0},{4,6},{6,4},{8,10},{10,8},{12,14},{14,12},{1,3},{3,1},... | collective-permute-start | bytes 442376 | tf_op jit(solution)/shard_map/ppermute | solution.py:323
  17.5 1.6 %collective-permute-start.3 = (f32[72,512]{1,0:T(8,128)S(1)}, f32[72,512]{1,0:T(8,128)S(1)}, u32[]{:S(2)}, u32[]{:S(2)}) collective-permute-start(f32[72,512]{1,0:T(8,128)S(1)} %get-tuple-element.31), channel_id=1, source_target_pairs={{0,4},{2,6},{4,0},{6,2},{8,12},{10,14},{12,8},{14,10},{1,5},{3,7},... | collective-permute-start | bytes 442376 | tf_op jit(solution)/shard_map/ppermute | solution.py:323
  19.1 0.4 collective-permute-start.4
  19.5 0.0 collective-permute-done.7
  19.5 0.1 add.42
  19.6 1.6 %collective-permute-start.8 = (f32[72,512]{1,0:T(8,128)S(1)}, f32[72,512]{1,0:T(8,128)S(1)}, u32[]{:S(2)}, u32[]{:S(2)}) collective-permute-start(f32[72,512]{1,0:T(8,128)S(1)} %get-tuple-element.29), channel_id=1, source_target_pairs={{0,2},{2,0},{4,6},{6,4},{8,10},{10,8},{12,14},{14,12},{1,3},{3,1},... | collective-permute-start | bytes 442376 | tf_op jit(solution)/shard_map/ppermute | solution.py:323
  21.2 1.6 %collective-permute-start.9 = (f32[72,512]{1,0:T(8,128)S(1)}, f32[72,512]{1,0:T(8,128)S(1)}, u32[]{:S(2)}, u32[]{:S(2)}) collective-permute-start(f32[72,512]{1,0:T(8,128)S(1)} %get-tuple-element.28), channel_id=1, source_target_pairs={{0,4},{2,6},{4,0},{6,2},{8,12},{10,14},{12,8},{14,10},{1,5},{3,7},... | collective-permute-start | bytes 442376 | tf_op jit(solution)/shard_map/ppermute | solution.py:323
  22.8 0.0 collective-permute-done.2
  22.8 2.1 %collective-permute-start.10 = (f32[72,512]{1,0:T(8,128)S(1)}, f32[72,512]{1,0:T(8,128)S(1)}, u32[]{:S(2)}, u32[]{:S(2)}) collective-permute-start(f32[72,512]{1,0:T(8,128)S(1)} %get-tuple-element.27), channel_id=1, source_target_pairs={{0,6},{2,4},{4,2},{6,0},{8,14},{10,12},{12,10},{14,8},{1,7},{3,5},... | collective-permute-start | bytes 442376 | tf_op jit(solution)/shard_map/ppermute | solution.py:323
  24.8 0.0 collective-permute-done.3
  24.9 2.2 %collective-permute-done.4 = f32[72,512]{1,0:T(8,128)S(1)} collective-permute-done((f32[72,512]{1,0:T(8,128)S(1)}, f32[72,512]{1,0:T(8,128)S(1)}, u32[]{:S(2)}, u32[]{:S(2)}) %collective-permute-start.4) | collective-permute-done | bytes 147488 | tf_op jit(solution)/shard_map/ppermute | solution.py:323
  27.1 2.7 %collective-permute-start.5 = (f32[72,512]{1,0:T(8,128)S(1)}, f32[72,512]{1,0:T(8,128)S(1)}, u32[]{:S(2)}, u32[]{:S(2)}) collective-permute-start(f32[72,512]{1,0:T(8,128)S(1)} %add.40), channel_id=1, source_target_pairs={{0,8},{2,10},{4,12},{6,14},{8,0},{10,2},{12,4},{14,6},{1,9},{3,11}... | collective-permute-start | bytes 442376 | tf_op jit(solution)/shard_map/ppermute | solution.py:323
  29.8 0.0 collective-permute-done.8
  29.8 3.9 %collective-permute-done.9 = f32[72,512]{1,0:T(8,128)S(1)} collective-permute-done((f32[72,512]{1,0:T(8,128)S(1)}, f32[72,512]{1,0:T(8,128)S(1)}, u32[]{:S(2)}, u32[]{:S(2)}) %collective-permute-start.9) | collective-permute-done | bytes 147488 | tf_op jit(solution)/shard_map/ppermute | solution.py:323
  33.7 1.9 %collective-permute-done.10 = f32[72,512]{1,0:T(8,128)S(1)} collective-permute-done((f32[72,512]{1,0:T(8,128)S(1)}, f32[72,512]{1,0:T(8,128)S(1)}, u32[]{:S(2)}, u32[]{:S(2)}) %collective-permute-start.10) | collective-permute-done | bytes 147488 | tf_op jit(solution)/shard_map/ppermute | solution.py:323
  35.7 1.0 %collective-permute-start.11 = (f32[72,512]{1,0:T(8,128)S(1)}, f32[72,512]{1,0:T(8,128)S(1)}, u32[]{:S(2)}, u32[]{:S(2)}) collective-permute-start(f32[72,512]{1,0:T(8,128)S(1)} %add.45), channel_id=1, source_target_pairs={{0,8},{2,10},{4,12},{6,14},{8,0},{10,2},{12,4},{14,6},{1,9},{3,11}... | collective-permute-start | bytes 442376 | tf_op jit(solution)/shard_map/ppermute | solution.py:323
  36.7 0.0 collective-permute-done.5
  36.8 1.2 %collective-permute-start.12 = (f32[64,512]{1,0:T(8,128)S(1)}, f32[64,512]{1,0:T(8,128)S(1)}, u32[]{:S(2)}, u32[]{:S(2)}) collective-permute-start(f32[64,512]{1,0:T(8,128)S(1)} %slice.68.refs_0_), channel_id=1, source_target_pairs={{0,2},{2,0},{4,6},{6,4},{8,10},{10,8},{12,14},{14,12},{1,3},{3,1},... | collective-permute-start | bytes 393224 | tf_op jit(solution)/shard_map/ppermute | solution.py:323
  38.0 0.7 %collective-permute-start.6 = (f32[8,512]{1,0:T(8,128)S(1)}, f32[8,512]{1,0:T(8,128)S(1)}, u32[]{:S(2)}, u32[]{:S(2)}) collective-permute-start(f32[8,512]{1,0:T(8,128)S(1)} %slice.62.own_ref), channel_id=1, source_target_pairs={{0,1},{1,0},{2,3},{3,2},{4,5},{5,4},{6,7},{7,6},{8,9},{9,8},{10,11... | collective-permute-start | bytes 49160 | tf_op jit(solution)/shard_map/ppermute | solution.py:359
  38.7 2.8 %collective-permute-start.13 = (f32[64,512]{1,0:T(8,128)S(1)}, f32[64,512]{1,0:T(8,128)S(1)}, u32[]{:S(2)}, u32[]{:S(2)}) collective-permute-start(f32[64,512]{1,0:T(8,128)S(1)} %slice.68.refs_0_), channel_id=1, source_target_pairs={{0,4},{2,6},{4,0},{6,2},{8,12},{10,14},{12,8},{14,10},{1,5},{3,7},... | collective-permute-start | bytes 393224 | tf_op jit(solution)/shard_map/ppermute | solution.py:323
  41.5 0.0 collective-permute-start.14
  41.5 2.6 %collective-permute-done.11 = f32[72,512]{1,0:T(8,128)S(1)} collective-permute-done((f32[72,512]{1,0:T(8,128)S(1)}, f32[72,512]{1,0:T(8,128)S(1)}, u32[]{:S(2)}, u32[]{:S(2)}) %collective-permute-start.11) | collective-permute-done | bytes 147488 | tf_op jit(solution)/shard_map/ppermute | solution.py:323
  44.1 1.8 %collective-permute-start.15 = (f32[64,512]{1,0:T(8,128)S(1)}, f32[64,512]{1,0:T(8,128)S(1)}, u32[]{:S(2)}, u32[]{:S(2)}) collective-permute-start(f32[64,512]{1,0:T(8,128)S(1)} %slice.69.refs_4_), channel_id=1, source_target_pairs={{0,2},{2,0},{4,6},{6,4},{8,10},{10,8},{12,14},{14,12},{1,3},{3,1},... | collective-permute-start | bytes 393224 | tf_op jit(solution)/shard_map/ppermute | solution.py:323
  46.0 0.0 collective-permute-done.6.other_ref
  46.0 0.0 collective-permute-start.16
  46.0 0.0 collective-permute-done.12.refs_1_
  46.0 1.7 %collective-permute-start.17 = (f32[64,512]{1,0:T(8,128)S(1)}, f32[64,512]{1,0:T(8,128)S(1)}, u32[]{:S(2)}, u32[]{:S(2)}) collective-permute-start(f32[64,512]{1,0:T(8,128)S(1)} %slice.69.refs_4_), channel_id=1, source_target_pairs={{0,6},{2,4},{4,2},{6,0},{8,14},{10,12},{12,10},{14,8},{1,7},{3,5},... | collective-permute-start | bytes 393224 | tf_op jit(solution)/shard_map/ppermute | solution.py:323
  47.7 5.1 %gram_factor.1.inverse_ref = f32[128,128]{1,0:T(8,128)S(1)} custom-call(s32[4]{0:T(128)S(1)} %pad_add_fusion.info_ref, f32[8,512]{1,0:T(8,128)S(1)} %slice.62.own_ref, f32[8,512]{1,0:T(8,128)S(1)} %collective-permute-done.6.other_ref, f32[8,512]{1,0:T(8,128)S(1)} %slice.67.pair_ref), custom_call_target="tpu_custom_call" | custom-call | tf_op jit(solution)/shard_map/gram_factor/pallas_call | solution.py:362
  52.8 0.0 collective-permute-done.13.refs_2_
  52.8 0.0 collective-permute-done.14.refs_3_
  52.8 0.0 collective-permute-done.15.refs_5_
  52.9 0.0 collective-permute-done.16.refs_6_
  52.9 1.4 %collective-permute-done.17.refs_7_ = f32[64,512]{1,0:T(8,128)S(1)} collective-permute-done((f32[64,512]{1,0:T(8,128)S(1)}, f32[64,512]{1,0:T(8,128)S(1)}, u32[]{:S(2)}, u32[]{:S(2)}) %collective-permute-start.17) | collective-permute-done | bytes 131104 | tf_op jit(solution)/shard_map/ppermute | solution.py:323
  54.2 1.9 %apply_inverse.1 = f32[1,128,2048]{2,1,0:T(8,128)} custom-call(s32[4]{0:T(128)S(1)} %pad_add_fusion.info_ref, f32[128,128]{1,0:T(8,128)S(1)} %gram_factor.1.inverse_ref, f32[64,512]{1,0:T(8,128)S(1)} %slice.68.refs_0_, f32[64,512]{1,0:T(8,128)S(1)} %collective-permute-done.12.refs_1_, f32[64,512]{1,0:T(8,128)S(1)} %collective-permute-done.13.refs_2_, ...), custom_call_target="tpu_custom_call" | custom-call | tf_op jit(solution)/shard_map/apply_inverse/pallas_call | solution.py:371
  (16 shorter events, 0.3 us)
Async XLA Ops:
  2.1 10.3 %collective-permute-start = (f32[64,1024]{1,0:T(8,128)S(1)}, f32[64,1024]{1,0:T(8,128)S(1)}, u32[]{:S(2)}, u32[]{:S(2)}) collective-permute-start(f32[64,1024]{1,0:T(8,128)S(1)} %get-tuple-element.17.lead_ref.own_ref), channel_id=1, source_target_pairs={{0,1},{1,0},{2,3},{3,2},{4,5},{5,4},{6,7},{7,6},{8,9},{9,8},{10,11... | collective-permute-start | bytes 786440 | tf_op jit(solution)/shard_map/ppermute | solution.py:288
  5.2 0.7 %copy-start = (s32[16,1]{0,1:T(1,128)S(1)}, s32[16,1]{0,1:T(1,128)}, u32[]{:S(2)}) copy-start(s32[16,1]{0,1:T(1,128)} %param.5) | copy-start | bytes 196
  12.4 3.4 %collective-permute-start.1 = (f32[4,72,512]{2,1,0:T(8,128)S(1)}, f32[4,72,512]{2,1,0:T(8,128)S(1)}, u32[]{:S(2)}, u32[]{:S(2)}) collective-permute-start(f32[4,72,512]{2,1,0:T(8,128)S(1)} %get-tuple-element.20), channel_id=1, source_target_pairs={{0,16},{16,0},{1,17},{17,1},{2,18},{18,2},{3,19},{19,3},{4,20},{20... | collective-permute-start | bytes 1769480 | tf_op jit(solution)/shard_map/ppermute | solution.py:320
  15.2 4.3 %collective-permute-start.7 = (f32[4,72,512]{2,1,0:T(8,128)S(1)}, f32[4,72,512]{2,1,0:T(8,128)S(1)}, u32[]{:S(2)}, u32[]{:S(2)}) collective-permute-start(f32[4,72,512]{2,1,0:T(8,128)S(1)} %get-tuple-element.26), channel_id=1, source_target_pairs={{0,16},{16,0},{1,17},{17,1},{2,18},{18,2},{3,19},{19,3},{4,20},{20... | collective-permute-start | bytes 1769480 | tf_op jit(solution)/shard_map/ppermute | solution.py:320
  15.9 6.8 %collective-permute-start.2 = (f32[72,512]{1,0:T(8,128)S(1)}, f32[72,512]{1,0:T(8,128)S(1)}, u32[]{:S(2)}, u32[]{:S(2)}) collective-permute-start(f32[72,512]{1,0:T(8,128)S(1)} %get-tuple-element.32), channel_id=1, source_target_pairs={{0,2},{2,0},{4,6},{6,4},{8,10},{10,8},{12,14},{14,12},{1,3},{3,1},... | collective-permute-start | bytes 442376 | tf_op jit(solution)/shard_map/ppermute | solution.py:323
  17.5 7.4 %collective-permute-start.3 = (f32[72,512]{1,0:T(8,128)S(1)}, f32[72,512]{1,0:T(8,128)S(1)}, u32[]{:S(2)}, u32[]{:S(2)}) collective-permute-start(f32[72,512]{1,0:T(8,128)S(1)} %get-tuple-element.31), channel_id=1, source_target_pairs={{0,4},{2,6},{4,0},{6,2},{8,12},{10,14},{12,8},{14,10},{1,5},{3,7},... | collective-permute-start | bytes 442376 | tf_op jit(solution)/shard_map/ppermute | solution.py:323
  19.1 8.0 %collective-permute-start.4 = (f32[72,512]{1,0:T(8,128)S(1)}, f32[72,512]{1,0:T(8,128)S(1)}, u32[]{:S(2)}, u32[]{:S(2)}) collective-permute-start(f32[72,512]{1,0:T(8,128)S(1)} %get-tuple-element.30), channel_id=1, source_target_pairs={{0,6},{2,4},{4,2},{6,0},{8,14},{10,12},{12,10},{14,8},{1,7},{3,5},... | collective-permute-start | bytes 442376 | tf_op jit(solution)/shard_map/ppermute | solution.py:323
  19.6 10.2 %collective-permute-start.8 = (f32[72,512]{1,0:T(8,128)S(1)}, f32[72,512]{1,0:T(8,128)S(1)}, u32[]{:S(2)}, u32[]{:S(2)}) collective-permute-start(f32[72,512]{1,0:T(8,128)S(1)} %get-tuple-element.29), channel_id=1, source_target_pairs={{0,2},{2,0},{4,6},{6,4},{8,10},{10,8},{12,14},{14,12},{1,3},{3,1},... | collective-permute-start | bytes 442376 | tf_op jit(solution)/shard_map/ppermute | solution.py:323
  21.2 12.5 %collective-permute-start.9 = (f32[72,512]{1,0:T(8,128)S(1)}, f32[72,512]{1,0:T(8,128)S(1)}, u32[]{:S(2)}, u32[]{:S(2)}) collective-permute-start(f32[72,512]{1,0:T(8,128)S(1)} %get-tuple-element.28), channel_id=1, source_target_pairs={{0,4},{2,6},{4,0},{6,2},{8,12},{10,14},{12,8},{14,10},{1,5},{3,7},... | collective-permute-start | bytes 442376 | tf_op jit(solution)/shard_map/ppermute | solution.py:323
  22.8 12.9 %collective-permute-start.10 = (f32[72,512]{1,0:T(8,128)S(1)}, f32[72,512]{1,0:T(8,128)S(1)}, u32[]{:S(2)}, u32[]{:S(2)}) collective-permute-start(f32[72,512]{1,0:T(8,128)S(1)} %get-tuple-element.27), channel_id=1, source_target_pairs={{0,6},{2,4},{4,2},{6,0},{8,14},{10,12},{12,10},{14,8},{1,7},{3,5},... | collective-permute-start | bytes 442376 | tf_op jit(solution)/shard_map/ppermute | solution.py:323
  27.1 9.6 %collective-permute-start.5 = (f32[72,512]{1,0:T(8,128)S(1)}, f32[72,512]{1,0:T(8,128)S(1)}, u32[]{:S(2)}, u32[]{:S(2)}) collective-permute-start(f32[72,512]{1,0:T(8,128)S(1)} %add.40), channel_id=1, source_target_pairs={{0,8},{2,10},{4,12},{6,14},{8,0},{10,2},{12,4},{14,6},{1,9},{3,11}... | collective-permute-start | bytes 442376 | tf_op jit(solution)/shard_map/ppermute | solution.py:323
  35.7 8.4 %collective-permute-start.11 = (f32[72,512]{1,0:T(8,128)S(1)}, f32[72,512]{1,0:T(8,128)S(1)}, u32[]{:S(2)}, u32[]{:S(2)}) collective-permute-start(f32[72,512]{1,0:T(8,128)S(1)} %add.45), channel_id=1, source_target_pairs={{0,8},{2,10},{4,12},{6,14},{8,0},{10,2},{12,4},{14,6},{1,9},{3,11}... | collective-permute-start | bytes 442376 | tf_op jit(solution)/shard_map/ppermute | solution.py:323
  36.8 9.2 %collective-permute-start.12 = (f32[64,512]{1,0:T(8,128)S(1)}, f32[64,512]{1,0:T(8,128)S(1)}, u32[]{:S(2)}, u32[]{:S(2)}) collective-permute-start(f32[64,512]{1,0:T(8,128)S(1)} %slice.68.refs_0_), channel_id=1, source_target_pairs={{0,2},{2,0},{4,6},{6,4},{8,10},{10,8},{12,14},{14,12},{1,3},{3,1},... | collective-permute-start | bytes 393224 | tf_op jit(solution)/shard_map/ppermute | solution.py:323
  38.0 8.0 %collective-permute-start.6 = (f32[8,512]{1,0:T(8,128)S(1)}, f32[8,512]{1,0:T(8,128)S(1)}, u32[]{:S(2)}, u32[]{:S(2)}) collective-permute-start(f32[8,512]{1,0:T(8,128)S(1)} %slice.62.own_ref), channel_id=1, source_target_pairs={{0,1},{1,0},{2,3},{3,2},{4,5},{5,4},{6,7},{7,6},{8,9},{9,8},{10,11... | collective-permute-start | bytes 49160 | tf_op jit(solution)/shard_map/ppermute | solution.py:359
  38.7 14.1 %collective-permute-start.13 = (f32[64,512]{1,0:T(8,128)S(1)}, f32[64,512]{1,0:T(8,128)S(1)}, u32[]{:S(2)}, u32[]{:S(2)}) collective-permute-start(f32[64,512]{1,0:T(8,128)S(1)} %slice.68.refs_0_), channel_id=1, source_target_pairs={{0,4},{2,6},{4,0},{6,2},{8,12},{10,14},{12,8},{14,10},{1,5},{3,7},... | collective-permute-start | bytes 393224 | tf_op jit(solution)/shard_map/ppermute | solution.py:323
  41.5 11.4 %collective-permute-start.14 = (f32[64,512]{1,0:T(8,128)S(1)}, f32[64,512]{1,0:T(8,128)S(1)}, u32[]{:S(2)}, u32[]{:S(2)}) collective-permute-start(f32[64,512]{1,0:T(8,128)S(1)} %slice.68.refs_0_), channel_id=1, source_target_pairs={{0,6},{2,4},{4,2},{6,0},{8,14},{10,12},{12,10},{14,8},{1,7},{3,5},... | collective-permute-start | bytes 393224 | tf_op jit(solution)/shard_map/ppermute | solution.py:323
  44.1 8.7 %collective-permute-start.15 = (f32[64,512]{1,0:T(8,128)S(1)}, f32[64,512]{1,0:T(8,128)S(1)}, u32[]{:S(2)}, u32[]{:S(2)}) collective-permute-start(f32[64,512]{1,0:T(8,128)S(1)} %slice.69.refs_4_), channel_id=1, source_target_pairs={{0,2},{2,0},{4,6},{6,4},{8,10},{10,8},{12,14},{14,12},{1,3},{3,1},... | collective-permute-start | bytes 393224 | tf_op jit(solution)/shard_map/ppermute | solution.py:323
  46.0 6.9 %collective-permute-start.16 = (f32[64,512]{1,0:T(8,128)S(1)}, f32[64,512]{1,0:T(8,128)S(1)}, u32[]{:S(2)}, u32[]{:S(2)}) collective-permute-start(f32[64,512]{1,0:T(8,128)S(1)} %slice.69.refs_4_), channel_id=1, source_target_pairs={{0,4},{2,6},{4,0},{6,2},{8,12},{10,14},{12,8},{14,10},{1,5},{3,7},... | collective-permute-start | bytes 393224 | tf_op jit(solution)/shard_map/ppermute | solution.py:323
  46.0 8.3 %collective-permute-start.17 = (f32[64,512]{1,0:T(8,128)S(1)}, f32[64,512]{1,0:T(8,128)S(1)}, u32[]{:S(2)}, u32[]{:S(2)}) collective-permute-start(f32[64,512]{1,0:T(8,128)S(1)} %slice.69.refs_4_), channel_id=1, source_target_pairs={{0,6},{2,4},{4,2},{6,0},{8,14},{10,12},{12,10},{14,8},{1,7},{3,5},... | collective-permute-start | bytes 393224 | tf_op jit(solution)/shard_map/ppermute | solution.py:323

commit v5 on v4

--- a/solution.py
+++ b/solution.py
@@ -268,7 +268,9 @@
     width = columns // pieces
     row, leaf, col = lax.axis_index("row"), lax.axis_index("leaf"), lax.axis_index("col")
     own_panel = col if col_count == PANELS else jnp.zeros_like(col)
-    info = jnp.stack([row % pieces, leaf, own_panel, col]).astype(jnp.int32)
+    mirror = pieces // 2
+    piece = row % pieces ^ (row // pieces % 2 * mirror)
+    info = jnp.stack([piece, leaf, own_panel, col]).astype(jnp.int32)
     params = pltpu.CompilerParams(vmem_limit_bytes=VMEM_LIMIT)
     wide_params = pltpu.CompilerParams(vmem_limit_bytes=OWN_VMEM_LIMIT)
 
@@ -330,15 +332,21 @@
 
     def reduce_far(total):
         for bit in range(split_bits, bits):
-            total = total + over_row(total, 1 << bit)
+            total = total + over_row(total, 1 << bit | (mirror if bit == split_bits else 0))
         return total
+
+    def gather_by_steps(total):
+        held = [total[:edge]]
+        for bit in range(1, split_bits):
+            held = held + [over_row(piece, 1 << bit) for piece in held]
+        return [piece for even in held for piece in (even, over_row(even, 1))]
 
     def gather_pieces(total):
         return [total[:edge]] + [over_row(total[:edge], near) for near in range(1, pieces)]
 
     send, lead_other = lax.optimization_barrier((send, lead_other))
     own_sum = reduce_far(reduce_near(over_leaf(keep, send), range(1, pieces)))
-    own_pieces = gather_pieces(own_sum)
+    own_pieces = gather_by_steps(own_sum)
 
     pair_rows = gram_rows if swap else 2 * gram_rows
     keep, send = pl.pallas_call(

time: 56.4 us -> 55.4 us (0.982)
  waiting for transfers between devices: 12.1 us -> 5.19 us
  starting transfers between devices: 24.3 us -> 30.2 us
    ppermute x14, waiting for transfers between devices: 12 us -> 5.18 us  [over_row(): return lax.ppermute(value, 'row', [(i, i ^ bit) for i in range(row_count)])]
    ppermute x14, starting transfers between devices: 20 us -> 25.7 us  [over_row(): return lax.ppermute(value, 'row', [(i, i ^ bit) for i in range(row_count)])]
  transfers between devices with their start and end apart: 18 -> 18, of which waited for: 5 -> 4; matrix products, arithmetic and copies ran while one was open for 1% -> 1% of each run, Pallas kernels for 26% -> 26%
where the time goes in v5:
time: 55.4 us; the launch traced here: 55.1 us
  starting transfers between devices  30.2 us (55%)
  Pallas kernels  16.6 us (30%)
  waiting for transfers between devices  5.19 us (9%)
  local copies, waits for them, and re-layouts  1.83 us (3%)
  other arithmetic  1.18 us (2%)
    ppermute x14, starting transfers between devices, over_row(): return lax.ppermute(value, 'row', [(i, i ^ bit) for i in range(row_count)])  25.7 us
    pallas_call x1, Pallas kernels, per_device(): pl.pallas_call(functools.partial(own_kernel, row_count), out_shape=(sums(...  6.54 us
    ppermute x14, waiting for transfers between devices, over_row(): return lax.ppermute(value, 'row', [(i, i ^ bit) for i in range(row_count)])  5.18 us
    pallas_call x1, Pallas kernels, per_device(): pl.pallas_call(functools.partial(factor_kernel, start), out_shape=jax.Sha...  5.12 us
    ppermute x1, starting transfers between devices, per_device(): lead_other = lax.ppermute(lead, 'col', [(i, 1 - i) for i in range(PANELS)])  3.03 us
    pallas_call x1, Pallas kernels, per_device(): pl.pallas_call(functools.partial(pair_kernel, not swap), out_shape=(sums(...  2.73 us
    pallas_call x1, Pallas kernels, per_device(): pl.pallas_call(functools.partial(final_kernel, pieces, edge), out_shape=j...  1.93 us
  transfers between devices with their start and end apart: 18, of which 4 were waited for; matrix products, arithmetic and copies ran while one was open for 1% of the time, Pallas kernels for 26%

profile of v5, /device:TPU:0, one launch (start us, length us, event | category | flops | bytes accessed | tf_op | source)
XLA Modules:
  0.0 55.1 jit_solution(3074997556240739920)
XLA Ops:
  0.0 0.7 %convert_element_type.5 = f32[16,32]{1,0:T(8,128)S(1)} convert(s32[16,32]{1,0:T(8,128)} %param.4) | non-fusion elementwise | flops 512 | bytes 4096 | tf_op jit(solution)/shard_map/convert_element_type | solution.py:278
  0.7 1.1 %slice.42 = f32[16,64,64]{2,1,0:T(8,128)S(1)} slice(f32[16,64,2048]{2,1,0:T(8,128)} %tiles_ref.1), slice={[0:16], [0:64], [0:64]} | slice | bytes 524288 | tf_op jit(solution)/shard_map/slice | solution.py:286
  1.8 0.3 lead_prep.1
  2.1 3.0 %collective-permute-start = (f32[64,1024]{1,0:T(8,128)S(1)}, f32[64,1024]{1,0:T(8,128)S(1)}, u32[]{:S(2)}, u32[]{:S(2)}) collective-permute-start(f32[64,1024]{1,0:T(8,128)S(1)} %get-tuple-element.17.lead_ref.own_ref), channel_id=1, source_target_pairs={{0,1},{1,0},{2,3},{3,2},{4,5},{5,4},{6,7},{7,6},{8,9},{9,8},{10,11... | collective-permute-start | bytes 786440 | tf_op jit(solution)/shard_map/ppermute | solution.py:290
  5.1 0.1 pad_add_fusion.info_ref
  5.2 0.0 copy-start
  5.2 0.7 %copy-done = s32[16,1]{0,1:T(1,128)S(1)} copy-done((s32[16,1]{0,1:T(1,128)S(1)}, s32[16,1]{0,1:T(1,128)}, u32[]{:S(2)}) %copy-start) | copy-done | bytes 88
  5.9 6.5 %panel_own.1 = (f32[4,72,512]{2,1,0:T(8,128)S(1)}, f32[4,72,512]{2,1,0:T(8,128)S(1)}, bf16[1024,2048]{1,0:T(8,128)(2,1)S(1)}, bf16[1024,2048]{1,0:T(8,128)(2,1)S(1)}, f32[1,1024]{1,0:T(1,128)S(1)}) custom-call(s32[4]{0:T(128)S(1)} %pad_add_fusion.info_ref, s32[1,16]{1,0:T(1,128)S(1)} %bitcast.26, f32[16,32]{1,0:T(8,128)S(1)} %get-tuple-element.16.mask_ref, ...), custom_call_target="tpu_custom_call" | custom-call | flops 1610612736 | bytes 8388608 | tf_op jit(solution)/shard_map/panel_own/pallas_call | solution.py:304
  12.4 0.0 collective-permute-done.lead_ref
  12.4 0.1 collective-permute-start.1
  12.5 2.7 %panel_pair.1 = (f32[4,72,512]{2,1,0:T(8,128)S(1)}, f32[4,72,512]{2,1,0:T(8,128)S(1)}) custom-call(s32[4]{0:T(128)S(1)} %pad_add_fusion.info_ref, f32[1,1024]{1,0:T(1,128)S(1)} %get-tuple-element.21.mine_ref, f32[64,1024]{1,0:T(8,128)S(1)} %collective-permute-done.lead_ref, f32[64,1024]{1,0:T(8,128)S(1)} %get-tuple-element.17.lead_ref.own_ref, ...), custom_call_target="tpu_custom_call" | custom-call | flops 1610612736 | bytes 8388608 | tf_op jit(solution)/shard_map/panel_pair/pallas_call | solution.py:352
  15.2 0.6 %collective-permute-start.7 = (f32[4,72,512]{2,1,0:T(8,128)S(1)}, f32[4,72,512]{2,1,0:T(8,128)S(1)}, u32[]{:S(2)}, u32[]{:S(2)}) collective-permute-start(f32[4,72,512]{2,1,0:T(8,128)S(1)} %get-tuple-element.26), channel_id=1, source_target_pairs={{0,16},{16,0},{1,17},{17,1},{2,18},{18,2},{3,19},{19,3},{4,20},{20... | collective-permute-start | bytes 1769480 | tf_op jit(solution)/shard_map/ppermute | solution.py:322
  15.8 0.0 collective-permute-done.1
  15.8 0.1 add.42
  15.9 1.6 %collective-permute-start.2 = (f32[72,512]{1,0:T(8,128)S(1)}, f32[72,512]{1,0:T(8,128)S(1)}, u32[]{:S(2)}, u32[]{:S(2)}) collective-permute-start(f32[72,512]{1,0:T(8,128)S(1)} %get-tuple-element.32), channel_id=1, source_target_pairs={{0,2},{2,0},{4,6},{6,4},{8,10},{10,8},{12,14},{14,12},{1,3},{3,1},... | collective-permute-start | bytes 442376 | tf_op jit(solution)/shard_map/ppermute | solution.py:325
  17.5 1.6 %collective-permute-start.3 = (f32[72,512]{1,0:T(8,128)S(1)}, f32[72,512]{1,0:T(8,128)S(1)}, u32[]{:S(2)}, u32[]{:S(2)}) collective-permute-start(f32[72,512]{1,0:T(8,128)S(1)} %get-tuple-element.31), channel_id=1, source_target_pairs={{0,4},{2,6},{4,0},{6,2},{8,12},{10,14},{12,8},{14,10},{1,5},{3,7},... | collective-permute-start | bytes 442376 | tf_op jit(solution)/shard_map/ppermute | solution.py:325
  19.1 0.4 collective-permute-start.4
  19.5 0.0 collective-permute-done.7
  19.5 0.1 add.47
  19.6 1.6 %collective-permute-start.8 = (f32[72,512]{1,0:T(8,128)S(1)}, f32[72,512]{1,0:T(8,128)S(1)}, u32[]{:S(2)}, u32[]{:S(2)}) collective-permute-start(f32[72,512]{1,0:T(8,128)S(1)} %get-tuple-element.29), channel_id=1, source_target_pairs={{0,2},{2,0},{4,6},{6,4},{8,10},{10,8},{12,14},{14,12},{1,3},{3,1},... | collective-permute-start | bytes 442376 | tf_op jit(solution)/shard_map/ppermute | solution.py:325
  21.2 1.6 %collective-permute-start.9 = (f32[72,512]{1,0:T(8,128)S(1)}, f32[72,512]{1,0:T(8,128)S(1)}, u32[]{:S(2)}, u32[]{:S(2)}) collective-permute-start(f32[72,512]{1,0:T(8,128)S(1)} %get-tuple-element.28), channel_id=1, source_target_pairs={{0,4},{2,6},{4,0},{6,2},{8,12},{10,14},{12,8},{14,10},{1,5},{3,7},... | collective-permute-start | bytes 442376 | tf_op jit(solution)/shard_map/ppermute | solution.py:325
  22.8 0.0 collective-permute-done.2
  22.8 2.1 %collective-permute-start.10 = (f32[72,512]{1,0:T(8,128)S(1)}, f32[72,512]{1,0:T(8,128)S(1)}, u32[]{:S(2)}, u32[]{:S(2)}) collective-permute-start(f32[72,512]{1,0:T(8,128)S(1)} %get-tuple-element.27), channel_id=1, source_target_pairs={{0,6},{2,4},{4,2},{6,0},{8,14},{10,12},{12,10},{14,8},{1,7},{3,5},... | collective-permute-start | bytes 442376 | tf_op jit(solution)/shard_map/ppermute | solution.py:325
  24.8 0.0 collective-permute-done.3
  24.9 2.2 %collective-permute-done.4 = f32[72,512]{1,0:T(8,128)S(1)} collective-permute-done((f32[72,512]{1,0:T(8,128)S(1)}, f32[72,512]{1,0:T(8,128)S(1)}, u32[]{:S(2)}, u32[]{:S(2)}) %collective-permute-start.4) | collective-permute-done | bytes 147488 | tf_op jit(solution)/shard_map/ppermute | solution.py:325
  27.1 3.9 %collective-permute-start.5 = (f32[72,512]{1,0:T(8,128)S(1)}, f32[72,512]{1,0:T(8,128)S(1)}, u32[]{:S(2)}, u32[]{:S(2)}) collective-permute-start(f32[72,512]{1,0:T(8,128)S(1)} %add.45), channel_id=1, source_target_pairs={{0,12},{2,14},{4,8},{6,10},{8,4},{10,6},{12,0},{14,2},{1,13},{3,15... | collective-permute-start | bytes 442376 | tf_op jit(solution)/shard_map/ppermute | solution.py:325
  31.1 0.0 collective-permute-done.8
  31.1 0.0 collective-permute-done.9
  31.1 1.7 %collective-permute-done.10 = f32[72,512]{1,0:T(8,128)S(1)} collective-permute-done((f32[72,512]{1,0:T(8,128)S(1)}, f32[72,512]{1,0:T(8,128)S(1)}, u32[]{:S(2)}, u32[]{:S(2)}) %collective-permute-start.10) | collective-permute-done | bytes 147488 | tf_op jit(solution)/shard_map/ppermute | solution.py:325
  32.8 6.5 %collective-permute-start.11 = (f32[72,512]{1,0:T(8,128)S(1)}, f32[72,512]{1,0:T(8,128)S(1)}, u32[]{:S(2)}, u32[]{:S(2)}) collective-permute-start(f32[72,512]{1,0:T(8,128)S(1)} %add.50), channel_id=1, source_target_pairs={{0,12},{2,14},{4,8},{6,10},{8,4},{10,6},{12,0},{14,2},{1,13},{3,15... | collective-permute-start | bytes 442376 | tf_op jit(solution)/shard_map/ppermute | solution.py:325
  39.3 0.0 collective-permute-done.5
  39.3 0.1 collective-permute-start.13
  39.4 0.8 %collective-permute-start.6 = (f32[8,512]{1,0:T(8,128)S(1)}, f32[8,512]{1,0:T(8,128)S(1)}, u32[]{:S(2)}, u32[]{:S(2)}) collective-permute-start(f32[8,512]{1,0:T(8,128)S(1)} %slice.59.own_ref), channel_id=1, source_target_pairs={{0,1},{1,0},{2,3},{3,2},{4,5},{5,4},{6,7},{7,6},{8,9},{9,8},{10,11... | collective-permute-start | bytes 49160 | tf_op jit(solution)/shard_map/ppermute | solution.py:367
  40.2 1.5 %collective-permute-start.12 = (f32[64,512]{1,0:T(8,128)S(1)}, f32[64,512]{1,0:T(8,128)S(1)}, u32[]{:S(2)}, u32[]{:S(2)}) collective-permute-start(f32[64,512]{1,0:T(8,128)S(1)} %slice.65.refs_0_), channel_id=1, source_target_pairs={{0,2},{2,0},{4,6},{6,4},{8,10},{10,8},{12,14},{14,12},{1,3},{3,1},... | collective-permute-start | bytes 393224 | tf_op jit(solution)/shard_map/ppermute | solution.py:325
  41.7 0.8 %collective-permute-done.11 = f32[72,512]{1,0:T(8,128)S(1)} collective-permute-done((f32[72,512]{1,0:T(8,128)S(1)}, f32[72,512]{1,0:T(8,128)S(1)}, u32[]{:S(2)}, u32[]{:S(2)}) %collective-permute-start.11) | collective-permute-done | bytes 147488 | tf_op jit(solution)/shard_map/ppermute | solution.py:325
  42.6 1.6 %collective-permute-start.15 = (f32[64,512]{1,0:T(8,128)S(1)}, f32[64,512]{1,0:T(8,128)S(1)}, u32[]{:S(2)}, u32[]{:S(2)}) collective-permute-start(f32[64,512]{1,0:T(8,128)S(1)} %slice.66.refs_4_), channel_id=1, source_target_pairs={{0,2},{2,0},{4,6},{6,4},{8,10},{10,8},{12,14},{14,12},{1,3},{3,1},... | collective-permute-start | bytes 393224 | tf_op jit(solution)/shard_map/ppermute | solution.py:325
  44.1 1.1 %collective-permute-start.16 = (f32[64,512]{1,0:T(8,128)S(1)}, f32[64,512]{1,0:T(8,128)S(1)}, u32[]{:S(2)}, u32[]{:S(2)}) collective-permute-start(f32[64,512]{1,0:T(8,128)S(1)} %slice.66.refs_4_), channel_id=1, source_target_pairs={{0,4},{2,6},{4,0},{6,2},{8,12},{10,14},{12,8},{14,10},{1,5},{3,7},... | collective-permute-start | bytes 393224 | tf_op jit(solution)/shard_map/ppermute | solution.py:325
  45.3 0.0 collective-permute-done.6.other_ref
  45.3 0.9 %collective-permute-start.17 = (f32[64,512]{1,0:T(8,128)S(1)}, f32[64,512]{1,0:T(8,128)S(1)}, u32[]{:S(2)}, u32[]{:S(2)}) collective-permute-start(f32[64,512]{1,0:T(8,128)S(1)} %slice.66.refs_4_), channel_id=1, source_target_pairs={{0,6},{2,4},{4,2},{6,0},{8,14},{10,12},{12,10},{14,8},{1,7},{3,5},... | collective-permute-start | bytes 393224 | tf_op jit(solution)/shard_map/ppermute | solution.py:325
  46.1 0.0 collective-permute-done.13.refs_2_
  46.1 1.5 %collective-permute-start.14 = (f32[64,512]{1,0:T(8,128)S(1)}, f32[64,512]{1,0:T(8,128)S(1)}, u32[]{:S(2)}, u32[]{:S(2)}) collective-permute-start(f32[64,512]{1,0:T(8,128)S(1)} %collective-permute-done.13.refs_2_), channel_id=1, source_target_pairs={{0,2},{2,0},{4,6},{6,4},{8,10},{10,8},{12,14},{14,12},{1,3},{3,1},... | collective-permute-start | bytes 393224 | tf_op jit(solution)/shard_map/ppermute | solution.py:325
  47.6 5.1 %gram_factor.1.inverse_ref = f32[128,128]{1,0:T(8,128)S(1)} custom-call(s32[4]{0:T(128)S(1)} %pad_add_fusion.info_ref, f32[8,512]{1,0:T(8,128)S(1)} %slice.59.own_ref, f32[8,512]{1,0:T(8,128)S(1)} %collective-permute-done.6.other_ref, f32[8,512]{1,0:T(8,128)S(1)} %slice.64.pair_ref), custom_call_target="tpu_custom_call" | custom-call | tf_op jit(solution)/shard_map/gram_factor/pallas_call | solution.py:370
  52.8 0.0 collective-permute-done.12.refs_1_
  52.8 0.0 collective-permute-done.15.refs_5_
  52.8 0.0 collective-permute-done.16.refs_6_
  52.8 0.0 collective-permute-done.17.refs_7_
  52.8 0.4 collective-permute-done.14.refs_3_
  53.2 1.9 %apply_inverse.1 = f32[1,128,2048]{2,1,0:T(8,128)} custom-call(s32[4]{0:T(128)S(1)} %pad_add_fusion.info_ref, f32[128,128]{1,0:T(8,128)S(1)} %gram_factor.1.inverse_ref, f32[64,512]{1,0:T(8,128)S(1)} %slice.65.refs_0_, f32[64,512]{1,0:T(8,128)S(1)} %collective-permute-done.12.refs_1_, f32[64,512]{1,0:T(8,128)S(1)} %collective-permute-done.13.refs_2_, ...), custom_call_target="tpu_custom_call" | custom-call | tf_op jit(solution)/shard_map/apply_inverse/pallas_call | solution.py:379
  (16 shorter events, 0.3 us)
Async XLA Ops:
  2.1 10.3 %collective-permute-start = (f32[64,1024]{1,0:T(8,128)S(1)}, f32[64,1024]{1,0:T(8,128)S(1)}, u32[]{:S(2)}, u32[]{:S(2)}) collective-permute-start(f32[64,1024]{1,0:T(8,128)S(1)} %get-tuple-element.17.lead_ref.own_ref), channel_id=1, source_target_pairs={{0,1},{1,0},{2,3},{3,2},{4,5},{5,4},{6,7},{7,6},{8,9},{9,8},{10,11... | collective-permute-start | bytes 786440 | tf_op jit(solution)/shard_map/ppermute | solution.py:290
  5.2 0.7 %copy-start = (s32[16,1]{0,1:T(1,128)S(1)}, s32[16,1]{0,1:T(1,128)}, u32[]{:S(2)}) copy-start(s32[16,1]{0,1:T(1,128)} %param.5) | copy-start | bytes 196
  12.4 3.4 %collective-permute-start.1 = (f32[4,72,512]{2,1,0:T(8,128)S(1)}, f32[4,72,512]{2,1,0:T(8,128)S(1)}, u32[]{:S(2)}, u32[]{:S(2)}) collective-permute-start(f32[4,72,512]{2,1,0:T(8,128)S(1)} %get-tuple-element.20), channel_id=1, source_target_pairs={{0,16},{16,0},{1,17},{17,1},{2,18},{18,2},{3,19},{19,3},{4,20},{20... | collective-permute-start | bytes 1769480 | tf_op jit(solution)/shard_map/ppermute | solution.py:322
  15.2 4.3 %collective-permute-start.7 = (f32[4,72,512]{2,1,0:T(8,128)S(1)}, f32[4,72,512]{2,1,0:T(8,128)S(1)}, u32[]{:S(2)}, u32[]{:S(2)}) collective-permute-start(f32[4,72,512]{2,1,0:T(8,128)S(1)} %get-tuple-element.26), channel_id=1, source_target_pairs={{0,16},{16,0},{1,17},{17,1},{2,18},{18,2},{3,19},{19,3},{4,20},{20... | collective-permute-start | bytes 1769480 | tf_op jit(solution)/shard_map/ppermute | solution.py:322
  15.9 6.8 %collective-permute-start.2 = (f32[72,512]{1,0:T(8,128)S(1)}, f32[72,512]{1,0:T(8,128)S(1)}, u32[]{:S(2)}, u32[]{:S(2)}) collective-permute-start(f32[72,512]{1,0:T(8,128)S(1)} %get-tuple-element.32), channel_id=1, source_target_pairs={{0,2},{2,0},{4,6},{6,4},{8,10},{10,8},{12,14},{14,12},{1,3},{3,1},... | collective-permute-start | bytes 442376 | tf_op jit(solution)/shard_map/ppermute | solution.py:325
  17.5 7.4 %collective-permute-start.3 = (f32[72,512]{1,0:T(8,128)S(1)}, f32[72,512]{1,0:T(8,128)S(1)}, u32[]{:S(2)}, u32[]{:S(2)}) collective-permute-start(f32[72,512]{1,0:T(8,128)S(1)} %get-tuple-element.31), channel_id=1, source_target_pairs={{0,4},{2,6},{4,0},{6,2},{8,12},{10,14},{12,8},{14,10},{1,5},{3,7},... | collective-permute-start | bytes 442376 | tf_op jit(solution)/shard_map/ppermute | solution.py:325
  19.1 8.0 %collective-permute-start.4 = (f32[72,512]{1,0:T(8,128)S(1)}, f32[72,512]{1,0:T(8,128)S(1)}, u32[]{:S(2)}, u32[]{:S(2)}) collective-permute-start(f32[72,512]{1,0:T(8,128)S(1)} %get-tuple-element.30), channel_id=1, source_target_pairs={{0,6},{2,4},{4,2},{6,0},{8,14},{10,12},{12,10},{14,8},{1,7},{3,5},... | collective-permute-start | bytes 442376 | tf_op jit(solution)/shard_map/ppermute | solution.py:325
  19.6 11.4 %collective-permute-start.8 = (f32[72,512]{1,0:T(8,128)S(1)}, f32[72,512]{1,0:T(8,128)S(1)}, u32[]{:S(2)}, u32[]{:S(2)}) collective-permute-start(f32[72,512]{1,0:T(8,128)S(1)} %get-tuple-element.29), channel_id=1, source_target_pairs={{0,2},{2,0},{4,6},{6,4},{8,10},{10,8},{12,14},{14,12},{1,3},{3,1},... | collective-permute-start | bytes 442376 | tf_op jit(solution)/shard_map/ppermute | solution.py:325
  21.2 9.9 %collective-permute-start.9 = (f32[72,512]{1,0:T(8,128)S(1)}, f32[72,512]{1,0:T(8,128)S(1)}, u32[]{:S(2)}, u32[]{:S(2)}) collective-permute-start(f32[72,512]{1,0:T(8,128)S(1)} %get-tuple-element.28), channel_id=1, source_target_pairs={{0,4},{2,6},{4,0},{6,2},{8,12},{10,14},{12,8},{14,10},{1,5},{3,7},... | collective-permute-start | bytes 442376 | tf_op jit(solution)/shard_map/ppermute | solution.py:325
  22.8 10.0 %collective-permute-start.10 = (f32[72,512]{1,0:T(8,128)S(1)}, f32[72,512]{1,0:T(8,128)S(1)}, u32[]{:S(2)}, u32[]{:S(2)}) collective-permute-start(f32[72,512]{1,0:T(8,128)S(1)} %get-tuple-element.27), channel_id=1, source_target_pairs={{0,6},{2,4},{4,2},{6,0},{8,14},{10,12},{12,10},{14,8},{1,7},{3,5},... | collective-permute-start | bytes 442376 | tf_op jit(solution)/shard_map/ppermute | solution.py:325
  27.1 12.2 %collective-permute-start.5 = (f32[72,512]{1,0:T(8,128)S(1)}, f32[72,512]{1,0:T(8,128)S(1)}, u32[]{:S(2)}, u32[]{:S(2)}) collective-permute-start(f32[72,512]{1,0:T(8,128)S(1)} %add.45), channel_id=1, source_target_pairs={{0,12},{2,14},{4,8},{6,10},{8,4},{10,6},{12,0},{14,2},{1,13},{3,15... | collective-permute-start | bytes 442376 | tf_op jit(solution)/shard_map/ppermute | solution.py:325
  32.8 9.7 %collective-permute-start.11 = (f32[72,512]{1,0:T(8,128)S(1)}, f32[72,512]{1,0:T(8,128)S(1)}, u32[]{:S(2)}, u32[]{:S(2)}) collective-permute-start(f32[72,512]{1,0:T(8,128)S(1)} %add.50), channel_id=1, source_target_pairs={{0,12},{2,14},{4,8},{6,10},{8,4},{10,6},{12,0},{14,2},{1,13},{3,15... | collective-permute-start | bytes 442376 | tf_op jit(solution)/shard_map/ppermute | solution.py:325
  39.3 6.8 %collective-permute-start.13 = (f32[64,512]{1,0:T(8,128)S(1)}, f32[64,512]{1,0:T(8,128)S(1)}, u32[]{:S(2)}, u32[]{:S(2)}) collective-permute-start(f32[64,512]{1,0:T(8,128)S(1)} %slice.65.refs_0_), channel_id=1, source_target_pairs={{0,4},{2,6},{4,0},{6,2},{8,12},{10,14},{12,8},{14,10},{1,5},{3,7},... | collective-permute-start | bytes 393224 | tf_op jit(solution)/shard_map/ppermute | solution.py:325
  39.4 5.8 %collective-permute-start.6 = (f32[8,512]{1,0:T(8,128)S(1)}, f32[8,512]{1,0:T(8,128)S(1)}, u32[]{:S(2)}, u32[]{:S(2)}) collective-permute-start(f32[8,512]{1,0:T(8,128)S(1)} %slice.59.own_ref), channel_id=1, source_target_pairs={{0,1},{1,0},{2,3},{3,2},{4,5},{5,4},{6,7},{7,6},{8,9},{9,8},{10,11... | collective-permute-start | bytes 49160 | tf_op jit(solution)/shard_map/ppermute | solution.py:367
  40.2 12.6 %collective-permute-start.12 = (f32[64,512]{1,0:T(8,128)S(1)}, f32[64,512]{1,0:T(8,128)S(1)}, u32[]{:S(2)}, u32[]{:S(2)}) collective-permute-start(f32[64,512]{1,0:T(8,128)S(1)} %slice.65.refs_0_), channel_id=1, source_target_pairs={{0,2},{2,0},{4,6},{6,4},{8,10},{10,8},{12,14},{14,12},{1,3},{3,1},... | collective-permute-start | bytes 393224 | tf_op jit(solution)/shard_map/ppermute | solution.py:325
  42.6 10.2 %collective-permute-start.15 = (f32[64,512]{1,0:T(8,128)S(1)}, f32[64,512]{1,0:T(8,128)S(1)}, u32[]{:S(2)}, u32[]{:S(2)}) collective-permute-start(f32[64,512]{1,0:T(8,128)S(1)} %slice.66.refs_4_), channel_id=1, source_target_pairs={{0,2},{2,0},{4,6},{6,4},{8,10},{10,8},{12,14},{14,12},{1,3},{3,1},... | collective-permute-start | bytes 393224 | tf_op jit(solution)/shard_map/ppermute | solution.py:325
  44.1 8.7 %collective-permute-start.16 = (f32[64,512]{1,0:T(8,128)S(1)}, f32[64,512]{1,0:T(8,128)S(1)}, u32[]{:S(2)}, u32[]{:S(2)}) collective-permute-start(f32[64,512]{1,0:T(8,128)S(1)} %slice.66.refs_4_), channel_id=1, source_target_pairs={{0,4},{2,6},{4,0},{6,2},{8,12},{10,14},{12,8},{14,10},{1,5},{3,7},... | collective-permute-start | bytes 393224 | tf_op jit(solution)/shard_map/ppermute | solution.py:325
  45.3 7.5 %collective-permute-start.17 = (f32[64,512]{1,0:T(8,128)S(1)}, f32[64,512]{1,0:T(8,128)S(1)}, u32[]{:S(2)}, u32[]{:S(2)}) collective-permute-start(f32[64,512]{1,0:T(8,128)S(1)} %slice.66.refs_4_), channel_id=1, source_target_pairs={{0,6},{2,4},{4,2},{6,0},{8,14},{10,12},{12,10},{14,8},{1,7},{3,5},... | collective-permute-start | bytes 393224 | tf_op jit(solution)/shard_map/ppermute | solution.py:325
  46.1 7.1 %collective-permute-start.14 = (f32[64,512]{1,0:T(8,128)S(1)}, f32[64,512]{1,0:T(8,128)S(1)}, u32[]{:S(2)}, u32[]{:S(2)}) collective-permute-start(f32[64,512]{1,0:T(8,128)S(1)} %collective-permute-done.13.refs_2_), channel_id=1, source_target_pairs={{0,2},{2,0},{4,6},{6,4},{8,10},{10,8},{12,14},{14,12},{1,3},{3,1},... | collective-permute-start | bytes 393224 | tf_op jit(solution)/shard_map/ppermute | solution.py:325

commit v6 on v5

--- a/solution.py
+++ b/solution.py
@@ -89,19 +89,19 @@
     gram = dot_nt(jnp.concatenate(parts, axis=0), lead)
     put_gram(halves_beside(gram[:edge]), keep_ref, edge)
     put_gram(halves_beside(gram[edge:]), send_ref, edge)
-    group = max(1, 256 // edge)
-    for first in range(0, tile_count, group):
-        for tile in range(first, first + group):
+    cuts = (0, tile_count // 2, tile_count)
+    for first, after in zip(cuts, cuts[1:]):
+        for tile in range(first, after):
             copies[tile].wait()
             value = held[tile] * wide_ref[tile : tile + 1, :]
             value_high, value_low = split(value)
             high[tile * edge : (tile + 1) * edge] = value_high
             low[tile * edge : (tile + 1) * edge] = value_low
-        deep = slice(first * edge, (first + group) * edge)
+        deep = slice(first * edge, after * edge)
         for piece in range(pieces):
             here = slice(piece * width, (piece + 1) * width)
             part = panel_product(lhs[:, deep], high[deep, here], low[deep, here], edge)
-            if first + group < tile_count:
+            if after < tile_count:
                 total_ref[:, here] = part if first == 0 else total_ref[:, here] + part
                 continue
             total = total_ref[:, here] + part if first else part

time: 55.4 us -> 54.9 us (level)
  transfers between devices with their start and end apart: 18 -> 18, of which waited for: 4 -> 4; matrix products, arithmetic and copies ran while one was open for 1% -> 1% of each run, Pallas kernels for 26% -> 25%
where the time goes in v6:
time: 54.9 us; the launch traced here: 54.7 us
  starting transfers between devices  30.6 us (56%)
  Pallas kernels  16.1 us (29%)
  waiting for transfers between devices  4.75 us (9%)
  local copies, waits for them, and re-layouts  1.83 us (3%)
  other arithmetic  1.18 us (2%)
    ppermute x14, starting transfers between devices, over_row(): return lax.ppermute(value, 'row', [(i, i ^ bit) for i in range(row_count)])  25.7 us
    pallas_call x1, Pallas kernels, per_device(): pl.pallas_call(functools.partial(own_kernel, row_count), out_shape=(sums(...  6.09 us
    pallas_call x1, Pallas kernels, per_device(): pl.pallas_call(functools.partial(factor_kernel, start), out_shape=jax.Sha...  5.12 us
    ppermute x14, waiting for transfers between devices, over_row(): return lax.ppermute(value, 'row', [(i, i ^ bit) for i in range(row_count)])  4.74 us
    ppermute x1, starting transfers between devices, per_device(): lead_other = lax.ppermute(lead, 'col', [(i, 1 - i) for i in range(PANELS)])  3.03 us
    pallas_call x1, Pallas kernels, per_device(): pl.pallas_call(functools.partial(pair_kernel, not swap), out_shape=(sums(...  2.73 us
    pallas_call x1, Pallas kernels, per_device(): pl.pallas_call(functools.partial(final_kernel, pieces, edge), out_shape=j...  1.93 us
    ppermute x1, starting transfers between devices, per_device(): lax.ppermute(own_gram, 'col', [(i, 1 - i) for i in range(PANELS)])  1.2 us
  transfers between devices with their start and end apart: 18, of which 4 were waited for; matrix products, arithmetic and copies ran while one was open for 1% of the time, Pallas kernels for 25%

profile of v6, /device:TPU:0, one launch (start us, length us, event | category | flops | bytes accessed | tf_op | source)
XLA Modules:
  0.0 54.7 jit_solution(2283748392373470734)
XLA Ops:
  0.0 0.7 %convert_element_type.5 = f32[16,32]{1,0:T(8,128)S(1)} convert(s32[16,32]{1,0:T(8,128)} %param.4) | non-fusion elementwise | flops 512 | bytes 4096 | tf_op jit(solution)/shard_map/convert_element_type | solution.py:278
  0.7 1.1 %slice.42 = f32[16,64,64]{2,1,0:T(8,128)S(1)} slice(f32[16,64,2048]{2,1,0:T(8,128)} %tiles_ref.1), slice={[0:16], [0:64], [0:64]} | slice | bytes 524288 | tf_op jit(solution)/shard_map/slice | solution.py:286
  1.8 0.3 lead_prep.1
  2.1 3.0 %collective-permute-start = (f32[64,1024]{1,0:T(8,128)S(1)}, f32[64,1024]{1,0:T(8,128)S(1)}, u32[]{:S(2)}, u32[]{:S(2)}) collective-permute-start(f32[64,1024]{1,0:T(8,128)S(1)} %get-tuple-element.17.lead_ref.own_ref), channel_id=1, source_target_pairs={{0,1},{1,0},{2,3},{3,2},{4,5},{5,4},{6,7},{7,6},{8,9},{9,8},{10,11... | collective-permute-start | bytes 786440 | tf_op jit(solution)/shard_map/ppermute | solution.py:290
  5.1 0.1 pad_add_fusion.info_ref
  5.2 0.0 copy-start
  5.2 0.7 %copy-done = s32[16,1]{0,1:T(1,128)S(1)} copy-done((s32[16,1]{0,1:T(1,128)S(1)}, s32[16,1]{0,1:T(1,128)}, u32[]{:S(2)}) %copy-start) | copy-done | bytes 88
  5.9 6.1 %panel_own.1 = (f32[4,72,512]{2,1,0:T(8,128)S(1)}, f32[4,72,512]{2,1,0:T(8,128)S(1)}, bf16[1024,2048]{1,0:T(8,128)(2,1)S(1)}, bf16[1024,2048]{1,0:T(8,128)(2,1)S(1)}, f32[1,1024]{1,0:T(1,128)S(1)}) custom-call(s32[4]{0:T(128)S(1)} %pad_add_fusion.info_ref, s32[1,16]{1,0:T(1,128)S(1)} %bitcast.26, f32[16,32]{1,0:T(8,128)S(1)} %get-tuple-element.16.mask_ref, ...), custom_call_target="tpu_custom_call" | custom-call | flops 1610612736 | bytes 8388608 | tf_op jit(solution)/shard_map/panel_own/pallas_call | solution.py:304
  12.0 0.0 collective-permute-done.lead_ref
  12.0 0.1 collective-permute-start.1
  12.1 2.7 %panel_pair.1 = (f32[4,72,512]{2,1,0:T(8,128)S(1)}, f32[4,72,512]{2,1,0:T(8,128)S(1)}) custom-call(s32[4]{0:T(128)S(1)} %pad_add_fusion.info_ref, f32[1,1024]{1,0:T(1,128)S(1)} %get-tuple-element.21.mine_ref, f32[64,1024]{1,0:T(8,128)S(1)} %collective-permute-done.lead_ref, f32[64,1024]{1,0:T(8,128)S(1)} %get-tuple-element.17.lead_ref.own_ref, ...), custom_call_target="tpu_custom_call" | custom-call | flops 1610612736 | bytes 8388608 | tf_op jit(solution)/shard_map/panel_pair/pallas_call | solution.py:352
  14.8 0.6 %collective-permute-start.7 = (f32[4,72,512]{2,1,0:T(8,128)S(1)}, f32[4,72,512]{2,1,0:T(8,128)S(1)}, u32[]{:S(2)}, u32[]{:S(2)}) collective-permute-start(f32[4,72,512]{2,1,0:T(8,128)S(1)} %get-tuple-element.26), channel_id=1, source_target_pairs={{0,16},{16,0},{1,17},{17,1},{2,18},{18,2},{3,19},{19,3},{4,20},{20... | collective-permute-start | bytes 1769480 | tf_op jit(solution)/shard_map/ppermute | solution.py:322
  15.4 0.0 collective-permute-done.1
  15.4 0.1 add.42
  15.5 1.6 %collective-permute-start.2 = (f32[72,512]{1,0:T(8,128)S(1)}, f32[72,512]{1,0:T(8,128)S(1)}, u32[]{:S(2)}, u32[]{:S(2)}) collective-permute-start(f32[72,512]{1,0:T(8,128)S(1)} %get-tuple-element.32), channel_id=1, source_target_pairs={{0,2},{2,0},{4,6},{6,4},{8,10},{10,8},{12,14},{14,12},{1,3},{3,1},... | collective-permute-start | bytes 442376 | tf_op jit(solution)/shard_map/ppermute | solution.py:325
  17.0 1.6 %collective-permute-start.3 = (f32[72,512]{1,0:T(8,128)S(1)}, f32[72,512]{1,0:T(8,128)S(1)}, u32[]{:S(2)}, u32[]{:S(2)}) collective-permute-start(f32[72,512]{1,0:T(8,128)S(1)} %get-tuple-element.31), channel_id=1, source_target_pairs={{0,4},{2,6},{4,0},{6,2},{8,12},{10,14},{12,8},{14,10},{1,5},{3,7},... | collective-permute-start | bytes 442376 | tf_op jit(solution)/shard_map/ppermute | solution.py:325
  18.6 0.4 collective-permute-start.4
  19.0 0.0 collective-permute-done.7
  19.1 0.1 add.47
  19.2 1.6 %collective-permute-start.8 = (f32[72,512]{1,0:T(8,128)S(1)}, f32[72,512]{1,0:T(8,128)S(1)}, u32[]{:S(2)}, u32[]{:S(2)}) collective-permute-start(f32[72,512]{1,0:T(8,128)S(1)} %get-tuple-element.29), channel_id=1, source_target_pairs={{0,2},{2,0},{4,6},{6,4},{8,10},{10,8},{12,14},{14,12},{1,3},{3,1},... | collective-permute-start | bytes 442376 | tf_op jit(solution)/shard_map/ppermute | solution.py:325
  20.7 1.6 %collective-permute-start.9 = (f32[72,512]{1,0:T(8,128)S(1)}, f32[72,512]{1,0:T(8,128)S(1)}, u32[]{:S(2)}, u32[]{:S(2)}) collective-permute-start(f32[72,512]{1,0:T(8,128)S(1)} %get-tuple-element.28), channel_id=1, source_target_pairs={{0,4},{2,6},{4,0},{6,2},{8,12},{10,14},{12,8},{14,10},{1,5},{3,7},... | collective-permute-start | bytes 442376 | tf_op jit(solution)/shard_map/ppermute | solution.py:325
  22.3 0.0 collective-permute-done.2
  22.3 2.1 %collective-permute-start.10 = (f32[72,512]{1,0:T(8,128)S(1)}, f32[72,512]{1,0:T(8,128)S(1)}, u32[]{:S(2)}, u32[]{:S(2)}) collective-permute-start(f32[72,512]{1,0:T(8,128)S(1)} %get-tuple-element.27), channel_id=1, source_target_pairs={{0,6},{2,4},{4,2},{6,0},{8,14},{10,12},{12,10},{14,8},{1,7},{3,5},... | collective-permute-start | bytes 442376 | tf_op jit(solution)/shard_map/ppermute | solution.py:325
  24.4 0.0 collective-permute-done.3
  24.4 2.2 %collective-permute-done.4 = f32[72,512]{1,0:T(8,128)S(1)} collective-permute-done((f32[72,512]{1,0:T(8,128)S(1)}, f32[72,512]{1,0:T(8,128)S(1)}, u32[]{:S(2)}, u32[]{:S(2)}) %collective-permute-start.4) | collective-permute-done | bytes 147488 | tf_op jit(solution)/shard_map/ppermute | solution.py:325
  26.7 3.9 %collective-permute-start.5 = (f32[72,512]{1,0:T(8,128)S(1)}, f32[72,512]{1,0:T(8,128)S(1)}, u32[]{:S(2)}, u32[]{:S(2)}) collective-permute-start(f32[72,512]{1,0:T(8,128)S(1)} %add.45), channel_id=1, source_target_pairs={{0,12},{2,14},{4,8},{6,10},{8,4},{10,6},{12,0},{14,2},{1,13},{3,15... | collective-permute-start | bytes 442376 | tf_op jit(solution)/shard_map/ppermute | solution.py:325
  30.6 0.0 collective-permute-done.8
  30.7 0.0 collective-permute-done.9
  30.7 1.7 %collective-permute-done.10 = f32[72,512]{1,0:T(8,128)S(1)} collective-permute-done((f32[72,512]{1,0:T(8,128)S(1)}, f32[72,512]{1,0:T(8,128)S(1)}, u32[]{:S(2)}, u32[]{:S(2)}) %collective-permute-start.10) | collective-permute-done | bytes 147488 | tf_op jit(solution)/shard_map/ppermute | solution.py:325
  32.4 6.5 %collective-permute-start.11 = (f32[72,512]{1,0:T(8,128)S(1)}, f32[72,512]{1,0:T(8,128)S(1)}, u32[]{:S(2)}, u32[]{:S(2)}) collective-permute-start(f32[72,512]{1,0:T(8,128)S(1)} %add.50), channel_id=1, source_target_pairs={{0,12},{2,14},{4,8},{6,10},{8,4},{10,6},{12,0},{14,2},{1,13},{3,15... | collective-permute-start | bytes 442376 | tf_op jit(solution)/shard_map/ppermute | solution.py:325
  38.9 0.0 collective-permute-done.5
  38.9 0.1 collective-permute-start.13
  39.0 1.2 %collective-permute-start.6 = (f32[8,512]{1,0:T(8,128)S(1)}, f32[8,512]{1,0:T(8,128)S(1)}, u32[]{:S(2)}, u32[]{:S(2)}) collective-permute-start(f32[8,512]{1,0:T(8,128)S(1)} %slice.59.own_ref), channel_id=1, source_target_pairs={{0,1},{1,0},{2,3},{3,2},{4,5},{5,4},{6,7},{7,6},{8,9},{9,8},{10,11... | collective-permute-start | bytes 49160 | tf_op jit(solution)/shard_map/ppermute | solution.py:367
  40.2 1.5 %collective-permute-start.12 = (f32[64,512]{1,0:T(8,128)S(1)}, f32[64,512]{1,0:T(8,128)S(1)}, u32[]{:S(2)}, u32[]{:S(2)}) collective-permute-start(f32[64,512]{1,0:T(8,128)S(1)} %slice.65.refs_0_), channel_id=1, source_target_pairs={{0,2},{2,0},{4,6},{6,4},{8,10},{10,8},{12,14},{14,12},{1,3},{3,1},... | collective-permute-start | bytes 393224 | tf_op jit(solution)/shard_map/ppermute | solution.py:325
  41.7 0.4 collective-permute-done.11
  42.1 1.6 %collective-permute-start.15 = (f32[64,512]{1,0:T(8,128)S(1)}, f32[64,512]{1,0:T(8,128)S(1)}, u32[]{:S(2)}, u32[]{:S(2)}) collective-permute-start(f32[64,512]{1,0:T(8,128)S(1)} %slice.66.refs_4_), channel_id=1, source_target_pairs={{0,2},{2,0},{4,6},{6,4},{8,10},{10,8},{12,14},{14,12},{1,3},{3,1},... | collective-permute-start | bytes 393224 | tf_op jit(solution)/shard_map/ppermute | solution.py:325
  43.7 1.1 %collective-permute-start.16 = (f32[64,512]{1,0:T(8,128)S(1)}, f32[64,512]{1,0:T(8,128)S(1)}, u32[]{:S(2)}, u32[]{:S(2)}) collective-permute-start(f32[64,512]{1,0:T(8,128)S(1)} %slice.66.refs_4_), channel_id=1, source_target_pairs={{0,4},{2,6},{4,0},{6,2},{8,12},{10,14},{12,8},{14,10},{1,5},{3,7},... | collective-permute-start | bytes 393224 | tf_op jit(solution)/shard_map/ppermute | solution.py:325
  44.8 0.0 collective-permute-done.6.other_ref
  44.8 0.9 %collective-permute-start.17 = (f32[64,512]{1,0:T(8,128)S(1)}, f32[64,512]{1,0:T(8,128)S(1)}, u32[]{:S(2)}, u32[]{:S(2)}) collective-permute-start(f32[64,512]{1,0:T(8,128)S(1)} %slice.66.refs_4_), channel_id=1, source_target_pairs={{0,6},{2,4},{4,2},{6,0},{8,14},{10,12},{12,10},{14,8},{1,7},{3,5},... | collective-permute-start | bytes 393224 | tf_op jit(solution)/shard_map/ppermute | solution.py:325
  45.7 0.0 collective-permute-done.13.refs_2_
  45.7 1.5 %collective-permute-start.14 = (f32[64,512]{1,0:T(8,128)S(1)}, f32[64,512]{1,0:T(8,128)S(1)}, u32[]{:S(2)}, u32[]{:S(2)}) collective-permute-start(f32[64,512]{1,0:T(8,128)S(1)} %collective-permute-done.13.refs_2_), channel_id=1, source_target_pairs={{0,2},{2,0},{4,6},{6,4},{8,10},{10,8},{12,14},{14,12},{1,3},{3,1},... | collective-permute-start | bytes 393224 | tf_op jit(solution)/shard_map/ppermute | solution.py:325
  47.2 5.1 %gram_factor.1.inverse_ref = f32[128,128]{1,0:T(8,128)S(1)} custom-call(s32[4]{0:T(128)S(1)} %pad_add_fusion.info_ref, f32[8,512]{1,0:T(8,128)S(1)} %slice.59.own_ref, f32[8,512]{1,0:T(8,128)S(1)} %collective-permute-done.6.other_ref, f32[8,512]{1,0:T(8,128)S(1)} %slice.64.pair_ref), custom_call_target="tpu_custom_call" | custom-call | tf_op jit(solution)/shard_map/gram_factor/pallas_call | solution.py:370
  52.3 0.0 collective-permute-done.12.refs_1_
  52.3 0.0 collective-permute-done.15.refs_5_
  52.3 0.0 collective-permute-done.16.refs_6_
  52.3 0.0 collective-permute-done.17.refs_7_
  52.4 0.4 collective-permute-done.14.refs_3_
  52.8 1.9 %apply_inverse.1 = f32[1,128,2048]{2,1,0:T(8,128)} custom-call(s32[4]{0:T(128)S(1)} %pad_add_fusion.info_ref, f32[128,128]{1,0:T(8,128)S(1)} %gram_factor.1.inverse_ref, f32[64,512]{1,0:T(8,128)S(1)} %slice.65.refs_0_, f32[64,512]{1,0:T(8,128)S(1)} %collective-permute-done.12.refs_1_, f32[64,512]{1,0:T(8,128)S(1)} %collective-permute-done.13.refs_2_, ...), custom_call_target="tpu_custom_call" | custom-call | tf_op jit(solution)/shard_map/apply_inverse/pallas_call | solution.py:379
  (16 shorter events, 0.3 us)
Async XLA Ops:
  2.1 9.9 %collective-permute-start = (f32[64,1024]{1,0:T(8,128)S(1)}, f32[64,1024]{1,0:T(8,128)S(1)}, u32[]{:S(2)}, u32[]{:S(2)}) collective-permute-start(f32[64,1024]{1,0:T(8,128)S(1)} %get-tuple-element.17.lead_ref.own_ref), channel_id=1, source_target_pairs={{0,1},{1,0},{2,3},{3,2},{4,5},{5,4},{6,7},{7,6},{8,9},{9,8},{10,11... | collective-permute-start | bytes 786440 | tf_op jit(solution)/shard_map/ppermute | solution.py:290
  5.2 0.7 %copy-start = (s32[16,1]{0,1:T(1,128)S(1)}, s32[16,1]{0,1:T(1,128)}, u32[]{:S(2)}) copy-start(s32[16,1]{0,1:T(1,128)} %param.5) | copy-start | bytes 196
  12.0 3.4 %collective-permute-start.1 = (f32[4,72,512]{2,1,0:T(8,128)S(1)}, f32[4,72,512]{2,1,0:T(8,128)S(1)}, u32[]{:S(2)}, u32[]{:S(2)}) collective-permute-start(f32[4,72,512]{2,1,0:T(8,128)S(1)} %get-tuple-element.20), channel_id=1, source_target_pairs={{0,16},{16,0},{1,17},{17,1},{2,18},{18,2},{3,19},{19,3},{4,20},{20... | collective-permute-start | bytes 1769480 | tf_op jit(solution)/shard_map/ppermute | solution.py:322
  14.8 4.3 %collective-permute-start.7 = (f32[4,72,512]{2,1,0:T(8,128)S(1)}, f32[4,72,512]{2,1,0:T(8,128)S(1)}, u32[]{:S(2)}, u32[]{:S(2)}) collective-permute-start(f32[4,72,512]{2,1,0:T(8,128)S(1)} %get-tuple-element.26), channel_id=1, source_target_pairs={{0,16},{16,0},{1,17},{17,1},{2,18},{18,2},{3,19},{19,3},{4,20},{20... | collective-permute-start | bytes 1769480 | tf_op jit(solution)/shard_map/ppermute | solution.py:322
  15.5 6.8 %collective-permute-start.2 = (f32[72,512]{1,0:T(8,128)S(1)}, f32[72,512]{1,0:T(8,128)S(1)}, u32[]{:S(2)}, u32[]{:S(2)}) collective-permute-start(f32[72,512]{1,0:T(8,128)S(1)} %get-tuple-element.32), channel_id=1, source_target_pairs={{0,2},{2,0},{4,6},{6,4},{8,10},{10,8},{12,14},{14,12},{1,3},{3,1},... | collective-permute-start | bytes 442376 | tf_op jit(solution)/shard_map/ppermute | solution.py:325
  17.0 7.4 %collective-permute-start.3 = (f32[72,512]{1,0:T(8,128)S(1)}, f32[72,512]{1,0:T(8,128)S(1)}, u32[]{:S(2)}, u32[]{:S(2)}) collective-permute-start(f32[72,512]{1,0:T(8,128)S(1)} %get-tuple-element.31), channel_id=1, source_target_pairs={{0,4},{2,6},{4,0},{6,2},{8,12},{10,14},{12,8},{14,10},{1,5},{3,7},... | collective-permute-start | bytes 442376 | tf_op jit(solution)/shard_map/ppermute | solution.py:325
  18.6 8.0 %collective-permute-start.4 = (f32[72,512]{1,0:T(8,128)S(1)}, f32[72,512]{1,0:T(8,128)S(1)}, u32[]{:S(2)}, u32[]{:S(2)}) collective-permute-start(f32[72,512]{1,0:T(8,128)S(1)} %get-tuple-element.30), channel_id=1, source_target_pairs={{0,6},{2,4},{4,2},{6,0},{8,14},{10,12},{12,10},{14,8},{1,7},{3,5},... | collective-permute-start | bytes 442376 | tf_op jit(solution)/shard_map/ppermute | solution.py:325
  19.2 11.4 %collective-permute-start.8 = (f32[72,512]{1,0:T(8,128)S(1)}, f32[72,512]{1,0:T(8,128)S(1)}, u32[]{:S(2)}, u32[]{:S(2)}) collective-permute-start(f32[72,512]{1,0:T(8,128)S(1)} %get-tuple-element.29), channel_id=1, source_target_pairs={{0,2},{2,0},{4,6},{6,4},{8,10},{10,8},{12,14},{14,12},{1,3},{3,1},... | collective-permute-start | bytes 442376 | tf_op jit(solution)/shard_map/ppermute | solution.py:325
  20.7 9.9 %collective-permute-start.9 = (f32[72,512]{1,0:T(8,128)S(1)}, f32[72,512]{1,0:T(8,128)S(1)}, u32[]{:S(2)}, u32[]{:S(2)}) collective-permute-start(f32[72,512]{1,0:T(8,128)S(1)} %get-tuple-element.28), channel_id=1, source_target_pairs={{0,4},{2,6},{4,0},{6,2},{8,12},{10,14},{12,8},{14,10},{1,5},{3,7},... | collective-permute-start | bytes 442376 | tf_op jit(solution)/shard_map/ppermute | solution.py:325
  22.3 10.0 %collective-permute-start.10 = (f32[72,512]{1,0:T(8,128)S(1)}, f32[72,512]{1,0:T(8,128)S(1)}, u32[]{:S(2)}, u32[]{:S(2)}) collective-permute-start(f32[72,512]{1,0:T(8,128)S(1)} %get-tuple-element.27), channel_id=1, source_target_pairs={{0,6},{2,4},{4,2},{6,0},{8,14},{10,12},{12,10},{14,8},{1,7},{3,5},... | collective-permute-start | bytes 442376 | tf_op jit(solution)/shard_map/ppermute | solution.py:325
  26.7 12.2 %collective-permute-start.5 = (f32[72,512]{1,0:T(8,128)S(1)}, f32[72,512]{1,0:T(8,128)S(1)}, u32[]{:S(2)}, u32[]{:S(2)}) collective-permute-start(f32[72,512]{1,0:T(8,128)S(1)} %add.45), channel_id=1, source_target_pairs={{0,12},{2,14},{4,8},{6,10},{8,4},{10,6},{12,0},{14,2},{1,13},{3,15... | collective-permute-start | bytes 442376 | tf_op jit(solution)/shard_map/ppermute | solution.py:325
  32.4 9.7 %collective-permute-start.11 = (f32[72,512]{1,0:T(8,128)S(1)}, f32[72,512]{1,0:T(8,128)S(1)}, u32[]{:S(2)}, u32[]{:S(2)}) collective-permute-start(f32[72,512]{1,0:T(8,128)S(1)} %add.50), channel_id=1, source_target_pairs={{0,12},{2,14},{4,8},{6,10},{8,4},{10,6},{12,0},{14,2},{1,13},{3,15... | collective-permute-start | bytes 442376 | tf_op jit(solution)/shard_map/ppermute | solution.py:325
  38.9 6.8 %collective-permute-start.13 = (f32[64,512]{1,0:T(8,128)S(1)}, f32[64,512]{1,0:T(8,128)S(1)}, u32[]{:S(2)}, u32[]{:S(2)}) collective-permute-start(f32[64,512]{1,0:T(8,128)S(1)} %slice.65.refs_0_), channel_id=1, source_target_pairs={{0,4},{2,6},{4,0},{6,2},{8,12},{10,14},{12,8},{14,10},{1,5},{3,7},... | collective-permute-start | bytes 393224 | tf_op jit(solution)/shard_map/ppermute | solution.py:325
  39.0 5.8 %collective-permute-start.6 = (f32[8,512]{1,0:T(8,128)S(1)}, f32[8,512]{1,0:T(8,128)S(1)}, u32[]{:S(2)}, u32[]{:S(2)}) collective-permute-start(f32[8,512]{1,0:T(8,128)S(1)} %slice.59.own_ref), channel_id=1, source_target_pairs={{0,1},{1,0},{2,3},{3,2},{4,5},{5,4},{6,7},{7,6},{8,9},{9,8},{10,11... | collective-permute-start | bytes 49160 | tf_op jit(solution)/shard_map/ppermute | solution.py:367
  40.2 12.1 %collective-permute-start.12 = (f32[64,512]{1,0:T(8,128)S(1)}, f32[64,512]{1,0:T(8,128)S(1)}, u32[]{:S(2)}, u32[]{:S(2)}) collective-permute-start(f32[64,512]{1,0:T(8,128)S(1)} %slice.65.refs_0_), channel_id=1, source_target_pairs={{0,2},{2,0},{4,6},{6,4},{8,10},{10,8},{12,14},{14,12},{1,3},{3,1},... | collective-permute-start | bytes 393224 | tf_op jit(solution)/shard_map/ppermute | solution.py:325
  42.1 10.2 %collective-permute-start.15 = (f32[64,512]{1,0:T(8,128)S(1)}, f32[64,512]{1,0:T(8,128)S(1)}, u32[]{:S(2)}, u32[]{:S(2)}) collective-permute-start(f32[64,512]{1,0:T(8,128)S(1)} %slice.66.refs_4_), channel_id=1, source_target_pairs={{0,2},{2,0},{4,6},{6,4},{8,10},{10,8},{12,14},{14,12},{1,3},{3,1},... | collective-permute-start | bytes 393224 | tf_op jit(solution)/shard_map/ppermute | solution.py:325
  43.7 8.7 %collective-permute-start.16 = (f32[64,512]{1,0:T(8,128)S(1)}, f32[64,512]{1,0:T(8,128)S(1)}, u32[]{:S(2)}, u32[]{:S(2)}) collective-permute-start(f32[64,512]{1,0:T(8,128)S(1)} %slice.66.refs_4_), channel_id=1, source_target_pairs={{0,4},{2,6},{4,0},{6,2},{8,12},{10,14},{12,8},{14,10},{1,5},{3,7},... | collective-permute-start | bytes 393224 | tf_op jit(solution)/shard_map/ppermute | solution.py:325
  44.8 7.5 %collective-permute-start.17 = (f32[64,512]{1,0:T(8,128)S(1)}, f32[64,512]{1,0:T(8,128)S(1)}, u32[]{:S(2)}, u32[]{:S(2)}) collective-permute-start(f32[64,512]{1,0:T(8,128)S(1)} %slice.66.refs_4_), channel_id=1, source_target_pairs={{0,6},{2,4},{4,2},{6,0},{8,14},{10,12},{12,10},{14,8},{1,7},{3,5},... | collective-permute-start | bytes 393224 | tf_op jit(solution)/shard_map/ppermute | solution.py:325
  45.7 7.1 %collective-permute-start.14 = (f32[64,512]{1,0:T(8,128)S(1)}, f32[64,512]{1,0:T(8,128)S(1)}, u32[]{:S(2)}, u32[]{:S(2)}) collective-permute-start(f32[64,512]{1,0:T(8,128)S(1)} %collective-permute-done.13.refs_2_), channel_id=1, source_target_pairs={{0,2},{2,0},{4,6},{6,4},{8,10},{10,8},{12,14},{14,12},{1,3},{3,1},... | collective-permute-start | bytes 393224 | tf_op jit(solution)/shard_map/ppermute | solution.py:325

commit v7 on v6

--- a/solution.py
+++ b/solution.py
@@ -225,16 +225,15 @@
     left, right = inverse[:, :edge], inverse[:, edge:]
     inverse = jnp.concatenate([jnp.where(first, left, right), jnp.where(first, right, left)], axis=1)
     inverse_high, inverse_low = split(inverse)
-    both = jnp.concatenate([inverse_high, inverse_low], axis=0)
+    three = jnp.concatenate([inverse_high, inverse_high, inverse_low], axis=1)
     row = lax.broadcasted_iota(jnp.int32, (2 * edge, width), 0)
     lane = lax.broadcasted_iota(jnp.int32, (2 * edge, width), 1)
     copies = []
     for near in range(pieces):
         part = jnp.concatenate([own_refs[near][:edge], other_refs[near][:edge]], axis=0)
         part_high, part_low = split(part)
-        product = jnp.dot(both, part_high, preferred_element_type=F32)
-        small = jnp.dot(inverse_high, part_low, preferred_element_type=F32)
-        product = product[: 2 * edge] + (product[2 * edge :] + small)
+        stacked = jnp.concatenate([part_high, part_low, part_high], axis=0)
+        product = jnp.dot(three, stacked, preferred_element_type=F32)
         place = jnp.bitwise_xor(info_ref[0], near)
         place_lane = lane + place * width
         early = (place_lane < edge) & (place_lane + info_ref[3] * edge < row)

time: 54.9 us -> 54.8 us (level)
  transfers between devices with their start and end apart: 18 -> 18, of which waited for: 4 -> 4; matrix products, arithmetic and copies ran while one was open for 1% -> 1% of each run, Pallas kernels for 25% -> 26%
where the time goes in v7:
time: 54.8 us; the launch traced here: 54.6 us
  starting transfers between devices  30.6 us (56%)
  Pallas kernels  16 us (29%)
  waiting for transfers between devices  4.75 us (9%)
  local copies, waits for them, and re-layouts  1.83 us (3%)
  other arithmetic  1.18 us (2%)
    ppermute x14, starting transfers between devices, over_row(): return lax.ppermute(value, 'row', [(i, i ^ bit) for i in range(row_count)])  25.7 us
    pallas_call x1, Pallas kernels, per_device(): pl.pallas_call(functools.partial(own_kernel, row_count), out_shape=(sums(...  6.09 us
    pallas_call x1, Pallas kernels, per_device(): pl.pallas_call(functools.partial(factor_kernel, start), out_shape=jax.Sha...  5.12 us
    ppermute x14, waiting for transfers between devices, over_row(): return lax.ppermute(value, 'row', [(i, i ^ bit) for i in range(row_count)])  4.74 us
    ppermute x1, starting transfers between devices, per_device(): lead_other = lax.ppermute(lead, 'col', [(i, 1 - i) for i in range(PANELS)])  3.03 us
    pallas_call x1, Pallas kernels, per_device(): pl.pallas_call(functools.partial(pair_kernel, not swap), out_shape=(sums(...  2.73 us
    pallas_call x1, Pallas kernels, per_device(): pl.pallas_call(functools.partial(final_kernel, pieces, edge), out_shape=j...  1.83 us
    ppermute x1, starting transfers between devices, per_device(): lax.ppermute(own_gram, 'col', [(i, 1 - i) for i in range(PANELS)])  1.2 us
  transfers between devices with their start and end apart: 18, of which 4 were waited for; matrix products, arithmetic and copies ran while one was open for 1% of the time, Pallas kernels for 26%

profile of v7, /device:TPU:0, one launch (start us, length us, event | category | flops | bytes accessed | tf_op | source)
XLA Modules:
  0.0 54.6 jit_solution(6261039307755901138)
XLA Ops:
  0.0 0.7 %convert_element_type.5 = f32[16,32]{1,0:T(8,128)S(1)} convert(s32[16,32]{1,0:T(8,128)} %param.4) | non-fusion elementwise | flops 512 | bytes 4096 | tf_op jit(solution)/shard_map/convert_element_type | solution.py:277
  0.7 1.1 %slice.42 = f32[16,64,64]{2,1,0:T(8,128)S(1)} slice(f32[16,64,2048]{2,1,0:T(8,128)} %tiles_ref.1), slice={[0:16], [0:64], [0:64]} | slice | bytes 524288 | tf_op jit(solution)/shard_map/slice | solution.py:285
  1.8 0.3 lead_prep.1
  2.1 3.0 %collective-permute-start = (f32[64,1024]{1,0:T(8,128)S(1)}, f32[64,1024]{1,0:T(8,128)S(1)}, u32[]{:S(2)}, u32[]{:S(2)}) collective-permute-start(f32[64,1024]{1,0:T(8,128)S(1)} %get-tuple-element.17.lead_ref.own_ref), channel_id=1, source_target_pairs={{0,1},{1,0},{2,3},{3,2},{4,5},{5,4},{6,7},{7,6},{8,9},{9,8},{10,11... | collective-permute-start | bytes 786440 | tf_op jit(solution)/shard_map/ppermute | solution.py:289
  5.1 0.1 pad_add_fusion.info_ref
  5.2 0.0 copy-start
  5.2 0.7 %copy-done = s32[16,1]{0,1:T(1,128)S(1)} copy-done((s32[16,1]{0,1:T(1,128)S(1)}, s32[16,1]{0,1:T(1,128)}, u32[]{:S(2)}) %copy-start) | copy-done | bytes 88
  5.9 6.1 %panel_own.1 = (f32[4,72,512]{2,1,0:T(8,128)S(1)}, f32[4,72,512]{2,1,0:T(8,128)S(1)}, bf16[1024,2048]{1,0:T(8,128)(2,1)S(1)}, bf16[1024,2048]{1,0:T(8,128)(2,1)S(1)}, f32[1,1024]{1,0:T(1,128)S(1)}) custom-call(s32[4]{0:T(128)S(1)} %pad_add_fusion.info_ref, s32[1,16]{1,0:T(1,128)S(1)} %bitcast.26, f32[16,32]{1,0:T(8,128)S(1)} %get-tuple-element.16.mask_ref, ...), custom_call_target="tpu_custom_call" | custom-call | flops 1610612736 | bytes 8388608 | tf_op jit(solution)/shard_map/panel_own/pallas_call | solution.py:303
  12.0 0.0 collective-permute-done.lead_ref
  12.0 0.1 collective-permute-start.1
  12.1 2.7 %panel_pair.1 = (f32[4,72,512]{2,1,0:T(8,128)S(1)}, f32[4,72,512]{2,1,0:T(8,128)S(1)}) custom-call(s32[4]{0:T(128)S(1)} %pad_add_fusion.info_ref, f32[1,1024]{1,0:T(1,128)S(1)} %get-tuple-element.21.mine_ref, f32[64,1024]{1,0:T(8,128)S(1)} %collective-permute-done.lead_ref, f32[64,1024]{1,0:T(8,128)S(1)} %get-tuple-element.17.lead_ref.own_ref, ...), custom_call_target="tpu_custom_call" | custom-call | flops 1610612736 | bytes 8388608 | tf_op jit(solution)/shard_map/panel_pair/pallas_call | solution.py:351
  14.8 0.6 %collective-permute-start.7 = (f32[4,72,512]{2,1,0:T(8,128)S(1)}, f32[4,72,512]{2,1,0:T(8,128)S(1)}, u32[]{:S(2)}, u32[]{:S(2)}) collective-permute-start(f32[4,72,512]{2,1,0:T(8,128)S(1)} %get-tuple-element.26), channel_id=1, source_target_pairs={{0,16},{16,0},{1,17},{17,1},{2,18},{18,2},{3,19},{19,3},{4,20},{20... | collective-permute-start | bytes 1769480 | tf_op jit(solution)/shard_map/ppermute | solution.py:321
  15.4 0.0 collective-permute-done.1
  15.4 0.1 add.42
  15.5 1.6 %collective-permute-start.2 = (f32[72,512]{1,0:T(8,128)S(1)}, f32[72,512]{1,0:T(8,128)S(1)}, u32[]{:S(2)}, u32[]{:S(2)}) collective-permute-start(f32[72,512]{1,0:T(8,128)S(1)} %get-tuple-element.32), channel_id=1, source_target_pairs={{0,2},{2,0},{4,6},{6,4},{8,10},{10,8},{12,14},{14,12},{1,3},{3,1},... | collective-permute-start | bytes 442376 | tf_op jit(solution)/shard_map/ppermute | solution.py:324
  17.0 1.6 %collective-permute-start.3 = (f32[72,512]{1,0:T(8,128)S(1)}, f32[72,512]{1,0:T(8,128)S(1)}, u32[]{:S(2)}, u32[]{:S(2)}) collective-permute-start(f32[72,512]{1,0:T(8,128)S(1)} %get-tuple-element.31), channel_id=1, source_target_pairs={{0,4},{2,6},{4,0},{6,2},{8,12},{10,14},{12,8},{14,10},{1,5},{3,7},... | collective-permute-start | bytes 442376 | tf_op jit(solution)/shard_map/ppermute | solution.py:324
  18.6 0.4 collective-permute-start.4
  19.0 0.0 collective-permute-done.7
  19.1 0.1 add.47
  19.2 1.6 %collective-permute-start.8 = (f32[72,512]{1,0:T(8,128)S(1)}, f32[72,512]{1,0:T(8,128)S(1)}, u32[]{:S(2)}, u32[]{:S(2)}) collective-permute-start(f32[72,512]{1,0:T(8,128)S(1)} %get-tuple-element.29), channel_id=1, source_target_pairs={{0,2},{2,0},{4,6},{6,4},{8,10},{10,8},{12,14},{14,12},{1,3},{3,1},... | collective-permute-start | bytes 442376 | tf_op jit(solution)/shard_map/ppermute | solution.py:324
  20.7 1.6 %collective-permute-start.9 = (f32[72,512]{1,0:T(8,128)S(1)}, f32[72,512]{1,0:T(8,128)S(1)}, u32[]{:S(2)}, u32[]{:S(2)}) collective-permute-start(f32[72,512]{1,0:T(8,128)S(1)} %get-tuple-element.28), channel_id=1, source_target_pairs={{0,4},{2,6},{4,0},{6,2},{8,12},{10,14},{12,8},{14,10},{1,5},{3,7},... | collective-permute-start | bytes 442376 | tf_op jit(solution)/shard_map/ppermute | solution.py:324
  22.3 0.0 collective-permute-done.2
  22.3 2.1 %collective-permute-start.10 = (f32[72,512]{1,0:T(8,128)S(1)}, f32[72,512]{1,0:T(8,128)S(1)}, u32[]{:S(2)}, u32[]{:S(2)}) collective-permute-start(f32[72,512]{1,0:T(8,128)S(1)} %get-tuple-element.27), channel_id=1, source_target_pairs={{0,6},{2,4},{4,2},{6,0},{8,14},{10,12},{12,10},{14,8},{1,7},{3,5},... | collective-permute-start | bytes 442376 | tf_op jit(solution)/shard_map/ppermute | solution.py:324
  24.4 0.0 collective-permute-done.3
  24.4 2.2 %collective-permute-done.4 = f32[72,512]{1,0:T(8,128)S(1)} collective-permute-done((f32[72,512]{1,0:T(8,128)S(1)}, f32[72,512]{1,0:T(8,128)S(1)}, u32[]{:S(2)}, u32[]{:S(2)}) %collective-permute-start.4) | collective-permute-done | bytes 147488 | tf_op jit(solution)/shard_map/ppermute | solution.py:324
  26.7 3.9 %collective-permute-start.5 = (f32[72,512]{1,0:T(8,128)S(1)}, f32[72,512]{1,0:T(8,128)S(1)}, u32[]{:S(2)}, u32[]{:S(2)}) collective-permute-start(f32[72,512]{1,0:T(8,128)S(1)} %add.45), channel_id=1, source_target_pairs={{0,12},{2,14},{4,8},{6,10},{8,4},{10,6},{12,0},{14,2},{1,13},{3,15... | collective-permute-start | bytes 442376 | tf_op jit(solution)/shard_map/ppermute | solution.py:324
  30.6 0.0 collective-permute-done.8
  30.7 0.0 collective-permute-done.9
  30.7 1.7 %collective-permute-done.10 = f32[72,512]{1,0:T(8,128)S(1)} collective-permute-done((f32[72,512]{1,0:T(8,128)S(1)}, f32[72,512]{1,0:T(8,128)S(1)}, u32[]{:S(2)}, u32[]{:S(2)}) %collective-permute-start.10) | collective-permute-done | bytes 147488 | tf_op jit(solution)/shard_map/ppermute | solution.py:324
  32.4 6.5 %collective-permute-start.11 = (f32[72,512]{1,0:T(8,128)S(1)}, f32[72,512]{1,0:T(8,128)S(1)}, u32[]{:S(2)}, u32[]{:S(2)}) collective-permute-start(f32[72,512]{1,0:T(8,128)S(1)} %add.50), channel_id=1, source_target_pairs={{0,12},{2,14},{4,8},{6,10},{8,4},{10,6},{12,0},{14,2},{1,13},{3,15... | collective-permute-start | bytes 442376 | tf_op jit(solution)/shard_map/ppermute | solution.py:324
  38.9 0.0 collective-permute-done.5
  38.9 0.1 collective-permute-start.13
  39.0 1.2 %collective-permute-start.6 = (f32[8,512]{1,0:T(8,128)S(1)}, f32[8,512]{1,0:T(8,128)S(1)}, u32[]{:S(2)}, u32[]{:S(2)}) collective-permute-start(f32[8,512]{1,0:T(8,128)S(1)} %slice.59.own_ref), channel_id=1, source_target_pairs={{0,1},{1,0},{2,3},{3,2},{4,5},{5,4},{6,7},{7,6},{8,9},{9,8},{10,11... | collective-permute-start | bytes 49160 | tf_op jit(solution)/shard_map/ppermute | solution.py:366
  40.2 1.5 %collective-permute-start.12 = (f32[64,512]{1,0:T(8,128)S(1)}, f32[64,512]{1,0:T(8,128)S(1)}, u32[]{:S(2)}, u32[]{:S(2)}) collective-permute-start(f32[64,512]{1,0:T(8,128)S(1)} %slice.65.refs_0_), channel_id=1, source_target_pairs={{0,2},{2,0},{4,6},{6,4},{8,10},{10,8},{12,14},{14,12},{1,3},{3,1},... | collective-permute-start | bytes 393224 | tf_op jit(solution)/shard_map/ppermute | solution.py:324
  41.7 0.4 collective-permute-done.11
  42.1 1.6 %collective-permute-start.15 = (f32[64,512]{1,0:T(8,128)S(1)}, f32[64,512]{1,0:T(8,128)S(1)}, u32[]{:S(2)}, u32[]{:S(2)}) collective-permute-start(f32[64,512]{1,0:T(8,128)S(1)} %slice.66.refs_4_), channel_id=1, source_target_pairs={{0,2},{2,0},{4,6},{6,4},{8,10},{10,8},{12,14},{14,12},{1,3},{3,1},... | collective-permute-start | bytes 393224 | tf_op jit(solution)/shard_map/ppermute | solution.py:324
  43.7 1.1 %collective-permute-start.16 = (f32[64,512]{1,0:T(8,128)S(1)}, f32[64,512]{1,0:T(8,128)S(1)}, u32[]{:S(2)}, u32[]{:S(2)}) collective-permute-start(f32[64,512]{1,0:T(8,128)S(1)} %slice.66.refs_4_), channel_id=1, source_target_pairs={{0,4},{2,6},{4,0},{6,2},{8,12},{10,14},{12,8},{14,10},{1,5},{3,7},... | collective-permute-start | bytes 393224 | tf_op jit(solution)/shard_map/ppermute | solution.py:324
  44.8 0.0 collective-permute-done.6.other_ref
  44.8 0.9 %collective-permute-start.17 = (f32[64,512]{1,0:T(8,128)S(1)}, f32[64,512]{1,0:T(8,128)S(1)}, u32[]{:S(2)}, u32[]{:S(2)}) collective-permute-start(f32[64,512]{1,0:T(8,128)S(1)} %slice.66.refs_4_), channel_id=1, source_target_pairs={{0,6},{2,4},{4,2},{6,0},{8,14},{10,12},{12,10},{14,8},{1,7},{3,5},... | collective-permute-start | bytes 393224 | tf_op jit(solution)/shard_map/ppermute | solution.py:324
  45.7 0.0 collective-permute-done.13.refs_2_
  45.7 1.5 %collective-permute-start.14 = (f32[64,512]{1,0:T(8,128)S(1)}, f32[64,512]{1,0:T(8,128)S(1)}, u32[]{:S(2)}, u32[]{:S(2)}) collective-permute-start(f32[64,512]{1,0:T(8,128)S(1)} %collective-permute-done.13.refs_2_), channel_id=1, source_target_pairs={{0,2},{2,0},{4,6},{6,4},{8,10},{10,8},{12,14},{14,12},{1,3},{3,1},... | collective-permute-start | bytes 393224 | tf_op jit(solution)/shard_map/ppermute | solution.py:324
  47.2 5.1 %gram_factor.1.inverse_ref = f32[128,128]{1,0:T(8,128)S(1)} custom-call(s32[4]{0:T(128)S(1)} %pad_add_fusion.info_ref, f32[8,512]{1,0:T(8,128)S(1)} %slice.59.own_ref, f32[8,512]{1,0:T(8,128)S(1)} %collective-permute-done.6.other_ref, f32[8,512]{1,0:T(8,128)S(1)} %slice.64.pair_ref), custom_call_target="tpu_custom_call" | custom-call | tf_op jit(solution)/shard_map/gram_factor/pallas_call | solution.py:369
  52.3 0.0 collective-permute-done.12.refs_1_
  52.3 0.0 collective-permute-done.15.refs_5_
  52.3 0.0 collective-permute-done.16.refs_6_
  52.3 0.0 collective-permute-done.17.refs_7_
  52.4 0.4 collective-permute-done.14.refs_3_
  52.8 1.8 %apply_inverse.1 = f32[1,128,2048]{2,1,0:T(8,128)} custom-call(s32[4]{0:T(128)S(1)} %pad_add_fusion.info_ref, f32[128,128]{1,0:T(8,128)S(1)} %gram_factor.1.inverse_ref, f32[64,512]{1,0:T(8,128)S(1)} %slice.65.refs_0_, f32[64,512]{1,0:T(8,128)S(1)} %collective-permute-done.12.refs_1_, f32[64,512]{1,0:T(8,128)S(1)} %collective-permute-done.13.refs_2_, ...), custom_call_target="tpu_custom_call" | custom-call | tf_op jit(solution)/shard_map/apply_inverse/pallas_call | solution.py:378
  (16 shorter events, 0.3 us)
Async XLA Ops:
  2.1 9.9 %collective-permute-start = (f32[64,1024]{1,0:T(8,128)S(1)}, f32[64,1024]{1,0:T(8,128)S(1)}, u32[]{:S(2)}, u32[]{:S(2)}) collective-permute-start(f32[64,1024]{1,0:T(8,128)S(1)} %get-tuple-element.17.lead_ref.own_ref), channel_id=1, source_target_pairs={{0,1},{1,0},{2,3},{3,2},{4,5},{5,4},{6,7},{7,6},{8,9},{9,8},{10,11... | collective-permute-start | bytes 786440 | tf_op jit(solution)/shard_map/ppermute | solution.py:289
  5.2 0.7 %copy-start = (s32[16,1]{0,1:T(1,128)S(1)}, s32[16,1]{0,1:T(1,128)}, u32[]{:S(2)}) copy-start(s32[16,1]{0,1:T(1,128)} %param.5) | copy-start | bytes 196
  12.0 3.4 %collective-permute-start.1 = (f32[4,72,512]{2,1,0:T(8,128)S(1)}, f32[4,72,512]{2,1,0:T(8,128)S(1)}, u32[]{:S(2)}, u32[]{:S(2)}) collective-permute-start(f32[4,72,512]{2,1,0:T(8,128)S(1)} %get-tuple-element.20), channel_id=1, source_target_pairs={{0,16},{16,0},{1,17},{17,1},{2,18},{18,2},{3,19},{19,3},{4,20},{20... | collective-permute-start | bytes 1769480 | tf_op jit(solution)/shard_map/ppermute | solution.py:321
  14.8 4.3 %collective-permute-start.7 = (f32[4,72,512]{2,1,0:T(8,128)S(1)}, f32[4,72,512]{2,1,0:T(8,128)S(1)}, u32[]{:S(2)}, u32[]{:S(2)}) collective-permute-start(f32[4,72,512]{2,1,0:T(8,128)S(1)} %get-tuple-element.26), channel_id=1, source_target_pairs={{0,16},{16,0},{1,17},{17,1},{2,18},{18,2},{3,19},{19,3},{4,20},{20... | collective-permute-start | bytes 1769480 | tf_op jit(solution)/shard_map/ppermute | solution.py:321
  15.5 6.8 %collective-permute-start.2 = (f32[72,512]{1,0:T(8,128)S(1)}, f32[72,512]{1,0:T(8,128)S(1)}, u32[]{:S(2)}, u32[]{:S(2)}) collective-permute-start(f32[72,512]{1,0:T(8,128)S(1)} %get-tuple-element.32), channel_id=1, source_target_pairs={{0,2},{2,0},{4,6},{6,4},{8,10},{10,8},{12,14},{14,12},{1,3},{3,1},... | collective-permute-start | bytes 442376 | tf_op jit(solution)/shard_map/ppermute | solution.py:324
  17.0 7.4 %collective-permute-start.3 = (f32[72,512]{1,0:T(8,128)S(1)}, f32[72,512]{1,0:T(8,128)S(1)}, u32[]{:S(2)}, u32[]{:S(2)}) collective-permute-start(f32[72,512]{1,0:T(8,128)S(1)} %get-tuple-element.31), channel_id=1, source_target_pairs={{0,4},{2,6},{4,0},{6,2},{8,12},{10,14},{12,8},{14,10},{1,5},{3,7},... | collective-permute-start | bytes 442376 | tf_op jit(solution)/shard_map/ppermute | solution.py:324
  18.6 8.0 %collective-permute-start.4 = (f32[72,512]{1,0:T(8,128)S(1)}, f32[72,512]{1,0:T(8,128)S(1)}, u32[]{:S(2)}, u32[]{:S(2)}) collective-permute-start(f32[72,512]{1,0:T(8,128)S(1)} %get-tuple-element.30), channel_id=1, source_target_pairs={{0,6},{2,4},{4,2},{6,0},{8,14},{10,12},{12,10},{14,8},{1,7},{3,5},... | collective-permute-start | bytes 442376 | tf_op jit(solution)/shard_map/ppermute | solution.py:324
  19.2 11.4 %collective-permute-start.8 = (f32[72,512]{1,0:T(8,128)S(1)}, f32[72,512]{1,0:T(8,128)S(1)}, u32[]{:S(2)}, u32[]{:S(2)}) collective-permute-start(f32[72,512]{1,0:T(8,128)S(1)} %get-tuple-element.29), channel_id=1, source_target_pairs={{0,2},{2,0},{4,6},{6,4},{8,10},{10,8},{12,14},{14,12},{1,3},{3,1},... | collective-permute-start | bytes 442376 | tf_op jit(solution)/shard_map/ppermute | solution.py:324
  20.7 9.9 %collective-permute-start.9 = (f32[72,512]{1,0:T(8,128)S(1)}, f32[72,512]{1,0:T(8,128)S(1)}, u32[]{:S(2)}, u32[]{:S(2)}) collective-permute-start(f32[72,512]{1,0:T(8,128)S(1)} %get-tuple-element.28), channel_id=1, source_target_pairs={{0,4},{2,6},{4,0},{6,2},{8,12},{10,14},{12,8},{14,10},{1,5},{3,7},... | collective-permute-start | bytes 442376 | tf_op jit(solution)/shard_map/ppermute | solution.py:324
  22.3 10.0 %collective-permute-start.10 = (f32[72,512]{1,0:T(8,128)S(1)}, f32[72,512]{1,0:T(8,128)S(1)}, u32[]{:S(2)}, u32[]{:S(2)}) collective-permute-start(f32[72,512]{1,0:T(8,128)S(1)} %get-tuple-element.27), channel_id=1, source_target_pairs={{0,6},{2,4},{4,2},{6,0},{8,14},{10,12},{12,10},{14,8},{1,7},{3,5},... | collective-permute-start | bytes 442376 | tf_op jit(solution)/shard_map/ppermute | solution.py:324
  26.7 12.2 %collective-permute-start.5 = (f32[72,512]{1,0:T(8,128)S(1)}, f32[72,512]{1,0:T(8,128)S(1)}, u32[]{:S(2)}, u32[]{:S(2)}) collective-permute-start(f32[72,512]{1,0:T(8,128)S(1)} %add.45), channel_id=1, source_target_pairs={{0,12},{2,14},{4,8},{6,10},{8,4},{10,6},{12,0},{14,2},{1,13},{3,15... | collective-permute-start | bytes 442376 | tf_op jit(solution)/shard_map/ppermute | solution.py:324
  32.4 9.7 %collective-permute-start.11 = (f32[72,512]{1,0:T(8,128)S(1)}, f32[72,512]{1,0:T(8,128)S(1)}, u32[]{:S(2)}, u32[]{:S(2)}) collective-permute-start(f32[72,512]{1,0:T(8,128)S(1)} %add.50), channel_id=1, source_target_pairs={{0,12},{2,14},{4,8},{6,10},{8,4},{10,6},{12,0},{14,2},{1,13},{3,15... | collective-permute-start | bytes 442376 | tf_op jit(solution)/shard_map/ppermute | solution.py:324
  38.9 6.8 %collective-permute-start.13 = (f32[64,512]{1,0:T(8,128)S(1)}, f32[64,512]{1,0:T(8,128)S(1)}, u32[]{:S(2)}, u32[]{:S(2)}) collective-permute-start(f32[64,512]{1,0:T(8,128)S(1)} %slice.65.refs_0_), channel_id=1, source_target_pairs={{0,4},{2,6},{4,0},{6,2},{8,12},{10,14},{12,8},{14,10},{1,5},{3,7},... | collective-permute-start | bytes 393224 | tf_op jit(solution)/shard_map/ppermute | solution.py:324
  39.0 5.8 %collective-permute-start.6 = (f32[8,512]{1,0:T(8,128)S(1)}, f32[8,512]{1,0:T(8,128)S(1)}, u32[]{:S(2)}, u32[]{:S(2)}) collective-permute-start(f32[8,512]{1,0:T(8,128)S(1)} %slice.59.own_ref), channel_id=1, source_target_pairs={{0,1},{1,0},{2,3},{3,2},{4,5},{5,4},{6,7},{7,6},{8,9},{9,8},{10,11... | collective-permute-start | bytes 49160 | tf_op jit(solution)/shard_map/ppermute | solution.py:366
  40.2 12.1 %collective-permute-start.12 = (f32[64,512]{1,0:T(8,128)S(1)}, f32[64,512]{1,0:T(8,128)S(1)}, u32[]{:S(2)}, u32[]{:S(2)}) collective-permute-start(f32[64,512]{1,0:T(8,128)S(1)} %slice.65.refs_0_), channel_id=1, source_target_pairs={{0,2},{2,0},{4,6},{6,4},{8,10},{10,8},{12,14},{14,12},{1,3},{3,1},... | collective-permute-start | bytes 393224 | tf_op jit(solution)/shard_map/ppermute | solution.py:324
  42.1 10.2 %collective-permute-start.15 = (f32[64,512]{1,0:T(8,128)S(1)}, f32[64,512]{1,0:T(8,128)S(1)}, u32[]{:S(2)}, u32[]{:S(2)}) collective-permute-start(f32[64,512]{1,0:T(8,128)S(1)} %slice.66.refs_4_), channel_id=1, source_target_pairs={{0,2},{2,0},{4,6},{6,4},{8,10},{10,8},{12,14},{14,12},{1,3},{3,1},... | collective-permute-start | bytes 393224 | tf_op jit(solution)/shard_map/ppermute | solution.py:324
  43.7 8.7 %collective-permute-start.16 = (f32[64,512]{1,0:T(8,128)S(1)}, f32[64,512]{1,0:T(8,128)S(1)}, u32[]{:S(2)}, u32[]{:S(2)}) collective-permute-start(f32[64,512]{1,0:T(8,128)S(1)} %slice.66.refs_4_), channel_id=1, source_target_pairs={{0,4},{2,6},{4,0},{6,2},{8,12},{10,14},{12,8},{14,10},{1,5},{3,7},... | collective-permute-start | bytes 393224 | tf_op jit(solution)/shard_map/ppermute | solution.py:324
  44.8 7.5 %collective-permute-start.17 = (f32[64,512]{1,0:T(8,128)S(1)}, f32[64,512]{1,0:T(8,128)S(1)}, u32[]{:S(2)}, u32[]{:S(2)}) collective-permute-start(f32[64,512]{1,0:T(8,128)S(1)} %slice.66.refs_4_), channel_id=1, source_target_pairs={{0,6},{2,4},{4,2},{6,0},{8,14},{10,12},{12,10},{14,8},{1,7},{3,5},... | collective-permute-start | bytes 393224 | tf_op jit(solution)/shard_map/ppermute | solution.py:324
  45.7 7.1 %collective-permute-start.14 = (f32[64,512]{1,0:T(8,128)S(1)}, f32[64,512]{1,0:T(8,128)S(1)}, u32[]{:S(2)}, u32[]{:S(2)}) collective-permute-start(f32[64,512]{1,0:T(8,128)S(1)} %collective-permute-done.13.refs_2_), channel_id=1, source_target_pairs={{0,2},{2,0},{4,6},{6,4},{8,10},{10,8},{12,14},{14,12},{1,3},{3,1},... | collective-permute-start | bytes 393224 | tf_op jit(solution)/shard_map/ppermute | solution.py:324
